TPU v7x, 128 devices: a whole 4x4x4 slice. The times are simulated.
128 devices in a mesh: section: 16 (over y, x_hi, core), tensor: 8 (over x_lo, z).
Axes of the slice: x: 4 (x_hi: 2, x_lo: 2; x = x_hi * 2 + x_lo), y: 4, z: 4, core: 2. Of those that a mesh axis runs over, the one named last changes fastest.
Arguments:
- section_input: bfloat16 [16, 256, 8192], P('section', 'tensor')
- positions: int32 [16, 256], P('section'), may hold values from 0 to 127, as said below
- attn_gain: bfloat16 [16, 8192], P('section'), may hold values from 0.099609375 to 1.8984375
- w_query: bfloat16 [16, 8192, 4096], P('section', None, 'tensor')
- w_keyval: bfloat16 [16, 8192, 8, 256], P('section', None, 'tensor')
- w_out_proj: bfloat16 [16, 4096, 8192], P('section', 'tensor'), may hold values from -0.09375 to 0.09375
- final_gain: bfloat16 [8192], replicated, may hold values from 0.099609375 to 1.8984375
- w_vocab: bfloat16 [8192, 32768], P(None, ('section', 'tensor'))
- targets: int32 [256], replicated, may hold values from 0 to 32767
Outputs:
- handed: bfloat16 [16, 256, 8192], P('section', 'tensor')
- logprob: float32 [256], P('tensor')
Inputs may be any that keep to these rules, and one draw needn't show every extreme that they name: positions[s, i] counts the tokens since the start of token i's document; documents are packed in microbatches of 128 tokens, every microbatch starts one at its first token, and in every draw some microbatch is a single document.
All inputs are finite; a program needn't handle non-finite values.
Results may differ from a plain program's by a relative error of at most 0.011.
Values may be sent and summed in bfloat16 or wider, within the bound.
No kernel may reach another device: no remote copies, remote signals or barrier semaphores. Data moves between devices by JAX's collectives and lax.ppermute only.
A program may use at most 128 MiB of HBM per device.

v0:
```python
import math

import jax
import jax.numpy as jnp
from jax import lax
from jax.sharding import PartitionSpec as P

NORM_EPSILON = 1e-05
ROPE_THETA = 500000.0


def shifted(array, axis, by):
    size = lax.axis_size(axis)
    pairs = [(i, i + by) for i in range(size) if 0 <= i + by < size]
    return lax.ppermute(array, axis, pairs)


def broadcast(block, axis, holder):
    block = jnp.where(lax.axis_index(axis) == holder, block, jnp.zeros_like(block))
    return lax.psum(block, axis)


def rms_norm(row_block, gain_row):
    values = row_block.astype(jnp.float32)
    factor = lax.rsqrt(jnp.mean(values * values, axis=-1, keepdims=True) + NORM_EPSILON)
    return (values * factor * gain_row.astype(jnp.float32)).astype(jnp.bfloat16)


def rotary(values, token_pos):
    half_dim = values.shape[-1] // 2
    frequency = ROPE_THETA ** (-jnp.arange(half_dim, dtype=jnp.float32) * 2.0 / values.shape[-1])
    angles = token_pos.astype(jnp.float32)[:, None] * frequency[None, :]
    cosine = jnp.cos(angles)[:, None, :]
    sine_part = jnp.sin(angles)[:, None, :]
    lower_half = values[..., :half_dim]
    upper_half = values[..., half_dim:]
    return jnp.concatenate(
        [
            lower_half * cosine - upper_half * sine_part,
            upper_half * cosine + lower_half * sine_part,
        ],
        axis=-1,
    )


def allowed_mask(token_pos):
    token_count = token_pos.shape[0]
    query_pos = jnp.arange(token_count, dtype=jnp.int32)[:, None]
    key_pos = jnp.arange(token_count, dtype=jnp.int32)[None, :]
    return (key_pos <= query_pos) & (key_pos >= query_pos - token_pos[:, None])


def body(
    section_input, positions, attn_gain, w_query, w_keyval, w_out_proj, final_gain, w_vocab, targets
):
    my_rows = section_input[0]
    token_pos = positions[0]
    model_width = my_rows.shape[1]
    head_dim = w_keyval.shape[3] // 2
    kv_local = w_keyval.shape[2]
    query_cols = w_query.shape[2]
    query_heads = query_cols // head_dim
    group_size = query_heads // kv_local
    query_weight = w_query[0]
    keyval_weight = w_keyval[0].reshape(model_width, -1)
    output_weight = w_out_proj[0]
    normed = rms_norm(my_rows, attn_gain[0])
    piece_rows = lax.all_gather(normed, "tensor", axis=0, tiled=True)
    row_count = piece_rows.shape[0]
    queries = jnp.dot(piece_rows, query_weight, preferred_element_type=jnp.float32).reshape(
        row_count, query_heads, head_dim
    )
    keyvals = jnp.dot(piece_rows, keyval_weight, preferred_element_type=jnp.float32).reshape(
        row_count, kv_local, 2 * head_dim
    )
    queries = rotary(queries, token_pos).astype(jnp.bfloat16).reshape(row_count, query_cols)
    key_rows = rotary(keyvals[..., :head_dim], token_pos).astype(jnp.bfloat16)
    value_rows = keyvals[..., head_dim:].astype(jnp.bfloat16)
    joined = jnp.concatenate([key_rows, value_rows], axis=-1).reshape(row_count, -1)
    projected = jnp.concatenate([queries, joined], axis=1)
    token_count = projected.shape[0]
    grouped = projected[:, :query_cols].reshape(token_count, kv_local, group_size, head_dim)
    keyvals = projected[:, query_cols:].reshape(token_count, kv_local, 2 * head_dim)
    key_rows = keyvals[..., :head_dim]
    value_rows = keyvals[..., head_dim:]
    scores = jnp.einsum(
        "qkgd,skd->kgqs", grouped, key_rows, preferred_element_type=jnp.float32
    ) / math.sqrt(head_dim)
    allowed = allowed_mask(token_pos)
    scores = jnp.where(allowed, scores, -jnp.inf)
    maxima = jnp.max(scores, axis=-1, keepdims=True)
    exps = jnp.where(allowed, jnp.exp(scores - maxima), 0.0)
    weights = (exps / jnp.sum(exps, axis=-1, keepdims=True)).astype(jnp.bfloat16)
    context = jnp.einsum("kgqs,skd->qkgd", weights, value_rows, preferred_element_type=jnp.float32)
    context = context.astype(jnp.bfloat16).reshape(token_count, query_cols)
    share_rows = my_rows.shape[0]
    share_start = lax.axis_index("tensor") * share_rows
    summed = lax.psum_scatter(
        jnp.dot(context, output_weight, preferred_element_type=jnp.float32),
        "tensor",
        scatter_dimension=0,
        tiled=True,
    )
    layer_out = (my_rows.astype(jnp.float32) + summed).astype(jnp.bfloat16)
    handed = shifted(layer_out, "section", 1)[None]
    last_section = lax.axis_size("section") - 1
    vocab_local = w_vocab.shape[1]
    column_start = (
        lax.axis_index("section") * lax.axis_size("tensor") + lax.axis_index("tensor")
    ) * vocab_local
    final_rows = rms_norm(layer_out, final_gain)
    all_rows = lax.all_gather(final_rows, "tensor", axis=0, tiled=True)
    all_rows = broadcast(all_rows, "section", last_section)
    logits = jnp.dot(all_rows, w_vocab, preferred_element_type=jnp.float32)
    row_top = jnp.max(logits, axis=1)
    exp_total = jnp.sum(jnp.exp(logits - row_top[:, None]), axis=1)
    wanted = targets - column_start
    columns = jnp.arange(vocab_local, dtype=jnp.int32)[None, :]
    picked = jnp.sum(jnp.where(columns == wanted[:, None], logits, 0.0), axis=1)
    row_values = jnp.stack([row_top, exp_total, picked], axis=0)
    local_top = row_values[0]
    local_total = row_values[1]
    local_pick = row_values[2]
    row_top = lax.pmax(local_top, ("section", "tensor"))
    exp_total, picked = lax.psum(
        (local_total * jnp.exp(local_top - row_top), local_pick), ("section", "tensor")
    )
    logprob = picked - row_top - jnp.log(exp_total)
    mine_rows = lax.dynamic_slice_in_dim(logprob, share_start, share_rows)
    return (handed, mine_rows)


def solution(mesh):
    placed = (
        P("section", "tensor", None),
        P("section", None),
        P("section", None),
        P("section", None, "tensor"),
        P("section", None, "tensor", None),
        P("section", "tensor", None),
        P(),
        P(None, ("section", "tensor")),
        P(),
    )
    return jax.shard_map(
        body,
        mesh=mesh,
        in_specs=placed,
        out_specs=(P("section", "tensor", None), P("tensor")),
        check_vma=False,
    )
```

profile of v0, /device:TPU:1, one launch (start us, length us, event | category | flops | bytes accessed | tf_op | source)
XLA Modules:
  0.0 531.1 jit_solution(5388462509276532936)
XLA Ops:
  7.2 0.8 mul.169
  8.0 1.3 fusion.14
  9.3 2.0 fusion.16
  11.3 0.0 reduce-scatter.2.cloned.1.call-start
  11.4 11.4 %copy.19 = bf16[512,8192]{1,0:T(8,128)(2,1)} copy(bf16[512,8192]{0,1:T(8,128)(2,1)} %bitcast.58) | data formatting | bytes 16777216 | tf_op jit(solution)/shard_map/dot_general | solution.py:70
  22.9 0.3 multiply_cosine_fusion
  23.2 44.3 %all-gather.3.cloned.1.call-done = bf16[256,8192]{1,0:T(8,128)(2,1)} async-done(((bf16[32,8192]{1,0:T(8,128)(2,1)}), bf16[256,8192]{1,0:T(8,128)(2,1)}) %all-gather.3.cloned.1.call-update) | async-done | bytes 4194320 | tf_op jit(solution)/shard_map/all_gather | solution.py:68
  67.5 5.3 %fusion.8 = f32[256,1,256]{0,2,1:T(8,128)S(1)} fusion(bf16[256,8192]{1,0:T(8,128)(2,1)} %all-gather.3.cloned.1.call-done, bf16[1,8192,1,256]{3,1,2,0:T(8,128)(2,1)} %param.13), kind=kOutput, calls=%fused_computation.16 | convolution fusion | flops 1073741824 | bytes 8650752 | tf_op jit(solution)/shard_map/dot_general | solution.py:73
  72.8 0.3 fusion.38
  73.2 0.2 copy-done
  73.3 4.7 fusion.2
  78.0 0.1 subtract_convert_fusion
  78.1 0.3 fusion.42
  78.4 0.2 fusion.18
  78.7 0.4 convolution_convert_fusion
  79.1 5.8 %fusion = f32[256,8192]{1,0:T(8,128)} fusion(bf16[256,512]{0,1:T(8,128)(2,1)S(1)} %bitcast.63, bf16[1,512,8192]{2,1,0:T(8,128)(2,1)S(1)} %bitcast.60), kind=kOutput, calls=%fused_computation | convolution fusion | flops 2147483648 | bytes 17039360 | tf_op jit(solution)/shard_map/dot_general | solution.py:99
  84.9 0.0 all-gather.5.cloned.1.call-start
  84.9 0.6 copy-done.2
  85.6 91.0 %reduce-scatter.2.cloned.1.call-done = f32[32,8192]{1,0:T(8,128)} async-done(((f32[256,8192]{1,0:T(8,128)}), f32[32,8192]{1,0:T(8,128)}) %reduce-scatter.2.cloned.1.call-update) | async-done | bytes 1048592 | tf_op jit(solution)/shard_map/reduce_scatter | solution.py:98
  176.6 1.5 fusion.11
  178.1 1.0 fusion.13
  179.2 51.5 %all-gather.5.cloned.1.call-done = bf16[256,8192]{1,0:T(8,128)(2,1)} async-done(((bf16[32,8192]{1,0:T(8,128)(2,1)}), bf16[256,8192]{1,0:T(8,128)(2,1)}) %all-gather.5.cloned.1.call-update) | async-done | bytes 4194320 | tf_op jit(solution)/shard_map/all_gather | solution.py:112
  230.7 2.2 broadcast_select_fusion
  232.9 4.9 collective-permute-start
  237.8 8.9 %collective-permute-done = bf16[32,8192]{1,0:T(8,128)(2,1)S(1)} collective-permute-done((bf16[32,8192]{1,0:T(8,128)(2,1)S(1)}, bf16[32,8192]{1,0:T(8,128)(2,1)S(1)}, u32[]{:S(2)}, u32[]{:S(2)}) %collective-permute-start) | collective-permute-done | bytes 524320 | tf_op jit(solution)/shard_map/ppermute | solution.py:15
  246.7 141.1 %all-reduce.3.cloned.1.call-done = bf16[256,8192]{1,0:T(8,128)(2,1)} async-done(((bf16[256,8192]{1,0:T(8,128)(2,1)}), bf16[256,8192]{1,0:T(8,128)(2,1)}) %all-reduce.3.cloned.1.call-update) | async-done | bytes 4194320 | tf_op jit(solution)/shard_map/psum | solution.py:20
  387.8 5.2 fusion.43
  393.0 67.4 %pmax.7 = f32[256]{0:T(256)S(1)} all-reduce(f32[256]{0:T(256)S(1)} %get-tuple-element.16), channel_id=1, replica_groups=mesh['section'=16,'tensor'=8] {'section','tensor'}, use_global_device_ids=true, to_apply=%region_9.10 | all-reduce | flops 256 | bytes 2048 | tf_op jit(solution)/shard_map/pmax | solution.py:124
  460.4 0.1 select_reduce_fusion
  460.5 62.6 %all-reduce = (f32[256]{0:T(256)S(1)}, f32[256]{0:T(256)S(1)}) all-reduce(f32[256]{0:T(256)S(1)} %exponential_multiply_fusion, f32[256]{0:T(256)S(1)} %get-tuple-element.2), channel_id=1, replica_groups=mesh['section'=16,'tensor'=8] {'section','tensor'}, use_global_device_ids=true, to_apply=%region_11.12 | all-reduce | flops 512 | bytes 4096 | tf_op jit(solution)/shard_map/psum | solution.py:125
  523.1 0.6 dynamic_slice.3
  523.7 0.8 copy.22
  (29 shorter events, 0.3 us)
Async XLA Ops:
  7.2 60.3 %all-gather.3.cloned.1.call-start = ((), (), s32[]{:S(2)}) async-start(), calls=%async_computation.1 | async-start | bytes 4718592 | tf_op jit(solution)/shard_map/all_gather | solution.py:68
  11.3 165.3 %reduce-scatter.2.cloned.1.call-start = ((), (), s32[]{:S(2)}) async-start(), calls=%async_computation.2 | async-start | bytes 9437184 | tf_op jit(solution)/shard_map/reduce_scatter | solution.py:98
  11.4 11.4 %copy-start.3 = (s32[1,256]{1,0:T(1,128)S(1)}, s32[1,256]{1,0:T(1,128)}, u32[]{:S(2)}) copy-start(s32[1,256]{1,0:T(1,128)} %param.10) | copy-start | bytes 3076
  67.5 5.8 %copy-start = (bf16[512,8192]{1,0:T(8,128)(2,1)S(1)}, bf16[512,8192]{1,0:T(8,128)(2,1)}, u32[]{:S(2)}) copy-start(bf16[512,8192]{1,0:T(8,128)(2,1)} %copy.19) | copy-start | bytes 25165828
  73.2 5.9 %slice-start = ((s8[8388608]{0:T(1024)(128)(4,1)}), s8[4194304]{0:T(1024)(128)(4,1)S(1)}, s32[]{:S(2)}) async-start(s8[8388608]{0:T(1024)(128)(4,1)} %bitcast.59), calls=%async_computation.5 | async-start | bytes 8388608
  73.3 5.8 %slice-start.1 = ((s8[8388608]{0:T(1024)(128)(4,1)}), s8[4194304]{0:T(1024)(128)(4,1)S(1)}, s32[]{:S(2)}) async-start(s8[8388608]{0:T(1024)(128)(4,1)} %bitcast.59), calls=%async_computation.6 | async-start | bytes 8388608
  84.9 0.7 copy-start.2
  84.9 91.8 %copy-start.1 = (bf16[1,32,8192]{2,1,0:T(8,128)(2,1)S(1)}, bf16[1,32,8192]{2,1,0:T(8,128)(2,1)}, u32[]{:S(2)}) copy-start(bf16[1,32,8192]{2,1,0:T(8,128)(2,1)} %param.9) | copy-start | bytes 1572868
  84.9 145.8 %all-gather.5.cloned.1.call-start = ((), (), s32[]{:S(2)}) async-start(), calls=%async_computation.3 | async-start | bytes 4718592 | tf_op jit(solution)/shard_map/all_gather | solution.py:112
  179.1 208.6 %all-reduce.3.cloned.1.call-start = ((), (), s32[]{:S(2)}) async-start(), calls=%async_computation.4 | async-start | bytes 8388608 | tf_op jit(solution)/shard_map/psum | solution.py:20
  232.9 4.9 copy-start.4
  232.9 13.8 %collective-permute-start = (bf16[32,8192]{1,0:T(8,128)(2,1)S(1)}, bf16[32,8192]{1,0:T(8,128)(2,1)S(1)}, u32[]{:S(2)}, u32[]{:S(2)}) collective-permute-start(bf16[32,8192]{1,0:T(8,128)(2,1)S(1)} %get-tuple-element.7), channel_id=1, source_target_pairs={{0,8},{8,16},{16,24},{24,32},{32,40},{40,48},{48,56},{56,64},{64,7... | collective-permute-start | bytes 1572872 | tf_op jit(solution)/shard_map/ppermute | solution.py:15
Sparse Core Ops, SparseCore 0:
  11.4 55.9 all-gather.2
  85.0 91.5 reduce-scatter.1
  179.2 51.3 all-gather.4
  233.1 154.6 all-reduce.2
where the time goes:
time: 532 us; the launch traced here: 531 us
  waiting for transfers between devices  337 us (63%)
  blocking collectives  130 us (24%)
  matrix products  21.7 us (4%)
  between operations  13.9 us (3%)
  local copies, waits for them, and re-layouts  13.6 us (3%)
  other arithmetic  9.86 us (2%)
    psum x1, waiting for transfers between devices, broadcast(): return lax.psum(block, axis)  141 us
    reduce_scatter x1, waiting for transfers between devices, body(): lax.psum_scatter(jnp.dot(context, output_weight, preferred_element_type=j...  91 us
    pmax x1, blocking collectives, body(): row_top = lax.pmax(local_top, ('section', 'tensor'))  67.4 us
    psum x1, blocking collectives, body(): lax.psum((local_total * jnp.exp(local_top - row_top), local_pick), ('sect...  62.6 us
    all_gather x1, waiting for transfers between devices, body(): all_rows = lax.all_gather(final_rows, 'tensor', axis=0, tiled=True)  51.5 us
    all_gather x1, waiting for transfers between devices, body(): piece_rows = lax.all_gather(normed, 'tensor', axis=0, tiled=True)  44.3 us
    dot_general x1, local copies, waits for them, and re-layouts, body(): jnp.dot(piece_rows, query_weight, preferred_element_type=jnp.float32)  11.4 us
  transfers between devices with their start and end apart: 5, of which 5 were waited for; matrix products, arithmetic and copies ran while one was open for 2% of the time, Pallas kernels for 0%

commit v1 on v0

v1 whole, which is shorter than its diff:
```python
import math

import jax
import jax.numpy as jnp
from jax import lax
from jax.experimental import pallas as pl
from jax.experimental.pallas import tpu as pltpu
from jax.sharding import PartitionSpec as P

NORM_EPSILON = 1e-05
ROPE_THETA = 500000.0
BF16 = jnp.bfloat16
F32 = jnp.float32
NZ = 4
ROWS = 32
HALF = 16
WIDTH = 8192
HEAD = 128
HEADS = 4
MB = 128
VL = 256


def tensor_pairs(step):
    out = []
    for x in range(2):
        for z in range(NZ):
            x2, z2 = step(x, z)
            out.append((x * NZ + z, (x2 % 2) * NZ + z2 % NZ))
    return out


TO_X = tensor_pairs(lambda x, z: (x + 1, z))
TO_UP = tensor_pairs(lambda x, z: (x, z + 1))
TO_DOWN = tensor_pairs(lambda x, z: (x, z - 1))


def sec(y, h, c):
    return ((y % 4) * 2 + h % 2) * 2 + c


SWAP_CORE = [(s, s ^ 1) for s in range(16)]


def over_tensor(block, pairs):
    return lax.ppermute(block, "tensor", pairs)


def over_section(block, pairs):
    return lax.ppermute(block, "section", pairs)


def rms_norm(row_block, gain_row):
    values = row_block.astype(F32)
    factor = lax.rsqrt(jnp.mean(values * values, axis=-1, keepdims=True) + NORM_EPSILON)
    return (values * factor * gain_row.astype(F32)).astype(BF16)


def gather_rows(own):
    half = own.shape[0] // 2
    from_x = over_tensor(own, TO_X)
    below = over_tensor(own, TO_UP)
    above = over_tensor(own, TO_DOWN)
    x_below = over_tensor(from_x, TO_UP)
    x_above = over_tensor(from_x, TO_DOWN)
    far_a = over_tensor(below[:half], TO_UP)
    far_b = over_tensor(above[half:], TO_DOWN)
    x_far_a = over_tensor(far_a, TO_X)
    x_far_b = over_tensor(far_b, TO_X)
    return own, above, far_a, far_b, below, from_x, x_above, x_far_a, x_far_b, x_below


LAYER_ROWS = [(0, 32), (32, 32), (64, 16), (80, 16), (96, 32), (128, 32), (160, 32), (192, 16), (208, 16), (224, 32)]
KC = 1024
NC = 1024


def layer_kernel(*refs):
    blocks = refs[:10]
    wq_ref, wkv_ref, wo_ref, cos_ref, sin_ref, allow_ref = refs[10:16]
    outs = refs[16:26]
    rows, wq, wkv, wo, q_acc, kv_acc, ctx, res, row_sem, w_sem, wo_sem, out_sem = refs[26:]
    steps = WIDTH // KC

    def row_copies(k):
        cols = pl.ds(k * KC, KC)
        return [
            pltpu.make_async_copy(b.at[:, cols], rows.at[pl.ds(at, n), cols], row_sem.at[k])
            for b, (at, n) in zip(blocks, LAYER_ROWS)
        ]

    def w_copies(k):
        part = pl.ds(k * KC, KC)
        return [
            pltpu.make_async_copy(wq_ref.at[part], wq.at[part], w_sem.at[0, k]),
            pltpu.make_async_copy(wkv_ref.at[part], wkv.at[part], w_sem.at[1, k]),
        ]

    def wo_copy(n):
        cols = pl.ds(n * NC, NC)
        return pltpu.make_async_copy(wo_ref.at[:, cols], wo.at[:, cols], wo_sem.at[n])

    for k in range(steps):
        for c in row_copies(k) + w_copies(k):
            c.start()
    for n in range(WIDTH // NC):
        wo_copy(n).start()
    for k in range(steps):
        cols = pl.ds(k * KC, KC)
        pltpu.make_async_copy(rows.at[:, cols], rows.at[:, cols], row_sem.at[k]).wait()
        for c in w_copies(k):
            c.wait()
        lhs = rows[:, cols]
        q_part = jnp.dot(lhs, wq[cols, :], preferred_element_type=F32)
        kv_part = jnp.dot(lhs, wkv[cols, :], preferred_element_type=F32)
        if k == 0:
            q_acc[...] = q_part
            kv_acc[...] = kv_part
        else:
            q_acc[...] += q_part
            kv_acc[...] += kv_part
    cos, sin = cos_ref[...], sin_ref[...]

    def rotate(v):
        return (v * cos + pltpu.roll(v, HEAD // 2, 1) * sin).astype(BF16)

    keys = rotate(kv_acc[:, :HEAD])
    values = kv_acc[:, HEAD:].astype(BF16)
    for h in range(HEADS):
        q = rotate(q_acc[:, h * HEAD : (h + 1) * HEAD])
        for b in range(2):
            at = slice(b * MB, (b + 1) * MB)
            allow = allow_ref[at, :] > 0
            s = lax.dot_general(q[at], keys[at], (((1,), (1,)), ((), ())), preferred_element_type=F32)
            s = jnp.where(allow, s * (1.0 / math.sqrt(HEAD)), -jnp.inf)
            e = jnp.exp(s - jnp.max(s, axis=1, keepdims=True))
            w = (e / jnp.sum(e, axis=1, keepdims=True)).astype(BF16)
            c = jnp.dot(w, values[at], preferred_element_type=F32)
            ctx[at, h * HEAD : (h + 1) * HEAD] = c.astype(BF16)

    def out_copies(n):
        cols = pl.ds(n * NC, NC)
        return [
            pltpu.make_async_copy(res.at[pl.ds(at, m), cols], o.at[:, cols], out_sem.at[n])
            for o, (at, m) in zip(outs, LAYER_ROWS)
        ]

    for n in range(WIDTH // NC):
        cols = pl.ds(n * NC, NC)
        wo_copy(n).wait()
        res[:, cols] = jnp.dot(ctx[...], wo[:, cols], preferred_element_type=F32).astype(BF16)
        for c in out_copies(n):
            c.start()
    for n in range(WIDTH // NC):
        cols = pl.ds(n * NC, NC)
        pltpu.make_async_copy(res.at[:, cols], res.at[:, cols], out_sem.at[n]).wait()


def layer(blocks, wq, wkv, wo, cos, sin, allow):
    steps = WIDTH // KC
    hbm = pl.BlockSpec(memory_space=pl.ANY)
    vmem = pl.BlockSpec(memory_space=pltpu.VMEM)
    return pl.pallas_call(
        layer_kernel,
        out_shape=[jax.ShapeDtypeStruct((n, WIDTH), BF16) for _, n in LAYER_ROWS],
        in_specs=[hbm] * 13 + [vmem] * 3,
        out_specs=[hbm] * 10,
        scratch_shapes=[
            pltpu.VMEM((2 * MB, WIDTH), BF16),
            pltpu.VMEM((WIDTH, HEADS * HEAD), BF16),
            pltpu.VMEM((WIDTH, 2 * HEAD), BF16),
            pltpu.VMEM((HEADS * HEAD, WIDTH), BF16),
            pltpu.VMEM((2 * MB, HEADS * HEAD), F32),
            pltpu.VMEM((2 * MB, 2 * HEAD), F32),
            pltpu.VMEM((2 * MB, HEADS * HEAD), BF16),
            pltpu.VMEM((2 * MB, WIDTH), BF16),
            pltpu.SemaphoreType.DMA((steps,)),
            pltpu.SemaphoreType.DMA((2, steps)),
            pltpu.SemaphoreType.DMA((WIDTH // NC,)),
            pltpu.SemaphoreType.DMA((WIDTH // NC,)),
        ],
        compiler_params=pltpu.CompilerParams(vmem_limit_bytes=48 * 1024 * 1024),
        cost_estimate=pl.CostEstimate(flops=6 * 10**9, bytes_accessed=28 * 2**20, transcendentals=0),
        name="layer",
    )(*blocks, wq, wkv, wo, cos, sin, allow)


HALF_ROWS = [(0, 16), (16, 16), (32, 8), (40, 8), (48, 16), (64, 16), (80, 16), (96, 8), (104, 8), (112, 16)]
VC = 1024


def vocab_kernel(*refs):
    blocks = refs[:8]
    w0_ref, w1_ref, want_ref, out_ref, rows, w, acc, row_sem, w_sem = refs[8:]
    steps = WIDTH // VC

    def row_copies(k):
        cols = pl.ds(k * VC, VC)
        return [
            pltpu.make_async_copy(b.at[:, cols], rows.at[pl.ds(i * HALF, HALF), cols], row_sem.at[k])
            for i, b in enumerate(blocks)
        ]

    def w_copies(k):
        part = pl.ds(k * VC, VC)
        return [
            pltpu.make_async_copy(r.at[part], w.at[part, pl.ds(i * VL, VL)], w_sem.at[i, k])
            for i, r in enumerate((w0_ref, w1_ref))
        ]

    for k in range(steps):
        for c in row_copies(k) + w_copies(k):
            c.start()
    for k in range(steps):
        cols = pl.ds(k * VC, VC)
        pltpu.make_async_copy(rows.at[:, cols], rows.at[:, cols], row_sem.at[k]).wait()
        for c in w_copies(k):
            c.wait()
        part = jnp.dot(rows[:, cols], w[cols, :], preferred_element_type=F32)
        if k == 0:
            acc[...] = part
        else:
            acc[...] += part
    logits = acc[...]
    top = jnp.max(logits, axis=1, keepdims=True)
    total = jnp.sum(jnp.exp(logits - top), axis=1, keepdims=True)
    column = lax.broadcasted_iota(jnp.int32, logits.shape, 1)
    picked = jnp.sum(jnp.where(column == want_ref[:, :1], logits, 0.0), axis=1, keepdims=True)
    lane = lax.broadcasted_iota(jnp.int32, (8 * HALF, 128), 1)
    out_ref[...] = jnp.where(lane == 0, top, jnp.where(lane == 1, total, picked))


def vocab(blocks, w0, w1, want):
    steps = WIDTH // VC
    hbm = pl.BlockSpec(memory_space=pl.ANY)
    vmem = pl.BlockSpec(memory_space=pltpu.VMEM)
    return pl.pallas_call(
        vocab_kernel,
        out_shape=jax.ShapeDtypeStruct((8 * HALF, 128), F32),
        in_specs=[hbm] * 10 + [vmem],
        out_specs=vmem,
        scratch_shapes=[
            pltpu.VMEM((8 * HALF, WIDTH), BF16),
            pltpu.VMEM((WIDTH, 2 * VL), BF16),
            pltpu.VMEM((8 * HALF, 2 * VL), F32),
            pltpu.SemaphoreType.DMA((steps,)),
            pltpu.SemaphoreType.DMA((2, steps)),
        ],
        compiler_params=pltpu.CompilerParams(vmem_limit_bytes=24 * 1024 * 1024),
        cost_estimate=pl.CostEstimate(flops=10**9, bytes_accessed=10 * 2**20, transcendentals=0),
        name="vocab",
    )(*blocks, w0, w1, want)


def add(*terms):
    return sum(t.astype(F32) for t in terms)


def spread_from_last(final_rows, section, core):
    first = over_section(final_rows[:HALF], [(15, 14)])
    cur = jnp.where(section == 14, first, final_rows[HALF:])
    y, h = section // 4, (section // 2) % 2

    def hop(block, moves):
        return over_section(
            block, [(sec(*a, c), sec(*b, c)) for a, b in moves for c in range(2)]
        )

    up = hop(cur, [((3, 1), (0, 1))])
    down = hop(cur, [((3, 1), (2, 1))])
    side = hop(cur, [((3, 1), (3, 0))])
    got = jnp.where(y == 0, up, jnp.where(y == 2, down, jnp.where(h == 0, side, cur)))
    up = hop(got, [((0, 1), (1, 1))])
    side = hop(got, [((0, 1), (0, 0)), ((2, 1), (2, 0))])
    got = jnp.where(y == 1, up, jnp.where((h == 0) & (y != 3), side, got))
    side = hop(got, [((1, 1), (1, 0))])
    return jnp.where((y == 1) & (h == 0), side, got)


def body(
    section_input, positions, attn_gain, w_query, w_keyval, w_out_proj, final_gain, w_vocab, targets
):
    section, rank = lax.axis_index("section"), lax.axis_index("tensor")
    core, x, z = section % 2, rank // NZ, rank % NZ
    my_rows = section_input[0]
    normed = rms_norm(my_rows, attn_gain[0])
    blocks = gather_rows(normed)
    other_vocab = over_section(w_vocab, SWAP_CORE)

    xs = jnp.stack([x, 1 - x])
    zs = (z + jnp.arange(NZ)) % NZ
    order = (xs[:, None] * NZ + zs[None, :]).reshape(-1)
    place = ((zs * ROWS)[:, None] + jnp.arange(ROWS)[None, :]).reshape(-1)
    pos = jnp.take(positions[0].reshape(8, ROWS), order, axis=0).reshape(-1)
    place2 = jnp.concatenate([place, place])
    frequency = ROPE_THETA ** (-jnp.arange(HEAD // 2, dtype=F32) * 2.0 / HEAD)
    angles = pos.astype(F32)[:, None] * frequency[None, :]
    cos, sin = jnp.cos(angles), jnp.sin(angles)
    cos = jnp.concatenate([cos, cos], axis=1)
    sin = jnp.concatenate([-sin, sin], axis=1)
    keys_at = place[None, :]
    allow = ((keys_at <= place2[:, None]) & (keys_at >= (place2 - pos)[:, None])).astype(F32)

    parts = layer(
        blocks, w_query[0], w_keyval[0].reshape(WIDTH, -1), w_out_proj[0], cos, sin, allow
    )
    own, above, far_a, far_b, below, x_own, x_above, x_far_a, x_far_b, x_below = parts
    got_far_a = over_tensor(x_far_a, TO_X)
    got_far_b = over_tensor(x_far_b, TO_X)
    got_x_down = over_tensor(x_above, TO_UP)
    got_x_up = over_tensor(x_below, TO_DOWN)
    far_a = add(far_a, got_far_a).astype(BF16)
    far_b = add(far_b, got_far_b).astype(BF16)
    got_a = over_tensor(far_a, TO_DOWN)
    got_b = over_tensor(far_b, TO_UP)
    x_own = add(x_own, got_x_down, got_x_up).astype(BF16)
    got_x = over_tensor(x_own, TO_X)
    below = jnp.concatenate([add(below[:HALF], got_a), below[HALF:].astype(F32)], axis=0).astype(BF16)
    above = jnp.concatenate([above[:HALF].astype(F32), add(above[HALF:], got_b)], axis=0).astype(BF16)
    got_down = over_tensor(below, TO_DOWN)
    got_up = over_tensor(above, TO_UP)
    layer_out = add(my_rows, own, got_x, got_down, got_up).astype(BF16)

    final_rows = rms_norm(layer_out, final_gain)
    mine = spread_from_last(final_rows, section, core)
    handed = over_section(layer_out, [(s, s + 1) for s in range(15)])[None]

    b = gather_rows(mine)
    blocks = (
        b[0], b[1], jnp.concatenate([b[2], b[3]]), b[4],
        b[5], b[6], jnp.concatenate([b[7], b[8]]), b[9],
    )
    starts = jnp.stack([section, section ^ 1]) * 8 * VL + rank * VL
    mine_targets = jnp.take(targets.reshape(8, 2, HALF), core, axis=1)
    want = jnp.take(mine_targets, order, axis=0).reshape(-1)
    at = want[:, None] - starts[None, :]
    inside = (at >= 0) & (at < VL)
    want = jnp.max(jnp.where(inside, at + jnp.arange(2)[None, :] * VL, -1), axis=1)
    want = jnp.broadcast_to(want[:, None], (8 * HALF, 128))
    stats = vocab(blocks, w_vocab, other_vocab, want)[:, :3]
    rank_x, rank_z = jnp.arange(8) // NZ, jnp.arange(8) % NZ
    seen_at = (rank_x ^ x) * NZ + (rank_z - z) % NZ
    stats = jnp.take(stats.reshape(8, HALF * 3), seen_at, axis=0)
    sent = jnp.broadcast_to(stats[None], (16, 8, HALF * 3)).reshape(128, HALF * 3)
    got = lax.all_to_all(sent, ("section", "tensor"), 0, 0, tiled=True)
    got = got.reshape(8, 2, 8, HALF, 3)
    tops, totals, picks = got[..., 0], got[..., 1], got[..., 2]
    top = jnp.max(tops, axis=(0, 2))
    total = jnp.sum(totals * jnp.exp(tops - top[None, :, None, :]), axis=(0, 2))
    logprob = jnp.sum(picks, axis=(0, 2)) - top - jnp.log(total)
    return handed, logprob.reshape(-1)


def solution(mesh):
    placed = (
        P("section", "tensor", None),
        P("section", None),
        P("section", None),
        P("section", None, "tensor"),
        P("section", None, "tensor", None),
        P("section", "tensor", None),
        P(),
        P(None, ("section", "tensor")),
        P(),
    )
    return jax.shard_map(
        body,
        mesh=mesh,
        in_specs=placed,
        out_specs=(P("section", "tensor", None), P("tensor")),
        check_vma=False,
    )
```

time: 532 us -> 183 us (0.34)
  waiting for transfers between devices: 337 us -> 90.5 us
  blocking collectives: 130 us -> 0 us
  starting transfers between devices: 5.04 us -> 52 us
  matrix products: 21.7 us -> 0 us
  Pallas kernels: 0 us -> 21.5 us
  between operations: 13.9 us -> 1.22 us
    psum x1 -> x0, waiting for transfers between devices: 141 us -> none  [broadcast(): return lax.psum(block, axis)]
    all_gather x2 -> x0, waiting for transfers between devices: 95.8 us -> none  [the longest x1 51.5 us: body(): all_rows = lax.all_gather(final_rows, 'tensor', axis=0, tiled=True)]
    reduce_scatter x1 -> x0, waiting for transfers between devices: 91 us -> none  [body(): lax.psum_scatter(jnp.dot(context, output_weight, preferred_element_type=j...]
    ppermute x1 -> x36, waiting for transfers between devices: 8.88 us -> 80.8 us  [the longest x27 62.1 us: over_tensor(): return lax.ppermute(block, 'tensor', pairs)]
    pmax x1 -> x0, blocking collectives: 67.4 us -> none  [body(): row_top = lax.pmax(local_top, ('section', 'tensor'))]
    psum x1 -> x0, blocking collectives: 62.6 us -> none  [body(): lax.psum((local_total * jnp.exp(local_top - row_top), local_pick), ('sect...]
    ppermute x1 -> x36, starting transfers between devices: 4.87 us -> 43.9 us  [the longest x27 30.1 us: over_tensor(): return lax.ppermute(block, 'tensor', pairs)]
    dot_general x6 -> x0, matrix products: 21.7 us -> none  [the longest x1 5.76 us: body(): jnp.dot(context, output_weight, preferred_element_type=jnp.float32)]
  transfers between devices with their start and end apart: 5 -> 37, of which waited for: 5 -> 20; matrix products, arithmetic and copies ran while one was open for 2% -> 4% of each run, Pallas kernels for 0% -> 2%
where the time goes in v1:
time: 183 us; the launch traced here: 182 us
  waiting for transfers between devices  90.5 us (49%)
  starting transfers between devices  52 us (28%)
  Pallas kernels  21.5 us (12%)
  local copies, waits for them, and re-layouts  8.86 us (5%)
  other arithmetic  8.08 us (4%)
    ppermute x27, waiting for transfers between devices, over_tensor(): return lax.ppermute(block, 'tensor', pairs)  62.1 us
    ppermute x27, starting transfers between devices, over_tensor(): return lax.ppermute(block, 'tensor', pairs)  30.1 us
    ppermute x9, waiting for transfers between devices, over_section(): return lax.ppermute(block, 'section', pairs)  18.7 us
    pallas_call x1, Pallas kernels, layer(): pl.pallas_call(layer_kernel, out_shape=[jax.ShapeDtypeStruct((n, WIDTH),...  17.7 us
    ppermute x9, starting transfers between devices, over_section(): return lax.ppermute(block, 'section', pairs)  13.8 us
    all_to_all x1, waiting for transfers between devices, body(): got = lax.all_to_all(sent, ('section', 'tensor'), 0, 0, tiled=True)  9.77 us
    all_to_all x1, starting transfers between devices, body(): got = lax.all_to_all(sent, ('section', 'tensor'), 0, 0, tiled=True)  8.05 us
    unnamed x21, local copies, waits for them, and re-layouts  4.32 us
  transfers between devices with their start and end apart: 37, of which 20 were waited for; matrix products, arithmetic and copies ran while one was open for 4% of the time, Pallas kernels for 2%

profile of v1, /device:TPU:1, one launch (start us, length us, event | category | flops | bytes accessed | tf_op | source)
XLA Modules:
  0.0 182.2 jit_solution(9362907900164958308)
XLA Ops:
  3.9 2.5 %collective-permute-start.1 = (bf16[32,8192]{1,0:T(8,128)(2,1)S(1)}, bf16[32,8192]{1,0:T(8,128)(2,1)S(1)}, u32[]{:S(2)}, u32[]{:S(2)}) collective-permute-start(bf16[32,8192]{1,0:T(8,128)(2,1)S(1)} %fusion.5.refs_0_), channel_id=1, source_target_pairs={{0,1},{1,2},{2,3},{3,0},{4,5},{5,6},{6,7},{7,4},{8,9},{9,10},{10,1... | collective-permute-start | bytes 1572872 | tf_op jit(solution)/shard_map/ppermute | solution.py:46
  6.5 2.2 %collective-permute-start = (bf16[32,8192]{1,0:T(8,128)(2,1)S(1)}, bf16[32,8192]{1,0:T(8,128)(2,1)S(1)}, u32[]{:S(2)}, u32[]{:S(2)}) collective-permute-start(bf16[32,8192]{1,0:T(8,128)(2,1)S(1)} %fusion.5.refs_0_), channel_id=1, source_target_pairs={{0,3},{1,0},{2,1},{3,2},{4,7},{5,4},{6,5},{7,6},{8,11},{9,8},{10,9... | collective-permute-start | bytes 1572872 | tf_op jit(solution)/shard_map/ppermute | solution.py:46
  13.1 7.2 %collective-permute-done.1.refs_4_ = bf16[32,8192]{1,0:T(8,128)(2,1)S(1)} collective-permute-done((bf16[32,8192]{1,0:T(8,128)(2,1)S(1)}, bf16[32,8192]{1,0:T(8,128)(2,1)S(1)}, u32[]{:S(2)}, u32[]{:S(2)}) %collective-permute-start.1) | collective-permute-done | bytes 524320 | tf_op jit(solution)/shard_map/ppermute | solution.py:46
  20.4 2.7 %collective-permute-start.3 = (bf16[16,8192]{1,0:T(8,128)(2,1)S(1)}, bf16[16,8192]{1,0:T(8,128)(2,1)S(1)}, u32[]{:S(2)}, u32[]{:S(2)}) collective-permute-start(bf16[16,8192]{1,0:T(8,128)(2,1)S(1)} %slice.72), channel_id=1, source_target_pairs={{0,3},{1,0},{2,1},{3,2},{4,7},{5,4},{6,5},{7,6},{8,11},{9,8},{10,9... | collective-permute-start | bytes 786440 | tf_op jit(solution)/shard_map/ppermute | solution.py:46
  23.2 1.4 collective-permute-start.8
  25.2 2.9 %collective-permute-done.2.refs_2_ = bf16[16,8192]{1,0:T(8,128)(2,1)S(1)} collective-permute-done((bf16[16,8192]{1,0:T(8,128)(2,1)S(1)}, bf16[16,8192]{1,0:T(8,128)(2,1)S(1)}, u32[]{:S(2)}, u32[]{:S(2)}) %collective-permute-start.2) | collective-permute-done | bytes 262176 | tf_op jit(solution)/shard_map/ppermute | solution.py:46
  29.8 3.8 %collective-permute-done.6.refs_7_ = bf16[16,8192]{1,0:T(8,128)(2,1)S(1)} collective-permute-done((bf16[16,8192]{1,0:T(8,128)(2,1)S(1)}, bf16[16,8192]{1,0:T(8,128)(2,1)S(1)}, u32[]{:S(2)}, u32[]{:S(2)}) %collective-permute-start.6) | collective-permute-done | bytes 262176 | tf_op jit(solution)/shard_map/ppermute | solution.py:46
  33.6 4.0 %collective-permute-done.7.refs_8_ = bf16[16,8192]{1,0:T(8,128)(2,1)S(1)} collective-permute-done((bf16[16,8192]{1,0:T(8,128)(2,1)S(1)}, bf16[16,8192]{1,0:T(8,128)(2,1)S(1)}, u32[]{:S(2)}, u32[]{:S(2)}) %collective-permute-start.7) | collective-permute-done | bytes 262176 | tf_op jit(solution)/shard_map/ppermute | solution.py:46
  40.1 17.7 %layer.1 = (bf16[32,8192]{1,0:T(8,128)(2,1)S(1)}, bf16[32,8192]{1,0:T(8,128)(2,1)S(1)}, bf16[16,8192]{1,0:T(8,128)(2,1)S(1)}, bf16[16,8192]{1,0:T(8,128)(2,1)S(1...) custom-call(bf16[32,8192]{1,0:T(8,128)(2,1)S(1)} %fusion.5.refs_0_, ...), custom_call_target="tpu_custom_call" | custom-call | flops 6000000000 | bytes 29360128 | tf_op jit(solution)/shard_map/layer/pallas_call | solution.py:163
  59.2 2.7 %collective-permute-start.10 = (bf16[32,8192]{1,0:T(8,128)(2,1)S(1)}, bf16[32,8192]{1,0:T(8,128)(2,1)S(1)}, u32[]{:S(2)}, u32[]{:S(2)}) collective-permute-start(bf16[32,8192]{1,0:T(8,128)(2,1)S(1)} %get-tuple-element.15), channel_id=1, source_target_pairs={{0,3},{1,0},{2,1},{3,2},{4,7},{5,4},{6,5},{7,6},{8,11},{9,8},{10,9... | collective-permute-start | bytes 1572872 | tf_op jit(solution)/shard_map/ppermute | solution.py:46
  63.3 2.7 %collective-permute-start.13 = (bf16[16,8192]{1,0:T(8,128)(2,1)S(1)}, bf16[16,8192]{1,0:T(8,128)(2,1)S(1)}, u32[]{:S(2)}, u32[]{:S(2)}) collective-permute-start(bf16[16,8192]{1,0:T(8,128)(2,1)S(1)} %add_convert_fusion.4), channel_id=1, source_target_pairs={{0,3},{1,0},{2,1},{3,2},{4,7},{5,4},{6,5},{7,6},{8,11},{9,8},{10,9... | collective-permute-start | bytes 786440 | tf_op jit(solution)/shard_map/ppermute | solution.py:46
  66.0 4.3 %collective-permute-done.15 = bf16[16,8192]{1,0:T(8,128)(2,1)S(1)} collective-permute-done((bf16[16,8192]{1,0:T(8,128)(2,1)S(1)}, bf16[16,8192]{1,0:T(8,128)(2,1)S(1)}, u32[]{:S(2)}, u32[]{:S(2)}) %collective-permute-start.15) | collective-permute-done | bytes 262176 | tf_op jit(solution)/shard_map/ppermute | solution.py:46
  70.5 3.0 %collective-permute-done.9 = bf16[32,8192]{1,0:T(8,128)(2,1)S(1)} collective-permute-done((bf16[32,8192]{1,0:T(8,128)(2,1)S(1)}, bf16[32,8192]{1,0:T(8,128)(2,1)S(1)}, u32[]{:S(2)}, u32[]{:S(2)}) %collective-permute-start.9) | collective-permute-done | bytes 524320 | tf_op jit(solution)/shard_map/ppermute | solution.py:46
  74.0 2.0 %collective-permute-done.13 = bf16[16,8192]{1,0:T(8,128)(2,1)S(1)} collective-permute-done((bf16[16,8192]{1,0:T(8,128)(2,1)S(1)}, bf16[16,8192]{1,0:T(8,128)(2,1)S(1)}, u32[]{:S(2)}, u32[]{:S(2)}) %collective-permute-start.13) | collective-permute-done | bytes 262176 | tf_op jit(solution)/shard_map/ppermute | solution.py:46
  76.1 3.5 %collective-permute-start.14 = (bf16[32,8192]{1,0:T(8,128)(2,1)S(1)}, bf16[32,8192]{1,0:T(8,128)(2,1)S(1)}, u32[]{:S(2)}, u32[]{:S(2)}) collective-permute-start(bf16[32,8192]{1,0:T(8,128)(2,1)S(1)} %pad_maximum_fusion), channel_id=1, source_target_pairs={{0,3},{1,0},{2,1},{3,2},{4,7},{5,4},{6,5},{7,6},{8,11},{9,8},{10,9... | collective-permute-start | bytes 1572872 | tf_op jit(solution)/shard_map/ppermute | solution.py:46
  80.5 1.6 collective-permute-done.11
  82.1 5.1 %collective-permute-done.14 = bf16[32,8192]{1,0:T(8,128)(2,1)S(1)} collective-permute-done((bf16[32,8192]{1,0:T(8,128)(2,1)S(1)}, bf16[32,8192]{1,0:T(8,128)(2,1)S(1)}, u32[]{:S(2)}, u32[]{:S(2)}) %collective-permute-start.14) | collective-permute-done | bytes 524320 | tf_op jit(solution)/shard_map/ppermute | solution.py:46
  87.2 4.5 %collective-permute-done.17 = bf16[32,8192]{1,0:T(8,128)(2,1)S(1)} collective-permute-done((bf16[32,8192]{1,0:T(8,128)(2,1)S(1)}, bf16[32,8192]{1,0:T(8,128)(2,1)S(1)}, u32[]{:S(2)}, u32[]{:S(2)}) %collective-permute-start.17) | collective-permute-done | bytes 524320 | tf_op jit(solution)/shard_map/ppermute | solution.py:46
  97.3 4.5 %collective-permute-start.35 = (bf16[8192,256]{1,0:T(8,128)(2,1)}, bf16[8192,256]{1,0:T(8,128)(2,1)}, u32[]{:S(2)}, u32[]{:S(2)}) collective-permute-start(bf16[8192,256]{1,0:T(8,128)(2,1)} %refs_8_.1), channel_id=1, source_target_pairs={{0,8},{8,0},{16,24},{24,16},{32,40},{40,32},{48,56},{56,48},{64,72... | collective-permute-start | bytes 12582920 | tf_op jit(solution)/shard_map/ppermute | solution.py:50
  102.4 18.7 %collective-permute-done.24 = bf16[16,8192]{1,0:T(8,128)(2,1)S(1)} collective-permute-done((bf16[16,8192]{1,0:T(8,128)(2,1)S(1)}, bf16[16,8192]{1,0:T(8,128)(2,1)S(1)}, u32[]{:S(2)}, u32[]{:S(2)}) %collective-permute-start.24) | collective-permute-done | bytes 262176 | tf_op jit(solution)/shard_map/ppermute | solution.py:50
  122.0 2.7 %collective-permute-start.26 = (bf16[16,8192]{1,0:T(8,128)(2,1)S(1)}, bf16[16,8192]{1,0:T(8,128)(2,1)S(1)}, u32[]{:S(2)}, u32[]{:S(2)}) collective-permute-start(bf16[16,8192]{1,0:T(8,128)(2,1)S(1)} %broadcast_select_fusion.refs_0_), channel_id=1, source_target_pairs={{0,3},{1,0},{2,1},{3,2},{4,7},{5,4},{6,5},{7,6},{8,11},{9,8},{10,9... | collective-permute-start | bytes 786440 | tf_op jit(solution)/shard_map/ppermute | solution.py:46
  124.8 4.7 %collective-permute-done.27.refs_3_ = bf16[16,8192]{1,0:T(8,128)(2,1)S(1)} collective-permute-done((bf16[16,8192]{1,0:T(8,128)(2,1)S(1)}, bf16[16,8192]{1,0:T(8,128)(2,1)S(1)}, u32[]{:S(2)}, u32[]{:S(2)}) %collective-permute-start.27) | collective-permute-done | bytes 262176 | tf_op jit(solution)/shard_map/ppermute | solution.py:46
  129.7 2.7 %collective-permute-start.29 = (bf16[8,8192]{1,0:T(8,128)(2,1)S(1)}, bf16[8,8192]{1,0:T(8,128)(2,1)S(1)}, u32[]{:S(2)}, u32[]{:S(2)}) collective-permute-start(bf16[8,8192]{1,0:T(8,128)(2,1)S(1)} %slice.76), channel_id=1, source_target_pairs={{0,3},{1,0},{2,1},{3,2},{4,7},{5,4},{6,5},{7,6},{8,11},{9,8},{10,9... | collective-permute-start | bytes 393224 | tf_op jit(solution)/shard_map/ppermute | solution.py:46
  132.6 4.0 %collective-permute-start.18 = (bf16[32,8192]{1,0:T(8,128)(2,1)S(1)}, bf16[32,8192]{1,0:T(8,128)(2,1)S(1)}, u32[]{:S(2)}, u32[]{:S(2)}) collective-permute-start(bf16[32,8192]{1,0:T(8,128)(2,1)S(1)} %get-tuple-element.36), channel_id=1, source_target_pairs={{0,8},{8,16},{16,24},{24,32},{32,40},{40,48},{48,56},{56,64},{64,7... | collective-permute-start | bytes 1572872 | tf_op jit(solution)/shard_map/ppermute | solution.py:50
  136.8 1.4 collective-permute-start.33
  138.3 9.0 %collective-permute-done.32 = bf16[8,8192]{1,0:T(8,128)(2,1)S(1)} collective-permute-done((bf16[8,8192]{1,0:T(8,128)(2,1)S(1)}, bf16[8,8192]{1,0:T(8,128)(2,1)S(1)}, u32[]{:S(2)}, u32[]{:S(2)}) %collective-permute-start.32) | collective-permute-done | bytes 131104 | tf_op jit(solution)/shard_map/ppermute | solution.py:46
  147.3 1.4 collective-permute-done.33
  148.7 5.6 %collective-permute-done.34.refs_7_ = bf16[16,8192]{1,0:T(8,128)(2,1)S(1)} collective-permute-done((bf16[16,8192]{1,0:T(8,128)(2,1)S(1)}, bf16[16,8192]{1,0:T(8,128)(2,1)S(1)}, u32[]{:S(2)}, u32[]{:S(2)}) %collective-permute-start.34) | collective-permute-done | bytes 262176 | tf_op jit(solution)/shard_map/ppermute | solution.py:46
  154.4 2.2 %copy-done = bf16[8192,256]{1,0:T(8,128)(2,1)S(1)} copy-done((bf16[8192,256]{1,0:T(8,128)(2,1)S(1)}, bf16[8192,256]{1,0:T(8,128)(2,1)}, u32[]{:S(2)}) %copy-start) | copy-done | bytes 4194328
  156.6 3.8 %vocab.1 = f32[128,128]{1,0:T(8,128)S(1)} custom-call(bf16[16,8192]{1,0:T(8,128)(2,1)S(1)} %broadcast_select_fusion.refs_0_, bf16[16,8192]{1,0:T(8,128)(2,1)S(1)} %collective-permute-done.26.refs_1_, bf16[16,8192]{1,0:T(8,128)(2,1)S(1)} %pad_maximum_fusion.2.refs_2_, bf16[16,8192]{1,0:T(8,128)(2,1)S(1)} %collective-permute-done.27.refs_3_, ...), custom_call_target="tpu_custom_call" | custom-call | flops 1000000000 | bytes 10485760 | tf_op jit(solution)/shard_map/vocab/pallas_call | solution.py:237
  161.8 8.1 %all-to-all-start = ((f32[128,1,48]{2,1,0:T(1,128)}), f32[128,1,48]{2,1,0:T(1,128)S(1)}, u32[]{:S(2)}, u32[]{:S(2)}) async-start(f32[128,1,48]{2,1,0:T(1,128)} %bitcast.15), calls=%async_computation | async-start | bytes 131072 | tf_op jit(solution)/shard_map/all_to_all | solution.py:345
  169.8 9.8 %all-to-all-done = f32[128,1,48]{2,1,0:T(1,128)S(1)} async-done(((f32[128,1,48]{2,1,0:T(1,128)}), f32[128,1,48]{2,1,0:T(1,128)S(1)}, u32[]{:S(2)}, u32[]{:S(2)}) %all-to-all-start) | async-done | bytes 24608 | tf_op jit(solution)/shard_map/all_to_all | solution.py:345
  (139 shorter events, 28.9 us)
Async XLA Ops:
  3.9 16.3 %collective-permute-start.1 = (bf16[32,8192]{1,0:T(8,128)(2,1)S(1)}, bf16[32,8192]{1,0:T(8,128)(2,1)S(1)}, u32[]{:S(2)}, u32[]{:S(2)}) collective-permute-start(bf16[32,8192]{1,0:T(8,128)(2,1)S(1)} %fusion.5.refs_0_), channel_id=1, source_target_pairs={{0,1},{1,2},{2,3},{3,0},{4,5},{5,6},{6,7},{7,4},{8,9},{9,10},{10,1... | collective-permute-start | bytes 1572872 | tf_op jit(solution)/shard_map/ppermute | solution.py:46
  6.5 13.9 %collective-permute-start = (bf16[32,8192]{1,0:T(8,128)(2,1)S(1)}, bf16[32,8192]{1,0:T(8,128)(2,1)S(1)}, u32[]{:S(2)}, u32[]{:S(2)}) collective-permute-start(bf16[32,8192]{1,0:T(8,128)(2,1)S(1)} %fusion.5.refs_0_), channel_id=1, source_target_pairs={{0,3},{1,0},{2,1},{3,2},{4,7},{5,4},{6,5},{7,6},{8,11},{9,8},{10,9... | collective-permute-start | bytes 1572872 | tf_op jit(solution)/shard_map/ppermute | solution.py:46
  8.7 14.4 %collective-permute-start.4 = (bf16[32,8192]{1,0:T(8,128)(2,1)S(1)}, bf16[32,8192]{1,0:T(8,128)(2,1)S(1)}, u32[]{:S(2)}, u32[]{:S(2)}) collective-permute-start(bf16[32,8192]{1,0:T(8,128)(2,1)S(1)} %fusion.5.refs_0_), channel_id=1, source_target_pairs={{0,4},{1,5},{2,6},{3,7},{4,0},{5,1},{6,2},{7,3},{8,12},{9,13},{10,... | collective-permute-start | bytes 1572872 | tf_op jit(solution)/shard_map/ppermute | solution.py:46
  20.3 7.9 %collective-permute-start.2 = (bf16[16,8192]{1,0:T(8,128)(2,1)S(1)}, bf16[16,8192]{1,0:T(8,128)(2,1)S(1)}, u32[]{:S(2)}, u32[]{:S(2)}) collective-permute-start(bf16[16,8192]{1,0:T(8,128)(2,1)S(1)} %slice.71), channel_id=1, source_target_pairs={{0,1},{1,2},{2,3},{3,0},{4,5},{5,6},{6,7},{7,4},{8,9},{9,10},{10,1... | collective-permute-start | bytes 786440 | tf_op jit(solution)/shard_map/ppermute | solution.py:46
  20.4 8.9 %collective-permute-start.3 = (bf16[16,8192]{1,0:T(8,128)(2,1)S(1)}, bf16[16,8192]{1,0:T(8,128)(2,1)S(1)}, u32[]{:S(2)}, u32[]{:S(2)}) collective-permute-start(bf16[16,8192]{1,0:T(8,128)(2,1)S(1)} %slice.72), channel_id=1, source_target_pairs={{0,3},{1,0},{2,1},{3,2},{4,7},{5,4},{6,5},{7,6},{8,11},{9,8},{10,9... | collective-permute-start | bytes 786440 | tf_op jit(solution)/shard_map/ppermute | solution.py:46
  23.1 15.3 %collective-permute-start.5 = (bf16[32,8192]{1,0:T(8,128)(2,1)S(1)}, bf16[32,8192]{1,0:T(8,128)(2,1)S(1)}, u32[]{:S(2)}, u32[]{:S(2)}) collective-permute-start(bf16[32,8192]{1,0:T(8,128)(2,1)S(1)} %collective-permute-done.4.refs_5_), channel_id=1, source_target_pairs={{0,3},{1,0},{2,1},{3,2},{4,7},{5,4},{6,5},{7,6},{8,11},{9,8},{10,9... | collective-permute-start | bytes 1572872 | tf_op jit(solution)/shard_map/ppermute | solution.py:46
  23.2 16.1 %collective-permute-start.8 = (bf16[32,8192]{1,0:T(8,128)(2,1)S(1)}, bf16[32,8192]{1,0:T(8,128)(2,1)S(1)}, u32[]{:S(2)}, u32[]{:S(2)}) collective-permute-start(bf16[32,8192]{1,0:T(8,128)(2,1)S(1)} %collective-permute-done.4.refs_5_), channel_id=1, source_target_pairs={{0,1},{1,2},{2,3},{3,0},{4,5},{5,6},{6,7},{7,4},{8,9},{9,10},{10,1... | collective-permute-start | bytes 1572872 | tf_op jit(solution)/shard_map/ppermute | solution.py:46
  28.1 5.5 %collective-permute-start.6 = (bf16[16,8192]{1,0:T(8,128)(2,1)S(1)}, bf16[16,8192]{1,0:T(8,128)(2,1)S(1)}, u32[]{:S(2)}, u32[]{:S(2)}) collective-permute-start(bf16[16,8192]{1,0:T(8,128)(2,1)S(1)} %collective-permute-done.2.refs_2_), channel_id=1, source_target_pairs={{0,4},{1,5},{2,6},{3,7},{4,0},{5,1},{6,2},{7,3},{8,12},{9,13},{10,... | collective-permute-start | bytes 786440 | tf_op jit(solution)/shard_map/ppermute | solution.py:46
  29.3 8.3 %collective-permute-start.7 = (bf16[16,8192]{1,0:T(8,128)(2,1)S(1)}, bf16[16,8192]{1,0:T(8,128)(2,1)S(1)}, u32[]{:S(2)}, u32[]{:S(2)}) collective-permute-start(bf16[16,8192]{1,0:T(8,128)(2,1)S(1)} %collective-permute-done.3.refs_3_), channel_id=1, source_target_pairs={{0,4},{1,5},{2,6},{3,7},{4,0},{5,1},{6,2},{7,3},{8,12},{9,13},{10,... | collective-permute-start | bytes 786440 | tf_op jit(solution)/shard_map/ppermute | solution.py:46
  57.9 5.3 %collective-permute-start.12 = (bf16[16,8192]{1,0:T(8,128)(2,1)S(1)}, bf16[16,8192]{1,0:T(8,128)(2,1)S(1)}, u32[]{:S(2)}, u32[]{:S(2)}) collective-permute-start(bf16[16,8192]{1,0:T(8,128)(2,1)S(1)} %get-tuple-element.18), channel_id=1, source_target_pairs={{0,4},{1,5},{2,6},{3,7},{4,0},{5,1},{6,2},{7,3},{8,12},{9,13},{10,... | collective-permute-start | bytes 786440 | tf_op jit(solution)/shard_map/ppermute | solution.py:46
  59.2 11.3 %collective-permute-start.10 = (bf16[32,8192]{1,0:T(8,128)(2,1)S(1)}, bf16[32,8192]{1,0:T(8,128)(2,1)S(1)}, u32[]{:S(2)}, u32[]{:S(2)}) collective-permute-start(bf16[32,8192]{1,0:T(8,128)(2,1)S(1)} %get-tuple-element.15), channel_id=1, source_target_pairs={{0,3},{1,0},{2,1},{3,2},{4,7},{5,4},{6,5},{7,6},{8,11},{9,8},{10,9... | collective-permute-start | bytes 1572872 | tf_op jit(solution)/shard_map/ppermute | solution.py:46
  61.9 11.6 %collective-permute-start.9 = (bf16[32,8192]{1,0:T(8,128)(2,1)S(1)}, bf16[32,8192]{1,0:T(8,128)(2,1)S(1)}, u32[]{:S(2)}, u32[]{:S(2)}) collective-permute-start(bf16[32,8192]{1,0:T(8,128)(2,1)S(1)} %get-tuple-element.14), channel_id=1, source_target_pairs={{0,1},{1,2},{2,3},{3,0},{4,5},{5,6},{6,7},{7,4},{8,9},{9,10},{10,1... | collective-permute-start | bytes 1572872 | tf_op jit(solution)/shard_map/ppermute | solution.py:46
  61.9 8.4 %collective-permute-start.15 = (bf16[16,8192]{1,0:T(8,128)(2,1)S(1)}, bf16[16,8192]{1,0:T(8,128)(2,1)S(1)}, u32[]{:S(2)}, u32[]{:S(2)}) collective-permute-start(bf16[16,8192]{1,0:T(8,128)(2,1)S(1)} %get-tuple-element.21), channel_id=1, source_target_pairs={{0,4},{1,5},{2,6},{3,7},{4,0},{5,1},{6,2},{7,3},{8,12},{9,13},{10,... | collective-permute-start | bytes 786440 | tf_op jit(solution)/shard_map/ppermute | solution.py:46
  63.3 12.7 %collective-permute-start.13 = (bf16[16,8192]{1,0:T(8,128)(2,1)S(1)}, bf16[16,8192]{1,0:T(8,128)(2,1)S(1)}, u32[]{:S(2)}, u32[]{:S(2)}) collective-permute-start(bf16[16,8192]{1,0:T(8,128)(2,1)S(1)} %add_convert_fusion.4), channel_id=1, source_target_pairs={{0,3},{1,0},{2,1},{3,2},{4,7},{5,4},{6,5},{7,6},{8,11},{9,8},{10,9... | collective-permute-start | bytes 786440 | tf_op jit(solution)/shard_map/ppermute | solution.py:46
  70.4 9.7 %collective-permute-start.16 = (bf16[16,8192]{1,0:T(8,128)(2,1)S(1)}, bf16[16,8192]{1,0:T(8,128)(2,1)S(1)}, u32[]{:S(2)}, u32[]{:S(2)}) collective-permute-start(bf16[16,8192]{1,0:T(8,128)(2,1)S(1)} %add_convert_fusion.2), channel_id=1, source_target_pairs={{0,1},{1,2},{2,3},{3,0},{4,5},{5,6},{6,7},{7,4},{8,9},{9,10},{10,1... | collective-permute-start | bytes 786440 | tf_op jit(solution)/shard_map/ppermute | solution.py:46
  73.7 8.4 %collective-permute-start.11 = (bf16[32,8192]{1,0:T(8,128)(2,1)S(1)}, bf16[32,8192]{1,0:T(8,128)(2,1)S(1)}, u32[]{:S(2)}, u32[]{:S(2)}) collective-permute-start(bf16[32,8192]{1,0:T(8,128)(2,1)S(1)} %add_convert_fusion), channel_id=1, source_target_pairs={{0,4},{1,5},{2,6},{3,7},{4,0},{5,1},{6,2},{7,3},{8,12},{9,13},{10,... | collective-permute-start | bytes 1572872 | tf_op jit(solution)/shard_map/ppermute | solution.py:46
  76.1 11.1 %collective-permute-start.14 = (bf16[32,8192]{1,0:T(8,128)(2,1)S(1)}, bf16[32,8192]{1,0:T(8,128)(2,1)S(1)}, u32[]{:S(2)}, u32[]{:S(2)}) collective-permute-start(bf16[32,8192]{1,0:T(8,128)(2,1)S(1)} %pad_maximum_fusion), channel_id=1, source_target_pairs={{0,3},{1,0},{2,1},{3,2},{4,7},{5,4},{6,5},{7,6},{8,11},{9,8},{10,9... | collective-permute-start | bytes 1572872 | tf_op jit(solution)/shard_map/ppermute | solution.py:46
  80.2 11.5 %collective-permute-start.17 = (bf16[32,8192]{1,0:T(8,128)(2,1)S(1)}, bf16[32,8192]{1,0:T(8,128)(2,1)S(1)}, u32[]{:S(2)}, u32[]{:S(2)}) collective-permute-start(bf16[32,8192]{1,0:T(8,128)(2,1)S(1)} %pad_maximum_fusion.1), channel_id=1, source_target_pairs={{0,1},{1,2},{2,3},{3,0},{4,5},{5,6},{6,7},{7,4},{8,9},{9,10},{10,1... | collective-permute-start | bytes 1572872 | tf_op jit(solution)/shard_map/ppermute | solution.py:46
  95.3 7.1 %collective-permute-start.23 = (bf16[16,8192]{1,0:T(8,128)(2,1)S(1)}, bf16[16,8192]{1,0:T(8,128)(2,1)S(1)}, u32[]{:S(2)}, u32[]{:S(2)}) collective-permute-start(bf16[16,8192]{1,0:T(8,128)(2,1)S(1)} %select_select_fusion.1), channel_id=1, source_target_pairs={{16,48},{24,56},{17,49},{25,57},{18,50},{26,58},{19,51},{27,59},{2... | collective-permute-start | bytes 786440 | tf_op jit(solution)/shard_map/ppermute | solution.py:50
  96.0 25.1 %collective-permute-start.24 = (bf16[16,8192]{1,0:T(8,128)(2,1)S(1)}, bf16[16,8192]{1,0:T(8,128)(2,1)S(1)}, u32[]{:S(2)}, u32[]{:S(2)}) collective-permute-start(bf16[16,8192]{1,0:T(8,128)(2,1)S(1)} %select_select_fusion.1), channel_id=1, source_target_pairs={{16,0},{24,8},{80,64},{88,72},{17,1},{25,9},{81,65},{89,73},{18,2}... | collective-permute-start | bytes 786440 | tf_op jit(solution)/shard_map/ppermute | solution.py:50
  97.3 57.1 %collective-permute-start.35 = (bf16[8192,256]{1,0:T(8,128)(2,1)}, bf16[8192,256]{1,0:T(8,128)(2,1)}, u32[]{:S(2)}, u32[]{:S(2)}) collective-permute-start(bf16[8192,256]{1,0:T(8,128)(2,1)} %refs_8_.1), channel_id=1, source_target_pairs={{0,8},{8,0},{16,24},{24,16},{32,40},{40,32},{48,56},{56,48},{64,72... | collective-permute-start | bytes 12582920 | tf_op jit(solution)/shard_map/ppermute | solution.py:50
  121.9 7.6 %collective-permute-start.27 = (bf16[16,8192]{1,0:T(8,128)(2,1)S(1)}, bf16[16,8192]{1,0:T(8,128)(2,1)S(1)}, u32[]{:S(2)}, u32[]{:S(2)}) collective-permute-start(bf16[16,8192]{1,0:T(8,128)(2,1)S(1)} %broadcast_select_fusion.refs_0_), channel_id=1, source_target_pairs={{0,1},{1,2},{2,3},{3,0},{4,5},{5,6},{6,7},{7,4},{8,9},{9,10},{10,1... | collective-permute-start | bytes 786440 | tf_op jit(solution)/shard_map/ppermute | solution.py:46
  122.0 7.6 %collective-permute-start.26 = (bf16[16,8192]{1,0:T(8,128)(2,1)S(1)}, bf16[16,8192]{1,0:T(8,128)(2,1)S(1)}, u32[]{:S(2)}, u32[]{:S(2)}) collective-permute-start(bf16[16,8192]{1,0:T(8,128)(2,1)S(1)} %broadcast_select_fusion.refs_0_), channel_id=1, source_target_pairs={{0,3},{1,0},{2,1},{3,2},{4,7},{5,4},{6,5},{7,6},{8,11},{9,8},{10,9... | collective-permute-start | bytes 786440 | tf_op jit(solution)/shard_map/ppermute | solution.py:46
  124.7 11.9 %collective-permute-start.30 = (bf16[16,8192]{1,0:T(8,128)(2,1)S(1)}, bf16[16,8192]{1,0:T(8,128)(2,1)S(1)}, u32[]{:S(2)}, u32[]{:S(2)}) collective-permute-start(bf16[16,8192]{1,0:T(8,128)(2,1)S(1)} %broadcast_select_fusion.refs_0_), channel_id=1, source_target_pairs={{0,4},{1,5},{2,6},{3,7},{4,0},{5,1},{6,2},{7,3},{8,12},{9,13},{10,... | collective-permute-start | bytes 786440 | tf_op jit(solution)/shard_map/ppermute | solution.py:46
  129.6 7.2 %collective-permute-start.28 = (bf16[8,8192]{1,0:T(8,128)(2,1)S(1)}, bf16[8,8192]{1,0:T(8,128)(2,1)S(1)}, u32[]{:S(2)}, u32[]{:S(2)}) collective-permute-start(bf16[8,8192]{1,0:T(8,128)(2,1)S(1)} %slice.75), channel_id=1, source_target_pairs={{0,1},{1,2},{2,3},{3,0},{4,5},{5,6},{6,7},{7,4},{8,9},{9,10},{10,1... | collective-permute-start | bytes 393224 | tf_op jit(solution)/shard_map/ppermute | solution.py:46
  129.7 7.2 %collective-permute-start.29 = (bf16[8,8192]{1,0:T(8,128)(2,1)S(1)}, bf16[8,8192]{1,0:T(8,128)(2,1)S(1)}, u32[]{:S(2)}, u32[]{:S(2)}) collective-permute-start(bf16[8,8192]{1,0:T(8,128)(2,1)S(1)} %slice.76), channel_id=1, source_target_pairs={{0,3},{1,0},{2,1},{3,2},{4,7},{5,4},{6,5},{7,6},{8,11},{9,8},{10,9... | collective-permute-start | bytes 393224 | tf_op jit(solution)/shard_map/ppermute | solution.py:46
  132.6 37.2 %collective-permute-start.18 = (bf16[32,8192]{1,0:T(8,128)(2,1)S(1)}, bf16[32,8192]{1,0:T(8,128)(2,1)S(1)}, u32[]{:S(2)}, u32[]{:S(2)}) collective-permute-start(bf16[32,8192]{1,0:T(8,128)(2,1)S(1)} %get-tuple-element.36), channel_id=1, source_target_pairs={{0,8},{8,16},{16,24},{24,32},{32,40},{40,48},{48,56},{56,64},{64,7... | collective-permute-start | bytes 1572872 | tf_op jit(solution)/shard_map/ppermute | solution.py:50
  136.7 12.1 %collective-permute-start.31 = (bf16[16,8192]{1,0:T(8,128)(2,1)S(1)}, bf16[16,8192]{1,0:T(8,128)(2,1)S(1)}, u32[]{:S(2)}, u32[]{:S(2)}) collective-permute-start(bf16[16,8192]{1,0:T(8,128)(2,1)S(1)} %collective-permute-done.30.refs_4_), channel_id=1, source_target_pairs={{0,3},{1,0},{2,1},{3,2},{4,7},{5,4},{6,5},{7,6},{8,11},{9,8},{10,9... | collective-permute-start | bytes 786440 | tf_op jit(solution)/shard_map/ppermute | solution.py:46
  136.7 10.5 %collective-permute-start.32 = (bf16[8,8192]{1,0:T(8,128)(2,1)S(1)}, bf16[8,8192]{1,0:T(8,128)(2,1)S(1)}, u32[]{:S(2)}, u32[]{:S(2)}) collective-permute-start(bf16[8,8192]{1,0:T(8,128)(2,1)S(1)} %collective-permute-done.28), channel_id=1, source_target_pairs={{0,4},{1,5},{2,6},{3,7},{4,0},{5,1},{6,2},{7,3},{8,12},{9,13},{10,... | collective-permute-start | bytes 393224 | tf_op jit(solution)/shard_map/ppermute | solution.py:46
  136.8 11.8 %collective-permute-start.33 = (bf16[8,8192]{1,0:T(8,128)(2,1)S(1)}, bf16[8,8192]{1,0:T(8,128)(2,1)S(1)}, u32[]{:S(2)}, u32[]{:S(2)}) collective-permute-start(bf16[8,8192]{1,0:T(8,128)(2,1)S(1)} %collective-permute-done.29), channel_id=1, source_target_pairs={{0,4},{1,5},{2,6},{3,7},{4,0},{5,1},{6,2},{7,3},{8,12},{9,13},{10,... | collective-permute-start | bytes 393224 | tf_op jit(solution)/shard_map/ppermute | solution.py:46
  147.3 7.0 %collective-permute-start.34 = (bf16[16,8192]{1,0:T(8,128)(2,1)S(1)}, bf16[16,8192]{1,0:T(8,128)(2,1)S(1)}, u32[]{:S(2)}, u32[]{:S(2)}) collective-permute-start(bf16[16,8192]{1,0:T(8,128)(2,1)S(1)} %collective-permute-done.30.refs_4_), channel_id=1, source_target_pairs={{0,1},{1,2},{2,3},{3,0},{4,5},{5,6},{6,7},{7,4},{8,9},{9,10},{10,1... | collective-permute-start | bytes 786440 | tf_op jit(solution)/shard_map/ppermute | solution.py:46
  161.8 17.8 %all-to-all-start = ((f32[128,1,48]{2,1,0:T(1,128)}), f32[128,1,48]{2,1,0:T(1,128)S(1)}, u32[]{:S(2)}, u32[]{:S(2)}) async-start(f32[128,1,48]{2,1,0:T(1,128)} %bitcast.15), calls=%async_computation | async-start | bytes 131072 | tf_op jit(solution)/shard_map/all_to_all | solution.py:345
  (14 other events, 134.0 us)

commit v2 on v0

v2 whole, which is shorter than its diff:
```python
import math

import jax
import jax.numpy as jnp
from jax import lax
from jax.experimental import pallas as pl
from jax.experimental.pallas import tpu as pltpu
from jax.sharding import PartitionSpec as P

NORM_EPSILON = 1e-05
ROPE_THETA = 500000.0
BF16 = jnp.bfloat16
F32 = jnp.float32
NZ = 4
ROWS = 32
HALF = 16
WIDTH = 8192
HEAD = 128
HEADS = 4
MB = 128
VL = 256


def tensor_pairs(step):
    out = []
    for x in range(2):
        for z in range(NZ):
            x2, z2 = step(x, z)
            out.append((x * NZ + z, (x2 % 2) * NZ + z2 % NZ))
    return out


TO_X = tensor_pairs(lambda x, z: (x + 1, z))
TO_UP = tensor_pairs(lambda x, z: (x, z + 1))
TO_DOWN = tensor_pairs(lambda x, z: (x, z - 1))


def sec(y, h, c):
    return ((y % 4) * 2 + h % 2) * 2 + c


def over_tensor(block, pairs):
    return lax.ppermute(block, "tensor", pairs)


def over_section(block, pairs):
    return lax.ppermute(block, "section", pairs)


def rms_norm(row_block, gain_row):
    values = row_block.astype(F32)
    factor = lax.rsqrt(jnp.mean(values * values, axis=-1, keepdims=True) + NORM_EPSILON)
    return (values * factor * gain_row.astype(F32)).astype(BF16)


def gather_rows(own):
    half = own.shape[0] // 2

    def move(block, pairs):
        return over_tensor(block, pairs)

    from_x = move(own, TO_X)
    below = move(own, TO_UP)
    above = move(own, TO_DOWN)
    far_a = move(below[:half], TO_UP)
    far_b = move(above[half:], TO_DOWN)
    x_below = move(from_x, TO_UP)
    x_above = move(from_x, TO_DOWN)
    x_far_a = move(far_a, TO_X)
    x_far_b = move(far_b, TO_X)
    return own, above, far_a, far_b, below, from_x, x_above, x_far_a, x_far_b, x_below


def scatter_sum(parts, my_rows):
    def move(block, pairs):
        return over_tensor(block, pairs)

    own, above, far_a, far_b, below, x_own, x_above, x_far_a, x_far_b, x_below = parts
    got_far_a = move(x_far_a, TO_X)
    got_far_b = move(x_far_b, TO_X)
    got_x_down = move(x_above, TO_UP)
    got_x_up = move(x_below, TO_DOWN)
    far_a = add(far_a, got_far_a).astype(BF16)
    far_b = add(far_b, got_far_b).astype(BF16)
    got_a = move(far_a, TO_DOWN)
    got_b = move(far_b, TO_UP)
    x_own = add(x_own, got_x_down, got_x_up).astype(BF16)
    got_x = move(x_own, TO_X)
    below = jnp.concatenate([add(below[:HALF], got_a), below[HALF:].astype(F32)], axis=0).astype(BF16)
    above = jnp.concatenate([above[:HALF].astype(F32), add(above[HALF:], got_b)], axis=0).astype(BF16)
    got_down = move(below, TO_DOWN)
    got_up = move(above, TO_UP)
    return add(my_rows, own, got_x, got_down, got_up).astype(BF16)


LAYER_ROWS = [(0, 32), (32, 32), (64, 16), (80, 16), (96, 32), (128, 32), (160, 32), (192, 16), (208, 16), (224, 32)]
KC = 2048
NC = 2048
QKV = (HEADS + 2) * HEAD


def at(k, size):
    return pl.ds(pl.multiple_of(k * size, size), size)


def layer_kernel(*refs):
    blocks = refs[:10]
    wq_ref, wkv_ref, wo_ref, cos_ref, sin_ref, allow_ref = refs[10:16]
    outs = refs[16:26]
    rows, w, wo, acc, ctx, res, row_sem, w_sem, wo_sem, out_sem = refs[26:]

    for b, (r, n) in zip(blocks, LAYER_ROWS):
        pltpu.make_async_copy(b, rows.at[pl.ds(r, n)], row_sem).start()

    @pl.loop(0, WIDTH // KC)
    def _(k):
        cols = at(k, KC)
        q_cols, kv_cols = pl.ds(0, HEADS * HEAD), pl.ds(HEADS * HEAD, 2 * HEAD)
        pltpu.make_async_copy(wq_ref.at[cols], w.at[cols, q_cols], w_sem.at[k]).start()
        pltpu.make_async_copy(wkv_ref.at[cols], w.at[cols, kv_cols], w_sem.at[k]).start()

    @pl.loop(0, WIDTH // NC)
    def _(n):
        cols = at(n, NC)
        pltpu.make_async_copy(wo_ref.at[:, cols], wo.at[:, cols], wo_sem.at[n]).start()

    acc[...] = jnp.zeros_like(acc)
    pltpu.make_async_copy(rows, rows, row_sem).wait()

    @pl.loop(0, WIDTH // KC)
    def _(k):
        cols = at(k, KC)
        pltpu.make_async_copy(w.at[cols], w.at[cols], w_sem.at[k]).wait()
        acc[...] += jnp.dot(rows[:, cols], w[cols, :], preferred_element_type=F32)

    cos, sin = cos_ref[...], sin_ref[...]

    def rotated(h):
        v = acc[:, h * HEAD : (h + 1) * HEAD]
        return (v * cos + pltpu.roll(v, HEAD // 2, 1) * sin).astype(BF16)

    keys = rotated(HEADS)
    values = acc[:, (HEADS + 1) * HEAD :].astype(BF16)
    heads = [rotated(h) for h in range(HEADS)]
    for b in range(2):
        mb = slice(b * MB, (b + 1) * MB)
        allow = jnp.concatenate([allow_ref[mb, :]] * HEADS, axis=0) > 0
        q = jnp.concatenate([head[mb] for head in heads], axis=0)
        s = lax.dot_general(q, keys[mb], (((1,), (1,)), ((), ())), preferred_element_type=F32)
        s = jnp.where(allow, s * (1.0 / math.sqrt(HEAD)), -jnp.inf)
        e = jnp.exp(s - jnp.max(s, axis=1, keepdims=True))
        p = (e / jnp.sum(e, axis=1, keepdims=True)).astype(BF16)
        c = jnp.dot(p, values[mb], preferred_element_type=F32).astype(BF16)
        for h in range(HEADS):
            ctx[mb, h * HEAD : (h + 1) * HEAD] = c[h * MB : (h + 1) * MB]

    @pl.loop(0, WIDTH // NC)
    def _(n):
        cols = at(n, NC)
        pltpu.make_async_copy(wo.at[:, cols], wo.at[:, cols], wo_sem.at[n]).wait()
        res[:, cols] = jnp.dot(ctx[...], wo[:, cols], preferred_element_type=F32).astype(BF16)
        for o, (r, m) in zip(outs, LAYER_ROWS):
            pltpu.make_async_copy(res.at[pl.ds(r, m), cols], o.at[:, cols], out_sem).start()

    pltpu.make_async_copy(res, res, out_sem).wait()


def layer(blocks, wq, wkv, wo, cos, sin, allow):
    hbm = pl.BlockSpec(memory_space=pl.ANY)
    vmem = pl.BlockSpec(memory_space=pltpu.VMEM)
    return pl.pallas_call(
        layer_kernel,
        out_shape=[jax.ShapeDtypeStruct((n, WIDTH), BF16) for _, n in LAYER_ROWS],
        in_specs=[hbm] * 13 + [vmem] * 3,
        out_specs=[hbm] * 10,
        scratch_shapes=[
            pltpu.VMEM((2 * MB, WIDTH), BF16),
            pltpu.VMEM((WIDTH, QKV), BF16),
            pltpu.VMEM((HEADS * HEAD, WIDTH), BF16),
            pltpu.VMEM((2 * MB, QKV), F32),
            pltpu.VMEM((2 * MB, HEADS * HEAD), BF16),
            pltpu.VMEM((2 * MB, WIDTH), BF16),
            pltpu.SemaphoreType.DMA,
            pltpu.SemaphoreType.DMA((WIDTH // KC,)),
            pltpu.SemaphoreType.DMA((WIDTH // NC,)),
            pltpu.SemaphoreType.DMA,
        ],
        compiler_params=pltpu.CompilerParams(vmem_limit_bytes=48 * 1024 * 1024),
        cost_estimate=pl.CostEstimate(flops=6 * 10**9, bytes_accessed=28 * 2**20, transcendentals=0),
        name="layer",
    )(*blocks, wq, wkv, wo, cos, sin, allow)


VC = 2048


def vocab_kernel(*refs):
    blocks = refs[:10]
    w0_ref, w1_ref, want_ref, out_ref, rows, w, acc, row_sem, w_sem = refs[10:]

    for b, (r, n) in zip(blocks, LAYER_ROWS):
        pltpu.make_async_copy(b, rows.at[pl.ds(r, n)], row_sem).start()

    @pl.loop(0, WIDTH // VC, unroll=True)
    def _(k):
        cols = at(k, VC)
        for i, r in enumerate((w0_ref, w1_ref)):
            pltpu.make_async_copy(r.at[cols], w.at[cols, pl.ds(i * VL, VL)], w_sem.at[k]).start()

    acc[...] = jnp.zeros_like(acc)
    pltpu.make_async_copy(rows, rows, row_sem).wait()

    @pl.loop(0, WIDTH // VC, unroll=True)
    def _(k):
        cols = at(k, VC)
        pltpu.make_async_copy(w.at[cols], w.at[cols], w_sem.at[k]).wait()
        acc[...] += jnp.dot(rows[:, cols], w[cols, :], preferred_element_type=F32)

    logits = acc[...]
    top = jnp.max(logits, axis=1, keepdims=True)
    total = jnp.sum(jnp.exp(logits - top), axis=1, keepdims=True)
    column = lax.broadcasted_iota(jnp.int32, logits.shape, 1)
    picked = jnp.sum(jnp.where(column == want_ref[:, :1], logits, 0.0), axis=1, keepdims=True)
    lane = lax.broadcasted_iota(jnp.int32, (2 * MB, 128), 1)
    out_ref[...] = jnp.where(lane == 0, top, jnp.where(lane == 1, total, picked))


def vocab(blocks, w0, w1, want):
    hbm = pl.BlockSpec(memory_space=pl.ANY)
    vmem = pl.BlockSpec(memory_space=pltpu.VMEM)
    return pl.pallas_call(
        vocab_kernel,
        out_shape=jax.ShapeDtypeStruct((2 * MB, 128), F32),
        in_specs=[hbm] * 12 + [vmem],
        out_specs=vmem,
        scratch_shapes=[
            pltpu.VMEM((2 * MB, WIDTH), BF16),
            pltpu.VMEM((WIDTH, 2 * VL), BF16),
            pltpu.VMEM((2 * MB, 2 * VL), F32),
            pltpu.SemaphoreType.DMA,
            pltpu.SemaphoreType.DMA((WIDTH // VC,)),
        ],
        compiler_params=pltpu.CompilerParams(vmem_limit_bytes=48 * 1024 * 1024),
        cost_estimate=pl.CostEstimate(flops=2 * 10**9, bytes_accessed=14 * 2**20, transcendentals=0),
        name="vocab",
    )(*blocks, w0, w1, want)


def add(*terms):
    return sum(t.astype(F32) for t in terms)


def spread_from_last(final_rows, section):
    y = section // 4

    def hop(block, moves):
        return over_section(block, [(sec(*a, 1), sec(*b, 1)) for a, b in moves])

    side = hop(final_rows, [((3, 1), (3, 0))])
    rows = jnp.where(section == 15, final_rows, side)
    up = hop(rows, [((3, h), (0, h)) for h in range(2)])
    down = hop(rows, [((3, h), (2, h)) for h in range(2)])
    across = hop(rows, [((3, h), (1, h)) for h in range(2)])
    return jnp.where(y == 3, rows, jnp.where(y == 0, up, jnp.where(y == 2, down, across)))


def body(
    section_input, positions, attn_gain, w_query, w_keyval, w_out_proj, final_gain, w_vocab, targets
):
    section, rank = lax.axis_index("section"), lax.axis_index("tensor")
    core, x, z = section % 2, rank // NZ, rank % NZ
    my_rows = section_input[0]
    normed = rms_norm(my_rows, attn_gain[0])
    other_vocab = over_section(w_vocab, [(s, s + 1) for s in range(0, 16, 2)])
    xs = jnp.stack([x, 1 - x])
    zs = (z + jnp.arange(NZ)) % NZ
    order = (xs[:, None] * NZ + zs[None, :]).reshape(-1)

    def tables():
        place = ((zs * ROWS)[:, None] + jnp.arange(ROWS)[None, :]).reshape(-1)
        pos = jnp.take(positions[0].reshape(8, ROWS), order, axis=0).reshape(-1)
        place2 = jnp.concatenate([place, place])
        frequency = ROPE_THETA ** (-jnp.arange(HEAD // 2, dtype=F32) * 2.0 / HEAD)
        angles = pos.astype(F32)[:, None] * frequency[None, :]
        cos, sin = jnp.cos(angles), jnp.sin(angles)
        cos = jnp.concatenate([cos, cos], axis=1)
        sin = jnp.concatenate([-sin, sin], axis=1)
        keys_at = place[None, :]
        allow = ((keys_at <= place2[:, None]) & (keys_at >= (place2 - pos)[:, None])).astype(F32)

        starts = jnp.stack([section, section ^ 1]) * 8 * VL + rank * VL
        want = jnp.take(targets.reshape(8, ROWS), order, axis=0).reshape(-1)
        local = want[:, None] - starts[None, :]
        inside = (local >= 0) & (local < VL)
        want = jnp.max(jnp.where(inside, local + jnp.arange(2)[None, :] * VL, -1), axis=1)
        want = jnp.broadcast_to(want[:, None], (2 * MB, 128))
        return cos, sin, allow, want

    odd_blocks, mark, (cos, sin, allow, want) = lax.cond(
        core == 1,
        lambda rows: (gather_rows(rows)[1:], rows[:HALF, :HEAD], tables()),
        lambda rows: (
            tuple(jnp.zeros((n, WIDTH), BF16) for _, n in LAYER_ROWS[1:]),
            rows[:HALF, :HEAD],
            tables(),
        ),
        normed,
    )
    token = over_section(mark, [(s, s - 1) for s in range(1, 16, 2)])
    weights = (w_query[0], w_keyval[0].reshape(WIDTH, -1), w_out_proj[0], cos, sin, allow)

    def odd_path():
        parts = layer((normed, *odd_blocks), *weights)
        layer_out = scatter_sum(parts, my_rows)
        mine = spread_from_last(rms_norm(layer_out, final_gain), section)
        stats = vocab(gather_rows(mine), w_vocab, other_vocab, want)
        return layer_out, stats[:, :3]

    def even_path():
        later = jnp.where(token[0, 0] > 1e4, jnp.zeros_like(normed), normed)
        parts = layer(gather_rows(later), *weights)
        return scatter_sum(parts, my_rows), jnp.zeros((2 * MB, 3), F32)

    layer_out, stats = lax.cond(core == 1, odd_path, even_path)
    handed = over_section(layer_out, [(s, s + 1) for s in range(15)])[None]
    rank_x, rank_z = jnp.arange(8) // NZ, jnp.arange(8) % NZ
    seen_at = (rank_x ^ x) * NZ + (rank_z - z) % NZ
    stats = jnp.take(stats.reshape(8, ROWS * 3), seen_at, axis=0)
    sent = jnp.broadcast_to(stats[None], (16, 8, ROWS * 3)).reshape(128, ROWS * 3)
    got = lax.all_to_all(sent, ("section", "tensor"), 0, 0, tiled=True)
    got = got.reshape(8, 2, 8, ROWS, 3)[:, 1]
    tops, totals, picks = got[..., 0], got[..., 1], got[..., 2]
    top = jnp.max(tops, axis=(0, 1))
    total = jnp.sum(totals * jnp.exp(tops - top), axis=(0, 1))
    logprob = jnp.sum(picks, axis=(0, 1)) - top - jnp.log(total)
    return handed, logprob


def solution(mesh):
    placed = (
        P("section", "tensor", None),
        P("section", None),
        P("section", None),
        P("section", None, "tensor"),
        P("section", None, "tensor", None),
        P("section", "tensor", None),
        P(),
        P(None, ("section", "tensor")),
        P(),
    )
    return jax.shard_map(
        body,
        mesh=mesh,
        in_specs=placed,
        out_specs=(P("section", "tensor", None), P("tensor")),
        check_vma=False,
    )
```

time: 532 us -> 168 us (0.32)
  waiting for transfers between devices: 337 us -> 65.2 us
  blocking collectives: 130 us -> 20.5 us
  starting transfers between devices: 5.04 us -> 39.5 us
  matrix products: 21.7 us -> 0 us
  Pallas kernels: 0 us -> 17.3 us
  between operations: 13.9 us -> 0.78 us
    psum x1 -> x0, waiting for transfers between devices: 141 us -> none  [broadcast(): return lax.psum(block, axis)]
    all_gather x2 -> x0, waiting for transfers between devices: 95.8 us -> none  [the longest x1 51.5 us: body(): all_rows = lax.all_gather(final_rows, 'tensor', axis=0, tiled=True)]
    reduce_scatter x1 -> x0, waiting for transfers between devices: 91 us -> none  [body(): lax.psum_scatter(jnp.dot(context, output_weight, preferred_element_type=j...]
    pmax x1 -> x0, blocking collectives: 67.4 us -> none  [body(): row_top = lax.pmax(local_top, ('section', 'tensor'))]
    psum x1 -> x0, blocking collectives: 62.6 us -> none  [body(): lax.psum((local_total * jnp.exp(local_top - row_top), local_pick), ('sect...]
    ppermute x1 -> x34, waiting for transfers between devices: 8.88 us -> 65.2 us  [the longest x27 42.8 us: over_tensor(): return lax.ppermute(block, 'tensor', pairs)]
    ppermute x1 -> x34, starting transfers between devices: 4.87 us -> 39.5 us  [the longest x27 31.6 us: over_tensor(): return lax.ppermute(block, 'tensor', pairs)]
    dot_general x6 -> x0, matrix products: 21.7 us -> none  [the longest x1 5.76 us: body(): jnp.dot(context, output_weight, preferred_element_type=jnp.float32)]
  transfers between devices with their start and end apart: 5 -> 34, of which waited for: 5 -> 15; matrix products, arithmetic and copies ran while one was open for 2% -> 11% of each run, Pallas kernels for 0% -> 0%
where the time goes in v2:
time: 168 us; the launch traced here: 167 us
  waiting for transfers between devices  65.2 us (39%)
  starting transfers between devices  39.5 us (24%)
  blocking collectives  20.5 us (12%)
  Pallas kernels  17.3 us (10%)
  other arithmetic  12.6 us (8%)
  local copies, waits for them, and re-layouts  10.5 us (6%)
    ppermute x27, waiting for transfers between devices, over_tensor(): return lax.ppermute(block, 'tensor', pairs)  42.8 us
    ppermute x27, starting transfers between devices, over_tensor(): return lax.ppermute(block, 'tensor', pairs)  31.6 us
    ppermute x7, waiting for transfers between devices, over_section(): return lax.ppermute(block, 'section', pairs)  22.4 us
    all_to_all x1, blocking collectives, body(): got = lax.all_to_all(sent, ('section', 'tensor'), 0, 0, tiled=True)  20.5 us
    pallas_call x1, Pallas kernels, layer(): pl.pallas_call(layer_kernel, out_shape=[jax.ShapeDtypeStruct((n, WIDTH),...  12.7 us
    ppermute x7, starting transfers between devices, over_section(): return lax.ppermute(block, 'section', pairs)  7.86 us
    pallas_call x1, Pallas kernels, vocab(): pl.pallas_call(vocab_kernel, out_shape=jax.ShapeDtypeStruct((2 * MB, 128)...  4.61 us
  transfers between devices with their start and end apart: 34, of which 15 were waited for; matrix products, arithmetic and copies ran while one was open for 11% of the time, Pallas kernels for 0%

profile of v2, /device:TPU:1, one launch (start us, length us, event | category | flops | bytes accessed | tf_op | source)
XLA Modules:
  0.0 166.9 jit_solution(603598055134502789)
XLA Ops:
  0.6 1.3 collective-permute-start.50
  5.4 28.2 %conditional.6 = (bf16[32,8192]{1,0:T(8,128)(2,1)}, bf16[16,8192]{1,0:T(8,128)(2,1)}, bf16[16,8192]{1,0:T(8,128)(2,1)}, bf16[32,8192]{1,0:T(8,128)(2,1)}, bf16[3...) conditional(s32[]{:T(128)} %convert_element_type.171, ...), branch_computations={%region_1.3_spmd, %region_2.4_spmd} | conditional | flops 199518 | bytes 16459224
  5.4 2.5 %collective-permute-start.41 = (bf16[32,8192]{1,0:T(8,128)(2,1)S(1)}, bf16[32,8192]{1,0:T(8,128)(2,1)}, u32[]{:S(2)}, u32[]{:S(2)}) collective-permute-start(bf16[32,8192]{1,0:T(8,128)(2,1)S(1)} %get-tuple-element.543), channel_id=1, source_target_pairs={{0,1},{1,2},{2,3},{3,0},{4,5},{5,6},{6,7},{7,4},{8,9},{9,10},{10,1... | collective-permute-start | bytes 1572872 | tf_op jit(solution)/shard_map/cond/branch_1_fun/ppermute | solution.py:43
  7.9 2.2 %collective-permute-start.40 = (bf16[32,8192]{1,0:T(8,128)(2,1)S(1)}, bf16[32,8192]{1,0:T(8,128)(2,1)}, u32[]{:S(2)}, u32[]{:S(2)}) collective-permute-start(bf16[32,8192]{1,0:T(8,128)(2,1)S(1)} %get-tuple-element.543), channel_id=1, source_target_pairs={{0,3},{1,0},{2,1},{3,2},{4,7},{5,4},{6,5},{7,6},{8,11},{9,8},{10,9... | collective-permute-start | bytes 1572872 | tf_op jit(solution)/shard_map/cond/branch_1_fun/ppermute | solution.py:43
  12.1 1.3 reduce.9
  18.8 2.7 %collective-permute-start.43 = (bf16[16,8192]{1,0:T(8,128)(2,1)S(1)}, bf16[16,8192]{1,0:T(8,128)(2,1)}, u32[]{:S(2)}, u32[]{:S(2)}) collective-permute-start(bf16[16,8192]{1,0:T(8,128)(2,1)S(1)} %slice.86), channel_id=1, source_target_pairs={{0,3},{1,0},{2,1},{3,2},{4,7},{5,4},{6,5},{7,6},{8,11},{9,8},{10,9... | collective-permute-start | bytes 786440 | tf_op jit(solution)/shard_map/cond/branch_1_fun/ppermute | solution.py:43
  26.3 3.5 %collective-permute-done.46 = bf16[16,8192]{1,0:T(8,128)(2,1)} collective-permute-done((bf16[16,8192]{1,0:T(8,128)(2,1)}, bf16[16,8192]{1,0:T(8,128)(2,1)}, u32[]{:S(2)}, u32[]{:S(2)}) %collective-permute-start.46) | collective-permute-done | bytes 262176 | tf_op jit(solution)/shard_map/cond/branch_1_fun/ppermute | solution.py:43
  29.9 2.8 %collective-permute-done.47 = bf16[16,8192]{1,0:T(8,128)(2,1)} collective-permute-done((bf16[16,8192]{1,0:T(8,128)(2,1)}, bf16[16,8192]{1,0:T(8,128)(2,1)}, u32[]{:S(2)}, u32[]{:S(2)}) %collective-permute-start.47) | collective-permute-done | bytes 262176 | tf_op jit(solution)/shard_map/cond/branch_1_fun/ppermute | solution.py:43
  35.7 104.3 %conditional.5 = (bf16[32,8192]{1,0:T(8,128)(2,1)}, f32[8,96]{1,0:T(8,128)S(1)}) conditional(s32[]{:T(128)} %convert_element_type.171, (bf16[32,8192]{1,0:T(8,128)(2,1)S(1)}, bf16[16,128]{1,0:T(8,128)(2,1)S(1)}, bf16[32,8192]{1,0:T(8,128)(2,1)S(1)}, bf16[8192,512]{1,0:T(8,128)(2,1)}, bf16[8192,256]{1,0:T(8,128)(2,1)}, ...), branch_computations={%region_3.5_spmd, %region_4.8_spmd} | conditional | flops 8012332032 | bytes 99876688 | solution.py:324
  35.9 12.7 %layer.3 = (bf16[32,8192]{1,0:T(8,128)(2,1)S(1)}, bf16[32,8192]{1,0:T(8,128)(2,1)S(1)}, bf16[16,8192]{1,0:T(8,128)(2,1)S(1)}, bf16[16,8192]{1,0:T(8,128)(2,1)S(1...) custom-call(bf16[32,8192]{1,0:T(8,128)(2,1)S(1)} %get-tuple-element., ...), custom_call_target="tpu_custom_call" | custom-call | flops 6000000000 | bytes 29360128 | tf_op jit(solution)/shard_map/cond/branch_1_fun/layer/pallas_call | solution.py:171
  50.2 2.7 %collective-permute-start.19 = (bf16[32,8192]{1,0:T(8,128)(2,1)S(1)}, bf16[32,8192]{1,0:T(8,128)(2,1)S(1)}, u32[]{:S(2)}, u32[]{:S(2)}) collective-permute-start(bf16[32,8192]{1,0:T(8,128)(2,1)S(1)} %get-tuple-element.244), channel_id=1, source_target_pairs={{0,3},{1,0},{2,1},{3,2},{4,7},{5,4},{6,5},{7,6},{8,11},{9,8},{10,9... | collective-permute-start | bytes 1572872 | tf_op jit(solution)/shard_map/cond/branch_1_fun/ppermute | solution.py:43
  52.9 1.3 collective-permute-done.21
  55.4 1.6 collective-permute-done.24
  57.2 11.5 %collective-permute-done.22 = bf16[16,8192]{1,0:T(8,128)(2,1)S(1)} collective-permute-done((bf16[16,8192]{1,0:T(8,128)(2,1)S(1)}, bf16[16,8192]{1,0:T(8,128)(2,1)S(1)}, u32[]{:S(2)}, u32[]{:S(2)}) %collective-permute-start.22) | collective-permute-done | bytes 262176 | tf_op jit(solution)/shard_map/cond/branch_1_fun/ppermute | solution.py:43
  68.8 3.2 %collective-permute-start.23 = (bf16[32,8192]{1,0:T(8,128)(2,1)S(1)}, bf16[32,8192]{1,0:T(8,128)(2,1)S(1)}, u32[]{:S(2)}, u32[]{:S(2)}) collective-permute-start(bf16[32,8192]{1,0:T(8,128)(2,1)S(1)} %pad_maximum_fusion.2), channel_id=1, source_target_pairs={{0,3},{1,0},{2,1},{3,2},{4,7},{5,4},{6,5},{7,6},{8,11},{9,8},{10,9... | collective-permute-start | bytes 1572872 | tf_op jit(solution)/shard_map/cond/branch_1_fun/ppermute | solution.py:43
  72.4 1.3 collective-permute-start.20
  73.7 4.4 %collective-permute-done.23 = bf16[32,8192]{1,0:T(8,128)(2,1)S(1)} collective-permute-done((bf16[32,8192]{1,0:T(8,128)(2,1)S(1)}, bf16[32,8192]{1,0:T(8,128)(2,1)S(1)}, u32[]{:S(2)}, u32[]{:S(2)}) %collective-permute-start.23) | collective-permute-done | bytes 524320 | tf_op jit(solution)/shard_map/cond/branch_1_fun/ppermute | solution.py:43
  78.1 3.3 %collective-permute-done.26 = bf16[32,8192]{1,0:T(8,128)(2,1)S(1)} collective-permute-done((bf16[32,8192]{1,0:T(8,128)(2,1)S(1)}, bf16[32,8192]{1,0:T(8,128)(2,1)S(1)}, u32[]{:S(2)}, u32[]{:S(2)}) %collective-permute-start.26) | collective-permute-done | bytes 524320 | tf_op jit(solution)/shard_map/cond/branch_1_fun/ppermute | solution.py:43
  81.4 1.3 fusion
  84.7 1.3 broadcast_select_fusion.1
  86.0 1.3 collective-permute-start.28
  88.7 21.7 %collective-permute-done.28 = bf16[32,8192]{1,0:T(8,128)(2,1)S(1)} collective-permute-done((bf16[32,8192]{1,0:T(8,128)(2,1)S(1)}, bf16[32,8192]{1,0:T(8,128)(2,1)S(1)}, u32[]{:S(2)}, u32[]{:S(2)}) %collective-permute-start.28) | collective-permute-done | bytes 524320 | tf_op jit(solution)/shard_map/cond/branch_1_fun/ppermute | solution.py:47
  110.6 2.7 %collective-permute-start.31 = (bf16[32,8192]{1,0:T(8,128)(2,1)S(1)}, bf16[32,8192]{1,0:T(8,128)(2,1)S(1)}, u32[]{:S(2)}, u32[]{:S(2)}) collective-permute-start(bf16[32,8192]{1,0:T(8,128)(2,1)S(1)} %select_select_fusion.refs_0_), channel_id=1, source_target_pairs={{0,3},{1,0},{2,1},{3,2},{4,7},{5,4},{6,5},{7,6},{8,11},{9,8},{10,9... | collective-permute-start | bytes 1572872 | tf_op jit(solution)/shard_map/cond/branch_1_fun/ppermute | solution.py:43
  114.4 5.4 %collective-permute-done.32.refs_4_ = bf16[32,8192]{1,0:T(8,128)(2,1)S(1)} collective-permute-done((bf16[32,8192]{1,0:T(8,128)(2,1)S(1)}, bf16[32,8192]{1,0:T(8,128)(2,1)S(1)}, u32[]{:S(2)}, u32[]{:S(2)}) %collective-permute-start.32) | collective-permute-done | bytes 524320 | tf_op jit(solution)/shard_map/cond/branch_1_fun/ppermute | solution.py:43
  121.3 2.7 %collective-permute-start.34 = (bf16[16,8192]{1,0:T(8,128)(2,1)}, bf16[16,8192]{1,0:T(8,128)(2,1)}, u32[]{:S(2)}, u32[]{:S(2)}) collective-permute-start(bf16[16,8192]{1,0:T(8,128)(2,1)} %slice.83), channel_id=1, source_target_pairs={{0,3},{1,0},{2,1},{3,2},{4,7},{5,4},{6,5},{7,6},{8,11},{9,8},{10,9... | collective-permute-start | bytes 786440 | tf_op jit(solution)/shard_map/cond/branch_1_fun/ppermute | solution.py:43
  124.0 1.4 collective-permute-start.39
  125.5 1.7 collective-permute-done.33.refs_2_
  128.9 3.5 %collective-permute-done.37.refs_7_ = bf16[16,8192]{1,0:T(8,128)(2,1)S(1)} collective-permute-done((bf16[16,8192]{1,0:T(8,128)(2,1)S(1)}, bf16[16,8192]{1,0:T(8,128)(2,1)S(1)}, u32[]{:S(2)}, u32[]{:S(2)}) %collective-permute-start.37) | collective-permute-done | bytes 262176 | tf_op jit(solution)/shard_map/cond/branch_1_fun/ppermute | solution.py:43
  132.4 2.8 %collective-permute-done.38.refs_8_ = bf16[16,8192]{1,0:T(8,128)(2,1)S(1)} collective-permute-done((bf16[16,8192]{1,0:T(8,128)(2,1)}, bf16[16,8192]{1,0:T(8,128)(2,1)S(1)}, u32[]{:S(2)}, u32[]{:S(2)}) %collective-permute-start.38) | collective-permute-done | bytes 262176 | tf_op jit(solution)/shard_map/cond/branch_1_fun/ppermute | solution.py:43
  135.3 4.6 %vocab.1 = f32[256,128]{1,0:T(8,128)S(1)} custom-call(bf16[32,8192]{1,0:T(8,128)(2,1)S(1)} %select_select_fusion.refs_0_, bf16[32,8192]{1,0:T(8,128)(2,1)S(1)} %collective-permute-done.31.refs_1_, bf16[16,8192]{1,0:T(8,128)(2,1)S(1)} %collective-permute-done.33.refs_2_, bf16[16,8192]{1,0:T(8,128)(2,1)} %collective-permute-done.34.refs_3_, ...), custom_call_target="tpu_custom_call" | custom-call | flops 2000000000 | bytes 14680064 | tf_op jit(solution)/shard_map/cond/branch_1_fun/vocab/pallas_call | solution.py:231
  140.0 1.9 %collective-permute-start.51 = (bf16[32,8192]{1,0:T(8,128)(2,1)}, bf16[32,8192]{1,0:T(8,128)(2,1)S(1)}, u32[]{:S(2)}, u32[]{:S(2)}) collective-permute-start(bf16[32,8192]{1,0:T(8,128)(2,1)} %get-tuple-element.294), channel_id=1, source_target_pairs={{0,8},{8,16},{16,24},{24,32},{32,40},{40,48},{48,56},{56,64},{64,7... | collective-permute-start | bytes 1572872 | tf_op jit(solution)/shard_map/ppermute | solution.py:47
  142.6 20.5 %all_to_all.9 = f32[128,1,96]{2,1,0:T(1,128)S(1)} all-to-all(f32[128,1,96]{2,1,0:T(1,128)S(1)} %bitcast.50), channel_id=1, replica_groups=mesh['section'=16,'tensor'=8] {'section','tensor'}, dimensions={0} | all-to-all | bytes 98304 | tf_op jit(solution)/shard_map/all_to_all | solution.py:330
  (124 shorter events, 34.5 us)
Async XLA Ops:
  0.6 35.1 %collective-permute-start.50 = (bf16[8192,256]{1,0:T(8,128)(2,1)}, bf16[8192,256]{1,0:T(8,128)(2,1)}, u32[]{:S(2)}, u32[]{:S(2)}) collective-permute-start(bf16[8192,256]{1,0:T(8,128)(2,1)} %param.22), channel_id=1, source_target_pairs={{0,8},{16,24},{32,40},{48,56},{64,72},{80,88},{96,104},{112,120},{... | collective-permute-start | bytes 12582920 | tf_op jit(solution)/shard_map/ppermute | solution.py:47
  5.4 11.3 %collective-permute-start.41 = (bf16[32,8192]{1,0:T(8,128)(2,1)S(1)}, bf16[32,8192]{1,0:T(8,128)(2,1)}, u32[]{:S(2)}, u32[]{:S(2)}) collective-permute-start(bf16[32,8192]{1,0:T(8,128)(2,1)S(1)} %get-tuple-element.543), channel_id=1, source_target_pairs={{0,1},{1,2},{2,3},{3,0},{4,5},{5,6},{6,7},{7,4},{8,9},{9,10},{10,1... | collective-permute-start | bytes 1572872 | tf_op jit(solution)/shard_map/cond/branch_1_fun/ppermute | solution.py:43
  7.9 9.9 %collective-permute-start.40 = (bf16[32,8192]{1,0:T(8,128)(2,1)S(1)}, bf16[32,8192]{1,0:T(8,128)(2,1)}, u32[]{:S(2)}, u32[]{:S(2)}) collective-permute-start(bf16[32,8192]{1,0:T(8,128)(2,1)S(1)} %get-tuple-element.543), channel_id=1, source_target_pairs={{0,3},{1,0},{2,1},{3,2},{4,7},{5,4},{6,5},{7,6},{8,11},{9,8},{10,9... | collective-permute-start | bytes 1572872 | tf_op jit(solution)/shard_map/cond/branch_1_fun/ppermute | solution.py:43
  10.1 11.5 %collective-permute-start.44 = (bf16[32,8192]{1,0:T(8,128)(2,1)S(1)}, bf16[32,8192]{1,0:T(8,128)(2,1)}, u32[]{:S(2)}, u32[]{:S(2)}) collective-permute-start(bf16[32,8192]{1,0:T(8,128)(2,1)S(1)} %get-tuple-element.543), channel_id=1, source_target_pairs={{0,4},{1,5},{2,6},{3,7},{4,0},{5,1},{6,2},{7,3},{8,12},{9,13},{10,... | collective-permute-start | bytes 1572872 | tf_op jit(solution)/shard_map/cond/branch_1_fun/ppermute | solution.py:43
  17.7 6.6 %collective-permute-start.42 = (bf16[16,8192]{1,0:T(8,128)(2,1)S(1)}, bf16[16,8192]{1,0:T(8,128)(2,1)}, u32[]{:S(2)}, u32[]{:S(2)}) collective-permute-start(bf16[16,8192]{1,0:T(8,128)(2,1)S(1)} %slice.85), channel_id=1, source_target_pairs={{0,1},{1,2},{2,3},{3,0},{4,5},{5,6},{6,7},{7,4},{8,9},{9,10},{10,1... | collective-permute-start | bytes 786440 | tf_op jit(solution)/shard_map/cond/branch_1_fun/ppermute | solution.py:43
  18.8 6.8 %collective-permute-start.43 = (bf16[16,8192]{1,0:T(8,128)(2,1)S(1)}, bf16[16,8192]{1,0:T(8,128)(2,1)}, u32[]{:S(2)}, u32[]{:S(2)}) collective-permute-start(bf16[16,8192]{1,0:T(8,128)(2,1)S(1)} %slice.86), channel_id=1, source_target_pairs={{0,3},{1,0},{2,1},{3,2},{4,7},{5,4},{6,5},{7,6},{8,11},{9,8},{10,9... | collective-permute-start | bytes 786440 | tf_op jit(solution)/shard_map/cond/branch_1_fun/ppermute | solution.py:43
  21.7 11.0 %collective-permute-start.45 = (bf16[32,8192]{1,0:T(8,128)(2,1)}, bf16[32,8192]{1,0:T(8,128)(2,1)}, u32[]{:S(2)}, u32[]{:S(2)}) collective-permute-start(bf16[32,8192]{1,0:T(8,128)(2,1)} %collective-permute-done.44), channel_id=1, source_target_pairs={{0,3},{1,0},{2,1},{3,2},{4,7},{5,4},{6,5},{7,6},{8,11},{9,8},{10,9... | collective-permute-start | bytes 1572872 | tf_op jit(solution)/shard_map/cond/branch_1_fun/ppermute | solution.py:43
  21.9 10.8 %collective-permute-start.48 = (bf16[32,8192]{1,0:T(8,128)(2,1)}, bf16[32,8192]{1,0:T(8,128)(2,1)}, u32[]{:S(2)}, u32[]{:S(2)}) collective-permute-start(bf16[32,8192]{1,0:T(8,128)(2,1)} %collective-permute-done.44), channel_id=1, source_target_pairs={{0,1},{1,2},{2,3},{3,0},{4,5},{5,6},{6,7},{7,4},{8,9},{9,10},{10,1... | collective-permute-start | bytes 1572872 | tf_op jit(solution)/shard_map/cond/branch_1_fun/ppermute | solution.py:43
  24.3 5.5 %collective-permute-start.46 = (bf16[16,8192]{1,0:T(8,128)(2,1)}, bf16[16,8192]{1,0:T(8,128)(2,1)}, u32[]{:S(2)}, u32[]{:S(2)}) collective-permute-start(bf16[16,8192]{1,0:T(8,128)(2,1)} %collective-permute-done.42), channel_id=1, source_target_pairs={{0,4},{1,5},{2,6},{3,7},{4,0},{5,1},{6,2},{7,3},{8,12},{9,13},{10,... | collective-permute-start | bytes 786440 | tf_op jit(solution)/shard_map/cond/branch_1_fun/ppermute | solution.py:43
  25.5 7.1 %collective-permute-start.47 = (bf16[16,8192]{1,0:T(8,128)(2,1)}, bf16[16,8192]{1,0:T(8,128)(2,1)}, u32[]{:S(2)}, u32[]{:S(2)}) collective-permute-start(bf16[16,8192]{1,0:T(8,128)(2,1)} %collective-permute-done.43), channel_id=1, source_target_pairs={{0,4},{1,5},{2,6},{3,7},{4,0},{5,1},{6,2},{7,3},{8,12},{9,13},{10,... | collective-permute-start | bytes 786440 | tf_op jit(solution)/shard_map/cond/branch_1_fun/ppermute | solution.py:43
  48.6 5.6 %collective-permute-start.21 = (bf16[16,8192]{1,0:T(8,128)(2,1)S(1)}, bf16[16,8192]{1,0:T(8,128)(2,1)S(1)}, u32[]{:S(2)}, u32[]{:S(2)}) collective-permute-start(bf16[16,8192]{1,0:T(8,128)(2,1)S(1)} %get-tuple-element.247), channel_id=1, source_target_pairs={{0,4},{1,5},{2,6},{3,7},{4,0},{5,1},{6,2},{7,3},{8,12},{9,13},{10,... | collective-permute-start | bytes 786440 | tf_op jit(solution)/shard_map/cond/branch_1_fun/ppermute | solution.py:43
  49.9 7.1 %collective-permute-start.24 = (bf16[16,8192]{1,0:T(8,128)(2,1)S(1)}, bf16[16,8192]{1,0:T(8,128)(2,1)S(1)}, u32[]{:S(2)}, u32[]{:S(2)}) collective-permute-start(bf16[16,8192]{1,0:T(8,128)(2,1)S(1)} %get-tuple-element.250), channel_id=1, source_target_pairs={{0,4},{1,5},{2,6},{3,7},{4,0},{5,1},{6,2},{7,3},{8,12},{9,13},{10,... | collective-permute-start | bytes 786440 | tf_op jit(solution)/shard_map/cond/branch_1_fun/ppermute | solution.py:43
  50.2 22.0 %collective-permute-start.18 = (bf16[32,8192]{1,0:T(8,128)(2,1)S(1)}, bf16[32,8192]{1,0:T(8,128)(2,1)S(1)}, u32[]{:S(2)}, u32[]{:S(2)}) collective-permute-start(bf16[32,8192]{1,0:T(8,128)(2,1)S(1)} %get-tuple-element.243), channel_id=1, source_target_pairs={{0,1},{1,2},{2,3},{3,0},{4,5},{5,6},{6,7},{7,4},{8,9},{9,10},{10,1... | collective-permute-start | bytes 1572872 | tf_op jit(solution)/shard_map/cond/branch_1_fun/ppermute | solution.py:43
  50.2 22.0 %collective-permute-start.19 = (bf16[32,8192]{1,0:T(8,128)(2,1)S(1)}, bf16[32,8192]{1,0:T(8,128)(2,1)S(1)}, u32[]{:S(2)}, u32[]{:S(2)}) collective-permute-start(bf16[32,8192]{1,0:T(8,128)(2,1)S(1)} %get-tuple-element.244), channel_id=1, source_target_pairs={{0,3},{1,0},{2,1},{3,2},{4,7},{5,4},{6,5},{7,6},{8,11},{9,8},{10,9... | collective-permute-start | bytes 1572872 | tf_op jit(solution)/shard_map/cond/branch_1_fun/ppermute | solution.py:43
  54.3 14.4 %collective-permute-start.22 = (bf16[16,8192]{1,0:T(8,128)(2,1)S(1)}, bf16[16,8192]{1,0:T(8,128)(2,1)S(1)}, u32[]{:S(2)}, u32[]{:S(2)}) collective-permute-start(bf16[16,8192]{1,0:T(8,128)(2,1)S(1)} %add_convert_fusion.11), channel_id=1, source_target_pairs={{0,3},{1,0},{2,1},{3,2},{4,7},{5,4},{6,5},{7,6},{8,11},{9,8},{10,9... | collective-permute-start | bytes 786440 | tf_op jit(solution)/shard_map/cond/branch_1_fun/ppermute | solution.py:43
  57.1 14.9 %collective-permute-start.25 = (bf16[16,8192]{1,0:T(8,128)(2,1)S(1)}, bf16[16,8192]{1,0:T(8,128)(2,1)S(1)}, u32[]{:S(2)}, u32[]{:S(2)}) collective-permute-start(bf16[16,8192]{1,0:T(8,128)(2,1)S(1)} %add_convert_fusion.9), channel_id=1, source_target_pairs={{0,1},{1,2},{2,3},{3,0},{4,5},{5,6},{6,7},{7,4},{8,9},{9,10},{10,1... | collective-permute-start | bytes 786440 | tf_op jit(solution)/shard_map/cond/branch_1_fun/ppermute | solution.py:43
  68.8 9.3 %collective-permute-start.23 = (bf16[32,8192]{1,0:T(8,128)(2,1)S(1)}, bf16[32,8192]{1,0:T(8,128)(2,1)S(1)}, u32[]{:S(2)}, u32[]{:S(2)}) collective-permute-start(bf16[32,8192]{1,0:T(8,128)(2,1)S(1)} %pad_maximum_fusion.2), channel_id=1, source_target_pairs={{0,3},{1,0},{2,1},{3,2},{4,7},{5,4},{6,5},{7,6},{8,11},{9,8},{10,9... | collective-permute-start | bytes 1572872 | tf_op jit(solution)/shard_map/cond/branch_1_fun/ppermute | solution.py:43
  72.1 9.3 %collective-permute-start.26 = (bf16[32,8192]{1,0:T(8,128)(2,1)S(1)}, bf16[32,8192]{1,0:T(8,128)(2,1)S(1)}, u32[]{:S(2)}, u32[]{:S(2)}) collective-permute-start(bf16[32,8192]{1,0:T(8,128)(2,1)S(1)} %pad_maximum_fusion.3), channel_id=1, source_target_pairs={{0,1},{1,2},{2,3},{3,0},{4,5},{5,6},{6,7},{7,4},{8,9},{9,10},{10,1... | collective-permute-start | bytes 1572872 | tf_op jit(solution)/shard_map/cond/branch_1_fun/ppermute | solution.py:43
  72.4 9.0 %collective-permute-start.20 = (bf16[32,8192]{1,0:T(8,128)(2,1)S(1)}, bf16[32,8192]{1,0:T(8,128)(2,1)S(1)}, u32[]{:S(2)}, u32[]{:S(2)}) collective-permute-start(bf16[32,8192]{1,0:T(8,128)(2,1)S(1)} %add_convert_fusion.7), channel_id=1, source_target_pairs={{0,4},{1,5},{2,6},{3,7},{4,0},{5,1},{6,2},{7,3},{8,12},{9,13},{10,... | collective-permute-start | bytes 1572872 | tf_op jit(solution)/shard_map/cond/branch_1_fun/ppermute | solution.py:43
  86.0 24.4 %collective-permute-start.28 = (bf16[32,8192]{1,0:T(8,128)(2,1)S(1)}, bf16[32,8192]{1,0:T(8,128)(2,1)S(1)}, u32[]{:S(2)}, u32[]{:S(2)}) collective-permute-start(bf16[32,8192]{1,0:T(8,128)(2,1)S(1)} %broadcast_select_fusion.1), channel_id=1, source_target_pairs={{104,8},{120,24},{105,9},{121,25},{106,10},{122,26},{107,11},{123,... | collective-permute-start | bytes 1572872 | tf_op jit(solution)/shard_map/cond/branch_1_fun/ppermute | solution.py:47
  87.3 23.1 %collective-permute-start.29 = (bf16[32,8192]{1,0:T(8,128)(2,1)S(1)}, bf16[32,8192]{1,0:T(8,128)(2,1)S(1)}, u32[]{:S(2)}, u32[]{:S(2)}) collective-permute-start(bf16[32,8192]{1,0:T(8,128)(2,1)S(1)} %broadcast_select_fusion.1), channel_id=1, source_target_pairs={{104,72},{120,88},{105,73},{121,89},{106,74},{122,90},{107,75},{12... | collective-permute-start | bytes 1572872 | tf_op jit(solution)/shard_map/cond/branch_1_fun/ppermute | solution.py:47
  88.0 22.4 %collective-permute-start.30 = (bf16[32,8192]{1,0:T(8,128)(2,1)S(1)}, bf16[32,8192]{1,0:T(8,128)(2,1)S(1)}, u32[]{:S(2)}, u32[]{:S(2)}) collective-permute-start(bf16[32,8192]{1,0:T(8,128)(2,1)S(1)} %broadcast_select_fusion.1), channel_id=1, source_target_pairs={{104,40},{120,56},{105,41},{121,57},{106,42},{122,58},{107,43},{12... | collective-permute-start | bytes 1572872 | tf_op jit(solution)/shard_map/cond/branch_1_fun/ppermute | solution.py:47
  110.5 9.3 %collective-permute-start.32 = (bf16[32,8192]{1,0:T(8,128)(2,1)S(1)}, bf16[32,8192]{1,0:T(8,128)(2,1)S(1)}, u32[]{:S(2)}, u32[]{:S(2)}) collective-permute-start(bf16[32,8192]{1,0:T(8,128)(2,1)S(1)} %select_select_fusion.refs_0_), channel_id=1, source_target_pairs={{0,1},{1,2},{2,3},{3,0},{4,5},{5,6},{6,7},{7,4},{8,9},{9,10},{10,1... | collective-permute-start | bytes 1572872 | tf_op jit(solution)/shard_map/cond/branch_1_fun/ppermute | solution.py:43
  110.6 10.0 %collective-permute-start.31 = (bf16[32,8192]{1,0:T(8,128)(2,1)S(1)}, bf16[32,8192]{1,0:T(8,128)(2,1)S(1)}, u32[]{:S(2)}, u32[]{:S(2)}) collective-permute-start(bf16[32,8192]{1,0:T(8,128)(2,1)S(1)} %select_select_fusion.refs_0_), channel_id=1, source_target_pairs={{0,3},{1,0},{2,1},{3,2},{4,7},{5,4},{6,5},{7,6},{8,11},{9,8},{10,9... | collective-permute-start | bytes 1572872 | tf_op jit(solution)/shard_map/cond/branch_1_fun/ppermute | solution.py:43
  113.2 10.7 %collective-permute-start.35 = (bf16[32,8192]{1,0:T(8,128)(2,1)S(1)}, bf16[32,8192]{1,0:T(8,128)(2,1)S(1)}, u32[]{:S(2)}, u32[]{:S(2)}) collective-permute-start(bf16[32,8192]{1,0:T(8,128)(2,1)S(1)} %select_select_fusion.refs_0_), channel_id=1, source_target_pairs={{0,4},{1,5},{2,6},{3,7},{4,0},{5,1},{6,2},{7,3},{8,12},{9,13},{10,... | collective-permute-start | bytes 1572872 | tf_op jit(solution)/shard_map/cond/branch_1_fun/ppermute | solution.py:43
  120.5 6.6 %collective-permute-start.33 = (bf16[16,8192]{1,0:T(8,128)(2,1)}, bf16[16,8192]{1,0:T(8,128)(2,1)S(1)}, u32[]{:S(2)}, u32[]{:S(2)}) collective-permute-start(bf16[16,8192]{1,0:T(8,128)(2,1)} %slice.82), channel_id=1, source_target_pairs={{0,1},{1,2},{2,3},{3,0},{4,5},{5,6},{6,7},{7,4},{8,9},{9,10},{10,1... | collective-permute-start | bytes 786440 | tf_op jit(solution)/shard_map/cond/branch_1_fun/ppermute | solution.py:43
  121.3 7.1 %collective-permute-start.34 = (bf16[16,8192]{1,0:T(8,128)(2,1)}, bf16[16,8192]{1,0:T(8,128)(2,1)}, u32[]{:S(2)}, u32[]{:S(2)}) collective-permute-start(bf16[16,8192]{1,0:T(8,128)(2,1)} %slice.83), channel_id=1, source_target_pairs={{0,3},{1,0},{2,1},{3,2},{4,7},{5,4},{6,5},{7,6},{8,11},{9,8},{10,9... | collective-permute-start | bytes 786440 | tf_op jit(solution)/shard_map/cond/branch_1_fun/ppermute | solution.py:43
  124.0 11.2 %collective-permute-start.36 = (bf16[32,8192]{1,0:T(8,128)(2,1)S(1)}, bf16[32,8192]{1,0:T(8,128)(2,1)S(1)}, u32[]{:S(2)}, u32[]{:S(2)}) collective-permute-start(bf16[32,8192]{1,0:T(8,128)(2,1)S(1)} %collective-permute-done.35.refs_5_), channel_id=1, source_target_pairs={{0,3},{1,0},{2,1},{3,2},{4,7},{5,4},{6,5},{7,6},{8,11},{9,8},{10,9... | collective-permute-start | bytes 1572872 | tf_op jit(solution)/shard_map/cond/branch_1_fun/ppermute | solution.py:43
  124.0 11.2 %collective-permute-start.39 = (bf16[32,8192]{1,0:T(8,128)(2,1)S(1)}, bf16[32,8192]{1,0:T(8,128)(2,1)S(1)}, u32[]{:S(2)}, u32[]{:S(2)}) collective-permute-start(bf16[32,8192]{1,0:T(8,128)(2,1)S(1)} %collective-permute-done.35.refs_5_), channel_id=1, source_target_pairs={{0,1},{1,2},{2,3},{3,0},{4,5},{5,6},{6,7},{7,4},{8,9},{9,10},{10,1... | collective-permute-start | bytes 1572872 | tf_op jit(solution)/shard_map/cond/branch_1_fun/ppermute | solution.py:43
  127.2 5.2 %collective-permute-start.37 = (bf16[16,8192]{1,0:T(8,128)(2,1)S(1)}, bf16[16,8192]{1,0:T(8,128)(2,1)S(1)}, u32[]{:S(2)}, u32[]{:S(2)}) collective-permute-start(bf16[16,8192]{1,0:T(8,128)(2,1)S(1)} %collective-permute-done.33.refs_2_), channel_id=1, source_target_pairs={{0,4},{1,5},{2,6},{3,7},{4,0},{5,1},{6,2},{7,3},{8,12},{9,13},{10,... | collective-permute-start | bytes 786440 | tf_op jit(solution)/shard_map/cond/branch_1_fun/ppermute | solution.py:43
  128.4 6.8 %collective-permute-start.38 = (bf16[16,8192]{1,0:T(8,128)(2,1)}, bf16[16,8192]{1,0:T(8,128)(2,1)S(1)}, u32[]{:S(2)}, u32[]{:S(2)}) collective-permute-start(bf16[16,8192]{1,0:T(8,128)(2,1)} %collective-permute-done.34.refs_3_), channel_id=1, source_target_pairs={{0,4},{1,5},{2,6},{3,7},{4,0},{5,1},{6,2},{7,3},{8,12},{9,13},{10,... | collective-permute-start | bytes 786440 | tf_op jit(solution)/shard_map/cond/branch_1_fun/ppermute | solution.py:43
  140.0 26.1 %collective-permute-start.51 = (bf16[32,8192]{1,0:T(8,128)(2,1)}, bf16[32,8192]{1,0:T(8,128)(2,1)S(1)}, u32[]{:S(2)}, u32[]{:S(2)}) collective-permute-start(bf16[32,8192]{1,0:T(8,128)(2,1)} %get-tuple-element.294), channel_id=1, source_target_pairs={{0,8},{8,16},{16,24},{24,32},{32,40},{40,48},{48,56},{56,64},{64,7... | collective-permute-start | bytes 1572872 | tf_op jit(solution)/shard_map/ppermute | solution.py:47
  (6 other events, 123.5 us)

commit v3 on v2

v3 whole, which is shorter than its diff:
```python
import math

import jax
import jax.numpy as jnp
from jax import lax
from jax.experimental import pallas as pl
from jax.experimental.pallas import tpu as pltpu
from jax.sharding import PartitionSpec as P

NORM_EPSILON = 1e-05
ROPE_THETA = 500000.0
BF16 = jnp.bfloat16
F32 = jnp.float32
NZ = 4
ROWS = 32
HALF = 16
WIDTH = 8192
HEAD = 128
HEADS = 4
MB = 128
VL = 256


def tensor_pairs(step):
    out = []
    for x in range(2):
        for z in range(NZ):
            x2, z2 = step(x, z)
            out.append((x * NZ + z, (x2 % 2) * NZ + z2 % NZ))
    return out


TO_X = tensor_pairs(lambda x, z: (x + 1, z))
TO_UP = tensor_pairs(lambda x, z: (x, z + 1))
TO_DOWN = tensor_pairs(lambda x, z: (x, z - 1))


def sec(y, h, c):
    return ((y % 4) * 2 + h % 2) * 2 + c


def over_tensor(block, pairs):
    return lax.ppermute(block, "tensor", pairs)


def over_section(block, pairs):
    return lax.ppermute(block, "section", pairs)


def gather_first(own):
    from_x = over_tensor(own, TO_X)
    below = over_tensor(own, TO_UP)
    above = over_tensor(own, TO_DOWN)
    return above, over_tensor(below, TO_UP), below, from_x


def gather_rest(own, first):
    above, far, below, from_x = first
    x_far = over_tensor(far, TO_X)
    x_below = over_tensor(from_x, TO_UP)
    x_above = over_tensor(from_x, TO_DOWN)
    return own, above, far, below, from_x, x_above, x_far, x_below


def gather_rows(own):
    return gather_rest(own, gather_first(own))


def scatter_sum(parts):
    own, above, far, below, x_own, x_above, x_far, x_below = parts
    got_far = over_tensor(x_far, TO_X)
    got_x_down = over_tensor(x_above, TO_UP)
    got_x_up = over_tensor(x_below, TO_DOWN)
    far_a = add(far[:HALF], got_far[:HALF]).astype(BF16)
    far_b = add(far[HALF:], got_far[HALF:]).astype(BF16)
    got_a = over_tensor(far_a, TO_DOWN)
    got_b = over_tensor(far_b, TO_UP)
    x_own = add(x_own, got_x_down, got_x_up).astype(BF16)
    got_x = over_tensor(x_own, TO_X)
    below = jnp.concatenate([add(below[:HALF], got_a), below[HALF:].astype(F32)], axis=0).astype(BF16)
    above = jnp.concatenate([above[:HALF].astype(F32), add(above[HALF:], got_b)], axis=0).astype(BF16)
    got_down = over_tensor(below, TO_DOWN)
    got_up = over_tensor(above, TO_UP)
    return own, got_x, got_down, got_up


def norm_value(values, gain):
    factor = lax.rsqrt(jnp.mean(values * values, axis=-1, keepdims=True) + NORM_EPSILON)
    return (values * factor * gain.astype(F32)).astype(BF16)


def norm_kernel(rows_ref, gain_ref, out_ref):
    out_ref[...] = norm_value(rows_ref[...].astype(F32), gain_ref[...])


def rms_norm(rows, gain):
    return pl.pallas_call(
        norm_kernel, out_shape=jax.ShapeDtypeStruct(rows.shape, BF16), name="norm"
    )(rows, gain.reshape(1, -1))


def finish_kernel(rows_ref, a_ref, b_ref, c_ref, d_ref, gain_ref, out_ref, final_ref):
    out = add(rows_ref[...], a_ref[...], b_ref[...], c_ref[...], d_ref[...]).astype(BF16)
    out_ref[...] = out
    final_ref[...] = norm_value(out.astype(F32), gain_ref[...])


def finish(rows, terms, gain):
    return pl.pallas_call(
        finish_kernel,
        out_shape=[jax.ShapeDtypeStruct(rows.shape, BF16)] * 2,
        compiler_params=pltpu.CompilerParams(vmem_limit_bytes=24 * 1024 * 1024),
        name="finish",
    )(rows, *terms, gain.reshape(1, -1))


def merge_kernel(got_ref, out_ref):
    got = got_ref[...].reshape(8, 2, 8, 128)[:, 1].reshape(64, 128)
    tops, totals, picks = got[:, :ROWS], got[:, ROWS : 2 * ROWS], got[:, 2 * ROWS : 3 * ROWS]
    top = jnp.max(tops, axis=0, keepdims=True)
    total = jnp.sum(totals * jnp.exp(tops - top), axis=0, keepdims=True)
    out_ref[...] = (jnp.sum(picks, axis=0, keepdims=True) - top - jnp.log(total))[0]


def merge(got):
    return pl.pallas_call(
        merge_kernel, out_shape=jax.ShapeDtypeStruct((ROWS,), F32), name="merge"
    )(got)


KC = 2048
NC = 2048
QKV = (HEADS + 2) * HEAD


def at(k, size):
    return pl.ds(pl.multiple_of(k * size, size), size)


def layer_kernel(*refs):
    blocks = refs[:8]
    wq_ref, wkv_ref, wo_ref, cos_ref, sin_ref, allow_ref = refs[8:14]
    outs = refs[14:22]
    rows, w, wo, acc, ctx, res, row_sem, w_sem, wo_sem, out_sem = refs[22:]

    for i, b in enumerate(blocks):
        pltpu.make_async_copy(b, rows.at[pl.ds(i * ROWS, ROWS)], row_sem).start()

    @pl.loop(0, WIDTH // KC)
    def _(k):
        cols = at(k, KC)
        q_cols, kv_cols = pl.ds(0, HEADS * HEAD), pl.ds(HEADS * HEAD, 2 * HEAD)
        pltpu.make_async_copy(wq_ref.at[cols], w.at[cols, q_cols], w_sem.at[k]).start()
        pltpu.make_async_copy(wkv_ref.at[cols], w.at[cols, kv_cols], w_sem.at[k]).start()

    @pl.loop(0, WIDTH // NC)
    def _(n):
        cols = at(n, NC)
        pltpu.make_async_copy(wo_ref.at[:, cols], wo.at[:, cols], wo_sem.at[n]).start()

    acc[...] = jnp.zeros_like(acc)
    pltpu.make_async_copy(rows, rows, row_sem).wait()

    @pl.loop(0, WIDTH // KC)
    def _(k):
        cols = at(k, KC)
        pltpu.make_async_copy(w.at[cols], w.at[cols], w_sem.at[k]).wait()
        acc[...] += jnp.dot(rows[:, cols], w[cols, :], preferred_element_type=F32)

    cos, sin = cos_ref[...], sin_ref[...]

    def rotated(h):
        v = acc[:, h * HEAD : (h + 1) * HEAD]
        return (v * cos + pltpu.roll(v, HEAD // 2, 1) * sin).astype(BF16)

    keys = rotated(HEADS)
    values = acc[:, (HEADS + 1) * HEAD :].astype(BF16)
    heads = [rotated(h) for h in range(HEADS)]
    for b in range(2):
        mb = slice(b * MB, (b + 1) * MB)
        allow = jnp.concatenate([allow_ref[mb, :]] * HEADS, axis=0) > 0
        q = jnp.concatenate([head[mb] for head in heads], axis=0)
        s = lax.dot_general(q, keys[mb], (((1,), (1,)), ((), ())), preferred_element_type=F32)
        s = jnp.where(allow, s * (1.0 / math.sqrt(HEAD)), -jnp.inf)
        e = jnp.exp(s - jnp.max(s, axis=1, keepdims=True))
        p = (e / jnp.sum(e, axis=1, keepdims=True)).astype(BF16)
        c = jnp.dot(p, values[mb], preferred_element_type=F32).astype(BF16)
        for h in range(HEADS):
            ctx[mb, h * HEAD : (h + 1) * HEAD] = c[h * MB : (h + 1) * MB]

    @pl.loop(0, WIDTH // NC)
    def _(n):
        cols = at(n, NC)
        pltpu.make_async_copy(wo.at[:, cols], wo.at[:, cols], wo_sem.at[n]).wait()
        res[:, cols] = jnp.dot(ctx[...], wo[:, cols], preferred_element_type=F32).astype(BF16)
        for i, o in enumerate(outs):
            pltpu.make_async_copy(res.at[pl.ds(i * ROWS, ROWS), cols], o.at[:, cols], out_sem).start()

    pltpu.make_async_copy(res, res, out_sem).wait()


def layer(blocks, wq, wkv, wo, cos, sin, allow):
    hbm = pl.BlockSpec(memory_space=pl.ANY)
    vmem = pl.BlockSpec(memory_space=pltpu.VMEM)
    return pl.pallas_call(
        layer_kernel,
        out_shape=[jax.ShapeDtypeStruct((ROWS, WIDTH), BF16)] * 8,
        in_specs=[hbm] * 11 + [vmem] * 3,
        out_specs=[hbm] * 8,
        scratch_shapes=[
            pltpu.VMEM((2 * MB, WIDTH), BF16),
            pltpu.VMEM((WIDTH, QKV), BF16),
            pltpu.VMEM((HEADS * HEAD, WIDTH), BF16),
            pltpu.VMEM((2 * MB, QKV), F32),
            pltpu.VMEM((2 * MB, HEADS * HEAD), BF16),
            pltpu.VMEM((2 * MB, WIDTH), BF16),
            pltpu.SemaphoreType.DMA,
            pltpu.SemaphoreType.DMA((WIDTH // KC,)),
            pltpu.SemaphoreType.DMA((WIDTH // NC,)),
            pltpu.SemaphoreType.DMA,
        ],
        compiler_params=pltpu.CompilerParams(vmem_limit_bytes=48 * 1024 * 1024),
        cost_estimate=pl.CostEstimate(flops=6 * 10**9, bytes_accessed=28 * 2**20, transcendentals=0),
        name="layer",
    )(*blocks, wq, wkv, wo, cos, sin, allow)


VC = 2048


def vocab_kernel(order_ref, *refs):
    blocks = refs[:8]
    w0_ref, w1_ref, want_ref, out_ref, rows, w, acc, row_sem, w_sem = refs[8:]
    for i, b in enumerate(blocks):
        pltpu.make_async_copy(b, rows.at[pl.ds(i * ROWS, ROWS)], row_sem).start()

    @pl.loop(0, WIDTH // VC)
    def _(k):
        cols = at(k, VC)
        for i, r in enumerate((w0_ref, w1_ref)):
            pltpu.make_async_copy(r.at[cols], w.at[cols, pl.ds(i * VL, VL)], w_sem.at[k]).start()

    acc[...] = jnp.zeros_like(acc)
    pltpu.make_async_copy(rows, rows, row_sem).wait()

    @pl.loop(0, WIDTH // VC, unroll=True)
    def _(k):
        cols = at(k, VC)
        pltpu.make_async_copy(w.at[cols], w.at[cols], w_sem.at[k]).wait()
        acc[...] += jnp.dot(rows[:, cols], w[cols, :], preferred_element_type=F32)

    logits = acc[...]
    top = jnp.max(logits, axis=1, keepdims=True)
    total = jnp.sum(jnp.exp(logits - top), axis=1, keepdims=True)
    column = lax.broadcasted_iota(jnp.int32, logits.shape, 1)
    picked = jnp.sum(jnp.where(column == want_ref[:, :1], logits, 0.0), axis=1, keepdims=True)
    lane = lax.broadcasted_iota(jnp.int32, (2 * MB, 128), 1)
    stats = jnp.where(lane == 0, top, jnp.where(lane == 1, total, picked)).T
    for i in range(8):
        mine = slice(i * ROWS, (i + 1) * ROWS)
        line = jnp.concatenate([stats[k : k + 1, mine] for k in (0, 1, 2, 2)], axis=1)
        out_ref[pl.ds(order_ref[i], 1), :] = line
    lines = out_ref[:8, :]
    for s in range(1, 16):
        out_ref[s * 8 : (s + 1) * 8, :] = lines


def vocab(order, blocks, w0, w1, want):
    hbm = pl.BlockSpec(memory_space=pl.ANY)
    vmem = pl.BlockSpec(memory_space=pltpu.VMEM)
    return pl.pallas_call(
        vocab_kernel,
        out_shape=jax.ShapeDtypeStruct((128, 128), F32),
        in_specs=[pl.BlockSpec(memory_space=pltpu.SMEM)] + [hbm] * 10 + [vmem],
        out_specs=vmem,
        scratch_shapes=[
            pltpu.VMEM((2 * MB, WIDTH), BF16),
            pltpu.VMEM((WIDTH, 2 * VL), BF16),
            pltpu.VMEM((2 * MB, 2 * VL), F32),
            pltpu.SemaphoreType.DMA,
            pltpu.SemaphoreType.DMA((WIDTH // VC,)),
        ],
        compiler_params=pltpu.CompilerParams(vmem_limit_bytes=48 * 1024 * 1024),
        cost_estimate=pl.CostEstimate(flops=2 * 10**9, bytes_accessed=14 * 2**20, transcendentals=0),
        name="vocab",
    )(order, *blocks, w0, w1, want)


def add(*terms):
    return sum(t.astype(F32) for t in terms)


BESIDE = [(r, r ^ (2 * 8) ^ NZ) for r in range(128)]


def spread_from_last(final_rows, section):
    y, h = section // 4, section // 2 % 2

    def hop(to):
        return over_section(final_rows, [(15, sec(to, 1, 1))])

    up, down, across = hop(0), hop(2), hop(1)
    rows = jnp.where(y == 3, final_rows, jnp.where(y == 0, up, jnp.where(y == 2, down, across)))
    here = [(r, to) for r, to in BESIDE if r // 8 % 4 == 3]
    return jnp.where(h == 1, rows, lax.ppermute(rows, ("section", "tensor"), here))


def body(
    section_input, positions, attn_gain, w_query, w_keyval, w_out_proj, final_gain, w_vocab, targets
):
    section, rank = lax.axis_index("section"), lax.axis_index("tensor")
    core, x, z = section % 2, rank // NZ, rank % NZ
    my_rows = section_input[0]
    normed = rms_norm(my_rows, attn_gain[0])
    other_vocab = over_section(w_vocab, [(s, s + 1) for s in range(0, 16, 2)])

    zs = (z + jnp.arange(NZ)) % NZ

    def order_from(first_x):
        return (jnp.stack([first_x, 1 - first_x])[:, None] * NZ + zs[None, :]).reshape(-1)

    def tables():
        place = ((zs * ROWS)[:, None] + jnp.arange(ROWS)[None, :]).reshape(-1)
        pos = jnp.take(positions[0].reshape(8, ROWS), order_from(x), axis=0).reshape(-1)
        place2 = jnp.concatenate([place, place])
        frequency = ROPE_THETA ** (-jnp.arange(HEAD // 2, dtype=F32) * 2.0 / HEAD)
        angles = pos.astype(F32)[:, None] * frequency[None, :]
        cos, sin = jnp.cos(angles), jnp.sin(angles)
        cos = jnp.concatenate([cos, cos], axis=1)
        sin = jnp.concatenate([-sin, sin], axis=1)
        keys_at = place[None, :]
        allow = ((keys_at <= place2[:, None]) & (keys_at >= (place2 - pos)[:, None])).astype(F32)
        return cos, sin, allow

    odd = core == 1
    blank = jnp.zeros((ROWS, WIDTH), BF16)
    weights = (w_query[0], w_keyval[0].reshape(WIDTH, -1), w_out_proj[0])
    blocks, angles = lax.cond(
        odd, lambda: (gather_rows(normed), tables()), lambda: ((blank,) * 8, tables())
    )
    def layer_rows(blocks):
        return finish(my_rows, scatter_sum(layer(blocks, *weights, *angles)), final_gain)

    def odd_path():
        layer_out, final_rows = layer_rows(blocks)
        order = order_from(jnp.where(section // 2 % 2 == 1, x, 1 - x))
        starts = jnp.stack([section, section ^ 1]) * 8 * VL + rank * VL
        want = jnp.take(targets.reshape(8, ROWS), order, axis=0).reshape(-1)
        local = want[:, None] - starts[None, :]
        inside = (local >= 0) & (local < VL)
        want = jnp.max(jnp.where(inside, local + jnp.arange(2)[None, :] * VL, -1), axis=1)
        want = jnp.broadcast_to(want[:, None], (2 * MB, 128))
        all_rows = gather_rows(spread_from_last(final_rows, section))
        return layer_out, vocab(order, all_rows, w_vocab, other_vocab, want)

    def even_path():
        return layer_rows(gather_rows(normed))[0], jnp.zeros((128, 128), F32)

    layer_out, stats = lax.cond(odd, odd_path, even_path)
    handed = over_section(layer_out, [(s, s + 1) for s in range(15)])[None]
    got = lax.all_to_all(stats, ("section", "tensor"), 0, 0, tiled=True)
    return handed, merge(got)


def solution(mesh):
    placed = (
        P("section", "tensor", None),
        P("section", None),
        P("section", None),
        P("section", None, "tensor"),
        P("section", None, "tensor", None),
        P("section", "tensor", None),
        P(),
        P(None, ("section", "tensor")),
        P(),
    )
    return jax.shard_map(
        body,
        mesh=mesh,
        in_specs=placed,
        out_specs=(P("section", "tensor", None), P("tensor")),
        check_vma=False,
    )
```

time: 168 us -> 156 us (0.929)
  other arithmetic: 12.6 us -> 3.55 us
  waiting for transfers between devices: 65.2 us -> 73.6 us
  starting transfers between devices: 39.5 us -> 31.6 us
  local copies, waits for them, and re-layouts: 10.5 us -> 3.21 us
  Pallas kernels: 17.3 us -> 22.6 us
    ppermute x7 -> x5, waiting for transfers between devices: 22.4 us -> 0.01 us  [over_section(): return lax.ppermute(block, 'section', pairs)]
    ppermute x0 -> x1, waiting for transfers between devices: none -> 18.8 us  [spread_from_last(): lax.ppermute(rows, ('section', 'tensor'), here)]
    ppermute x27 -> x22, waiting for transfers between devices: 42.8 us -> 54.7 us  [over_tensor(): return lax.ppermute(block, 'tensor', pairs)]
    ppermute x27 -> x22, starting transfers between devices: 31.6 us -> 25 us  [over_tensor(): return lax.ppermute(block, 'tensor', pairs)]
    pallas_call x2 -> x5, Pallas kernels: 17.3 us -> 22.6 us  [the longest x1 12.3 us: layer(): pl.pallas_call(layer_kernel, out_shape=[jax.ShapeDtypeStruct((ROWS, WIDTH...]
    slice x6 -> x0, local copies, waits for them, and re-layouts: 3.83 us -> none  [the longest x2 1.73 us: gather_rows(): far_b = move(above[half:], TO_DOWN)]
    reduce_sum x4 -> x0, other arithmetic: 3.35 us -> none  [the longest x2 2.54 us: rms_norm(): jnp.mean(values * values, axis=-1, keepdims=True) + NORM_EPSILON]
    ppermute x7 -> x5, starting transfers between devices: 7.86 us -> 5.28 us  [over_section(): return lax.ppermute(block, 'section', pairs)]
  transfers between devices with their start and end apart: 34 -> 28, of which waited for: 15 -> 13; matrix products, arithmetic and copies ran while one was open for 11% -> 4% of each run, Pallas kernels for 0% -> 2%
where the time goes in v3:
time: 156 us
  waiting for transfers between devices  73.6 us (47%)
  starting transfers between devices  31.6 us (20%)
  Pallas kernels  22.6 us (14%)
  blocking collectives  20 us (13%)
  other arithmetic  3.55 us (2%)
  local copies, waits for them, and re-layouts  3.21 us (2%)
    ppermute x22, waiting for transfers between devices, over_tensor(): return lax.ppermute(block, 'tensor', pairs)  54.7 us
    ppermute x22, starting transfers between devices, over_tensor(): return lax.ppermute(block, 'tensor', pairs)  25 us
    all_to_all x1, blocking collectives, body(): got = lax.all_to_all(stats, ('section', 'tensor'), 0, 0, tiled=True)  20 us
    ppermute x1, waiting for transfers between devices, spread_from_last(): lax.ppermute(rows, ('section', 'tensor'), here)  18.8 us
    pallas_call x1, Pallas kernels, layer(): pl.pallas_call(layer_kernel, out_shape=[jax.ShapeDtypeStruct((ROWS, WIDTH...  12.3 us
    pallas_call x1, Pallas kernels, vocab(): pl.pallas_call(vocab_kernel, out_shape=jax.ShapeDtypeStruct((128, 128), F...  6.14 us
    ppermute x5, starting transfers between devices, over_section(): return lax.ppermute(block, 'section', pairs)  5.28 us
  transfers between devices with their start and end apart: 28, of which 13 were waited for; matrix products, arithmetic and copies ran while one was open for 4% of the time, Pallas kernels for 2%

profile of v3, /device:TPU:1, one launch (start us, length us, event | category | flops | bytes accessed | tf_op | source)
XLA Modules:
  0.0 155.9 jit_solution(4368775624825192855)
XLA Ops:
  0.6 1.3 collective-permute-start.41
  2.0 1.4 norm.1
  3.4 32.1 %conditional.6 = (bf16[32,8192]{1,0:T(8,128)(2,1)S(1)}, bf16[32,8192]{1,0:T(8,128)(2,1)}, bf16[32,8192]{1,0:T(8,128)(2,1)}, bf16[32,8192]{1,0:T(8,128)(2,1)}, bf...) conditional(s32[]{:T(128)} %convert_element_type.122, ...), branch_computations={%region_0.2_spmd, %region_1.3_spmd} | conditional | flops 231513 | bytes 16541936
  3.4 2.5 %collective-permute-start.35 = (bf16[32,8192]{1,0:T(8,128)(2,1)S(1)}, bf16[32,8192]{1,0:T(8,128)(2,1)}, u32[]{:S(2)}, u32[]{:S(2)}) collective-permute-start(bf16[32,8192]{1,0:T(8,128)(2,1)S(1)} %get-tuple-element.237), channel_id=1, source_target_pairs={{0,1},{1,2},{2,3},{3,0},{4,5},{5,6},{6,7},{7,4},{8,9},{9,10},{10,1... | collective-permute-start | bytes 1572872 | tf_op jit(solution)/shard_map/cond/branch_1_fun/ppermute | solution.py:43
  7.2 2.2 %collective-permute-start.34 = (bf16[32,8192]{1,0:T(8,128)(2,1)S(1)}, bf16[32,8192]{1,0:T(8,128)(2,1)}, u32[]{:S(2)}, u32[]{:S(2)}) collective-permute-start(bf16[32,8192]{1,0:T(8,128)(2,1)S(1)} %get-tuple-element.237), channel_id=1, source_target_pairs={{0,3},{1,0},{2,1},{3,2},{4,7},{5,4},{6,5},{7,6},{8,11},{9,8},{10,9... | collective-permute-start | bytes 1572872 | tf_op jit(solution)/shard_map/cond/branch_1_fun/ppermute | solution.py:43
  10.2 1.3 reduce.7
  12.5 2.3 %collective-permute-done.35 = bf16[32,8192]{1,0:T(8,128)(2,1)} collective-permute-done((bf16[32,8192]{1,0:T(8,128)(2,1)S(1)}, bf16[32,8192]{1,0:T(8,128)(2,1)}, u32[]{:S(2)}, u32[]{:S(2)}) %collective-permute-start.35) | collective-permute-done | bytes 524320 | tf_op jit(solution)/shard_map/cond/branch_1_fun/ppermute | solution.py:43
  14.8 2.7 %collective-permute-start.38 = (bf16[32,8192]{1,0:T(8,128)(2,1)}, bf16[32,8192]{1,0:T(8,128)(2,1)}, u32[]{:S(2)}, u32[]{:S(2)}) collective-permute-start(bf16[32,8192]{1,0:T(8,128)(2,1)} %collective-permute-done.37), channel_id=1, source_target_pairs={{0,3},{1,0},{2,1},{3,2},{4,7},{5,4},{6,5},{7,6},{8,11},{9,8},{10,9... | collective-permute-start | bytes 1572872 | tf_op jit(solution)/shard_map/cond/branch_1_fun/ppermute | solution.py:43
  17.6 8.8 %collective-permute-done.36 = bf16[32,8192]{1,0:T(8,128)(2,1)} collective-permute-done((bf16[32,8192]{1,0:T(8,128)(2,1)}, bf16[32,8192]{1,0:T(8,128)(2,1)}, u32[]{:S(2)}, u32[]{:S(2)}) %collective-permute-start.36) | collective-permute-done | bytes 524320 | tf_op jit(solution)/shard_map/cond/branch_1_fun/ppermute | solution.py:43
  28.5 7.1 %collective-permute-done.40 = bf16[32,8192]{1,0:T(8,128)(2,1)} collective-permute-done((bf16[32,8192]{1,0:T(8,128)(2,1)}, bf16[32,8192]{1,0:T(8,128)(2,1)}, u32[]{:S(2)}, u32[]{:S(2)}) %collective-permute-start.40) | collective-permute-done | bytes 524320 | tf_op jit(solution)/shard_map/cond/branch_1_fun/ppermute | solution.py:43
  35.6 95.9 %conditional.5 = (bf16[32,8192]{1,0:T(8,128)(2,1)}, f32[128,128]{1,0:T(8,128)}) conditional(s32[]{:T(128)} %convert_element_type.122, (bf16[32,8192]{1,0:T(8,128)(2,1)S(1)}, bf16[8192,512]{1,0:T(8,128)(2,1)}, bf16[8192,256]{1,0:T(8,128)(2,1)}, bf16[512,8192]{1,0:T(8,128)(2,1)}, f32[256,128]{1,0:T(8,128)S(1)}, /*index=5*/f32[256,128]{1,0:T(8,128)S(1)}, ...), branch_computations={%region_2.4_spmd, %region_3.6_spmd} | conditional | flops 8006819840 | bytes 94618192 | solution.py:359
  35.8 12.3 %layer.3 = (bf16[32,8192]{1,0:T(8,128)(2,1)S(1)}, bf16[32,8192]{1,0:T(8,128)(2,1)S(1)}, bf16[32,8192]{1,0:T(8,128)(2,1)S(1)}, bf16[32,8192]{1,0:T(8,128)(2,1)S(1...) custom-call(bf16[32,8192]{1,0:T(8,128)(2,1)S(1)} %get-tuple-element., ...), custom_call_target="tpu_custom_call" | custom-call | flops 6000000000 | bytes 29360128 | tf_op jit(solution)/shard_map/cond/branch_1_fun/layer/pallas_call | solution.py:205
  48.1 1.3 collective-permute-start.18
  49.4 2.7 %collective-permute-start.16 = (bf16[32,8192]{1,0:T(8,128)(2,1)S(1)}, bf16[32,8192]{1,0:T(8,128)(2,1)S(1)}, u32[]{:S(2)}, u32[]{:S(2)}) collective-permute-start(bf16[32,8192]{1,0:T(8,128)(2,1)S(1)} %get-tuple-element.148), channel_id=1, source_target_pairs={{0,3},{1,0},{2,1},{3,2},{4,7},{5,4},{6,5},{7,6},{8,11},{9,8},{10,9... | collective-permute-start | bytes 1572872 | tf_op jit(solution)/shard_map/cond/branch_1_fun/ppermute | solution.py:43
  52.1 6.7 %collective-permute-done.18 = bf16[32,8192]{1,0:T(8,128)(2,1)S(1)} collective-permute-done((bf16[32,8192]{1,0:T(8,128)(2,1)S(1)}, bf16[32,8192]{1,0:T(8,128)(2,1)S(1)}, u32[]{:S(2)}, u32[]{:S(2)}) %collective-permute-start.18) | collective-permute-done | bytes 524320 | tf_op jit(solution)/shard_map/cond/branch_1_fun/ppermute | solution.py:43
  59.0 2.7 %collective-permute-start.19 = (bf16[16,8192]{1,0:T(8,128)(2,1)S(1)}, bf16[16,8192]{1,0:T(8,128)(2,1)S(1)}, u32[]{:S(2)}, u32[]{:S(2)}) collective-permute-start(bf16[16,8192]{1,0:T(8,128)(2,1)S(1)} %get-tuple-element.209), channel_id=1, source_target_pairs={{0,3},{1,0},{2,1},{3,2},{4,7},{5,4},{6,5},{7,6},{8,11},{9,8},{10,9... | collective-permute-start | bytes 786440 | tf_op jit(solution)/shard_map/cond/branch_1_fun/ppermute | solution.py:43
  61.8 1.3 collective-permute-start.17
  63.1 2.3 %collective-permute-done.21 = bf16[16,8192]{1,0:T(8,128)(2,1)S(1)} collective-permute-done((bf16[16,8192]{1,0:T(8,128)(2,1)S(1)}, bf16[16,8192]{1,0:T(8,128)(2,1)S(1)}, u32[]{:S(2)}, u32[]{:S(2)}) %collective-permute-start.21) | collective-permute-done | bytes 262176 | tf_op jit(solution)/shard_map/cond/branch_1_fun/ppermute | solution.py:43
  65.7 2.7 %collective-permute-start.20 = (bf16[32,8192]{1,0:T(8,128)(2,1)S(1)}, bf16[32,8192]{1,0:T(8,128)(2,1)S(1)}, u32[]{:S(2)}, u32[]{:S(2)}) collective-permute-start(bf16[32,8192]{1,0:T(8,128)(2,1)S(1)} %pad_maximum_fusion.2), channel_id=1, source_target_pairs={{0,3},{1,0},{2,1},{3,2},{4,7},{5,4},{6,5},{7,6},{8,11},{9,8},{10,9... | collective-permute-start | bytes 1572872 | tf_op jit(solution)/shard_map/cond/branch_1_fun/ppermute | solution.py:43
  68.5 1.5 collective-permute-done.17.b_ref
  69.9 4.9 %collective-permute-done.22.d_ref = bf16[32,8192]{1,0:T(8,128)(2,1)S(1)} collective-permute-done((bf16[32,8192]{1,0:T(8,128)(2,1)S(1)}, bf16[32,8192]{1,0:T(8,128)(2,1)S(1)}, u32[]{:S(2)}, u32[]{:S(2)}) %collective-permute-start.22) | collective-permute-done | bytes 524320 | tf_op jit(solution)/shard_map/cond/branch_1_fun/ppermute | solution.py:43
  78.2 1.3 collective-permute-start.26
  79.6 18.8 %collective-permute-done.26 = bf16[32,8192]{1,0:T(8,128)(2,1)S(1)} collective-permute-done((bf16[32,8192]{1,0:T(8,128)(2,1)S(1)}, bf16[32,8192]{1,0:T(8,128)(2,1)S(1)}, u32[]{:S(2)}, u32[]{:S(2)}) %collective-permute-start.26) | collective-permute-done | bytes 524320 | tf_op jit(solution)/shard_map/cond/branch_1_fun/ppermute | solution.py:305
  98.7 9.2 %collective-permute-done.28.refs_3_ = bf16[32,8192]{1,0:T(8,128)(2,1)S(1)} collective-permute-done((bf16[32,8192]{1,0:T(8,128)(2,1)S(1)}, bf16[32,8192]{1,0:T(8,128)(2,1)S(1)}, u32[]{:S(2)}, u32[]{:S(2)}) %collective-permute-start.28) | collective-permute-done | bytes 524320 | tf_op jit(solution)/shard_map/cond/branch_1_fun/ppermute | solution.py:43
  108.1 2.7 %collective-permute-start.27 = (bf16[32,8192]{1,0:T(8,128)(2,1)S(1)}, bf16[32,8192]{1,0:T(8,128)(2,1)S(1)}, u32[]{:S(2)}, u32[]{:S(2)}) collective-permute-start(bf16[32,8192]{1,0:T(8,128)(2,1)S(1)} %broadcast_select_fusion.refs_0_), channel_id=1, source_target_pairs={{0,3},{1,0},{2,1},{3,2},{4,7},{5,4},{6,5},{7,6},{8,11},{9,8},{10,9... | collective-permute-start | bytes 1572872 | tf_op jit(solution)/shard_map/cond/branch_1_fun/ppermute | solution.py:43
  112.3 4.8 %collective-permute-done.29.refs_2_ = bf16[32,8192]{1,0:T(8,128)(2,1)S(1)} collective-permute-done((bf16[32,8192]{1,0:T(8,128)(2,1)S(1)}, bf16[32,8192]{1,0:T(8,128)(2,1)S(1)}, u32[]{:S(2)}, u32[]{:S(2)}) %collective-permute-start.29) | collective-permute-done | bytes 524320 | tf_op jit(solution)/shard_map/cond/branch_1_fun/ppermute | solution.py:43
  118.0 4.6 %collective-permute-done.31.refs_5_ = bf16[32,8192]{1,0:T(8,128)(2,1)S(1)} collective-permute-done((bf16[32,8192]{1,0:T(8,128)(2,1)S(1)}, bf16[32,8192]{1,0:T(8,128)(2,1)S(1)}, u32[]{:S(2)}, u32[]{:S(2)}) %collective-permute-start.31) | collective-permute-done | bytes 524320 | tf_op jit(solution)/shard_map/cond/branch_1_fun/ppermute | solution.py:43
  122.8 2.4 %collective-permute-done.32.refs_6_ = bf16[32,8192]{1,0:T(8,128)(2,1)} collective-permute-done((bf16[32,8192]{1,0:T(8,128)(2,1)S(1)}, bf16[32,8192]{1,0:T(8,128)(2,1)}, u32[]{:S(2)}, u32[]{:S(2)}) %collective-permute-start.32) | collective-permute-done | bytes 524320 | tf_op jit(solution)/shard_map/cond/branch_1_fun/ppermute | solution.py:43
  125.3 6.1 %vocab.1 = f32[128,128]{1,0:T(8,128)} custom-call(s32[8]{0:T(128)S(1)} %add.172.order_ref, bf16[32,8192]{1,0:T(8,128)(2,1)S(1)} %broadcast_select_fusion.refs_0_, bf16[32,8192]{1,0:T(8,128)(2,1)S(1)} %collective-permute-done.27.refs_1_, bf16[32,8192]{1,0:T(8,128)(2,1)S(1)} %collective-permute-done.29.refs_2_, ...), custom_call_target="tpu_custom_call" | custom-call | flops 2000000000 | bytes 14680064 | tf_op jit(solution)/shard_map/cond/branch_1_fun/vocab/pallas_call | solution.py:271
  131.5 1.9 %collective-permute-start.42 = (bf16[32,8192]{1,0:T(8,128)(2,1)}, bf16[32,8192]{1,0:T(8,128)(2,1)S(1)}, u32[]{:S(2)}, u32[]{:S(2)}) collective-permute-start(bf16[32,8192]{1,0:T(8,128)(2,1)} %get-tuple-element.189), channel_id=1, source_target_pairs={{0,8},{8,16},{16,24},{24,32},{32,40},{40,48},{48,56},{56,64},{64,7... | collective-permute-start | bytes 1572872 | tf_op jit(solution)/shard_map/ppermute | solution.py:47
  133.4 20.0 %all_to_all.11 = f32[128,1,128]{2,1,0:T(1,128)} all-to-all(f32[128,1,128]{2,1,0:T(1,128)} %bitcast.13), channel_id=1, replica_groups=mesh['section'=16,'tensor'=8] {'section','tensor'}, dimensions={0} | all-to-all | bytes 131072 | tf_op jit(solution)/shard_map/all_to_all | solution.py:361
  153.5 1.6 %merge.1 = f32[32]{0:T(128)} custom-call(f32[128,128]{1,0:T(8,128)} %bitcast.25), custom_call_target="tpu_custom_call" | custom-call | tf_op jit(solution)/shard_map/merge/pallas_call | solution.py:126
  (88 shorter events, 13.1 us)
Async XLA Ops:
  0.6 34.9 %collective-permute-start.41 = (bf16[8192,256]{1,0:T(8,128)(2,1)}, bf16[8192,256]{1,0:T(8,128)(2,1)}, u32[]{:S(2)}, u32[]{:S(2)}) collective-permute-start(bf16[8192,256]{1,0:T(8,128)(2,1)} %param.22), channel_id=1, source_target_pairs={{0,8},{16,24},{32,40},{48,56},{64,72},{80,88},{96,104},{112,120},{... | collective-permute-start | bytes 12582920 | tf_op jit(solution)/shard_map/ppermute | solution.py:47
  3.4 32.2 %copy-start = (bf16[1,32,8192]{2,1,0:T(8,128)(2,1)S(1)}, bf16[1,32,8192]{2,1,0:T(8,128)(2,1)}, u32[]{:S(2)}) copy-start(bf16[1,32,8192]{2,1,0:T(8,128)(2,1)} %param.15) | copy-start | bytes 1572868
  3.4 32.2 %copy-start.7 = (s32[256]{0:T(256)S(1)}, s32[256]{0:T(256)}, u32[]{:S(2)}) copy-start(s32[256]{0:T(256)} %param.23) | copy-start | bytes 3076
  3.4 11.3 %collective-permute-start.35 = (bf16[32,8192]{1,0:T(8,128)(2,1)S(1)}, bf16[32,8192]{1,0:T(8,128)(2,1)}, u32[]{:S(2)}, u32[]{:S(2)}) collective-permute-start(bf16[32,8192]{1,0:T(8,128)(2,1)S(1)} %get-tuple-element.237), channel_id=1, source_target_pairs={{0,1},{1,2},{2,3},{3,0},{4,5},{5,6},{6,7},{7,4},{8,9},{9,10},{10,1... | collective-permute-start | bytes 1572872 | tf_op jit(solution)/shard_map/cond/branch_1_fun/ppermute | solution.py:43
  6.0 8.9 %collective-permute-start.37 = (bf16[32,8192]{1,0:T(8,128)(2,1)S(1)}, bf16[32,8192]{1,0:T(8,128)(2,1)}, u32[]{:S(2)}, u32[]{:S(2)}) collective-permute-start(bf16[32,8192]{1,0:T(8,128)(2,1)S(1)} %get-tuple-element.237), channel_id=1, source_target_pairs={{0,4},{1,5},{2,6},{3,7},{4,0},{5,1},{6,2},{7,3},{8,12},{9,13},{10,... | collective-permute-start | bytes 1572872 | tf_op jit(solution)/shard_map/cond/branch_1_fun/ppermute | solution.py:43
  7.2 21.3 %collective-permute-start.34 = (bf16[32,8192]{1,0:T(8,128)(2,1)S(1)}, bf16[32,8192]{1,0:T(8,128)(2,1)}, u32[]{:S(2)}, u32[]{:S(2)}) collective-permute-start(bf16[32,8192]{1,0:T(8,128)(2,1)S(1)} %get-tuple-element.237), channel_id=1, source_target_pairs={{0,3},{1,0},{2,1},{3,2},{4,7},{5,4},{6,5},{7,6},{8,11},{9,8},{10,9... | collective-permute-start | bytes 1572872 | tf_op jit(solution)/shard_map/cond/branch_1_fun/ppermute | solution.py:43
  14.8 11.6 %collective-permute-start.36 = (bf16[32,8192]{1,0:T(8,128)(2,1)}, bf16[32,8192]{1,0:T(8,128)(2,1)}, u32[]{:S(2)}, u32[]{:S(2)}) collective-permute-start(bf16[32,8192]{1,0:T(8,128)(2,1)} %collective-permute-done.35), channel_id=1, source_target_pairs={{0,1},{1,2},{2,3},{3,0},{4,5},{5,6},{6,7},{7,4},{8,9},{9,10},{10,1... | collective-permute-start | bytes 1572872 | tf_op jit(solution)/shard_map/cond/branch_1_fun/ppermute | solution.py:43
  14.8 13.6 %collective-permute-start.38 = (bf16[32,8192]{1,0:T(8,128)(2,1)}, bf16[32,8192]{1,0:T(8,128)(2,1)}, u32[]{:S(2)}, u32[]{:S(2)}) collective-permute-start(bf16[32,8192]{1,0:T(8,128)(2,1)} %collective-permute-done.37), channel_id=1, source_target_pairs={{0,3},{1,0},{2,1},{3,2},{4,7},{5,4},{6,5},{7,6},{8,11},{9,8},{10,9... | collective-permute-start | bytes 1572872 | tf_op jit(solution)/shard_map/cond/branch_1_fun/ppermute | solution.py:43
  17.6 18.0 %collective-permute-start.40 = (bf16[32,8192]{1,0:T(8,128)(2,1)}, bf16[32,8192]{1,0:T(8,128)(2,1)}, u32[]{:S(2)}, u32[]{:S(2)}) collective-permute-start(bf16[32,8192]{1,0:T(8,128)(2,1)} %collective-permute-done.37), channel_id=1, source_target_pairs={{0,1},{1,2},{2,3},{3,0},{4,5},{5,6},{6,7},{7,4},{8,9},{9,10},{10,1... | collective-permute-start | bytes 1572872 | tf_op jit(solution)/shard_map/cond/branch_1_fun/ppermute | solution.py:43
  26.4 9.2 %collective-permute-start.39 = (bf16[32,8192]{1,0:T(8,128)(2,1)}, bf16[32,8192]{1,0:T(8,128)(2,1)}, u32[]{:S(2)}, u32[]{:S(2)}) collective-permute-start(bf16[32,8192]{1,0:T(8,128)(2,1)} %collective-permute-done.36), channel_id=1, source_target_pairs={{0,4},{1,5},{2,6},{3,7},{4,0},{5,1},{6,2},{7,3},{8,12},{9,13},{10,... | collective-permute-start | bytes 1572872 | tf_op jit(solution)/shard_map/cond/branch_1_fun/ppermute | solution.py:43
  48.1 10.7 %collective-permute-start.18 = (bf16[32,8192]{1,0:T(8,128)(2,1)S(1)}, bf16[32,8192]{1,0:T(8,128)(2,1)S(1)}, u32[]{:S(2)}, u32[]{:S(2)}) collective-permute-start(bf16[32,8192]{1,0:T(8,128)(2,1)S(1)} %get-tuple-element.151), channel_id=1, source_target_pairs={{0,4},{1,5},{2,6},{3,7},{4,0},{5,1},{6,2},{7,3},{8,12},{9,13},{10,... | collective-permute-start | bytes 1572872 | tf_op jit(solution)/shard_map/cond/branch_1_fun/ppermute | solution.py:43
  49.4 12.3 %collective-permute-start.15 = (bf16[32,8192]{1,0:T(8,128)(2,1)S(1)}, bf16[32,8192]{1,0:T(8,128)(2,1)S(1)}, u32[]{:S(2)}, u32[]{:S(2)}) collective-permute-start(bf16[32,8192]{1,0:T(8,128)(2,1)S(1)} %get-tuple-element.147), channel_id=1, source_target_pairs={{0,1},{1,2},{2,3},{3,0},{4,5},{5,6},{6,7},{7,4},{8,9},{9,10},{10,1... | collective-permute-start | bytes 1572872 | tf_op jit(solution)/shard_map/cond/branch_1_fun/ppermute | solution.py:43
  49.4 12.3 %collective-permute-start.16 = (bf16[32,8192]{1,0:T(8,128)(2,1)S(1)}, bf16[32,8192]{1,0:T(8,128)(2,1)S(1)}, u32[]{:S(2)}, u32[]{:S(2)}) collective-permute-start(bf16[32,8192]{1,0:T(8,128)(2,1)S(1)} %get-tuple-element.148), channel_id=1, source_target_pairs={{0,3},{1,0},{2,1},{3,2},{4,7},{5,4},{6,5},{7,6},{8,11},{9,8},{10,9... | collective-permute-start | bytes 1572872 | tf_op jit(solution)/shard_map/cond/branch_1_fun/ppermute | solution.py:43
  52.1 16.4 %copy-start.6 = (bf16[8192]{0:T(1024)(128)(2,1)S(1)}, bf16[8192]{0:T(1024)(128)(2,1)}, u32[]{:S(2)}) copy-start(bf16[8192]{0:T(1024)(128)(2,1)} %get-tuple-element.153) | copy-start | bytes 49156 | tf_op jit(solution)/shard_map/cond
  58.9 6.5 %collective-permute-start.21 = (bf16[16,8192]{1,0:T(8,128)(2,1)S(1)}, bf16[16,8192]{1,0:T(8,128)(2,1)S(1)}, u32[]{:S(2)}, u32[]{:S(2)}) collective-permute-start(bf16[16,8192]{1,0:T(8,128)(2,1)S(1)} %get-tuple-element.208), channel_id=1, source_target_pairs={{0,1},{1,2},{2,3},{3,0},{4,5},{5,6},{6,7},{7,4},{8,9},{9,10},{10,1... | collective-permute-start | bytes 786440 | tf_op jit(solution)/shard_map/cond/branch_1_fun/ppermute | solution.py:43
  59.0 6.6 %collective-permute-start.19 = (bf16[16,8192]{1,0:T(8,128)(2,1)S(1)}, bf16[16,8192]{1,0:T(8,128)(2,1)S(1)}, u32[]{:S(2)}, u32[]{:S(2)}) collective-permute-start(bf16[16,8192]{1,0:T(8,128)(2,1)S(1)} %get-tuple-element.209), channel_id=1, source_target_pairs={{0,3},{1,0},{2,1},{3,2},{4,7},{5,4},{6,5},{7,6},{8,11},{9,8},{10,9... | collective-permute-start | bytes 786440 | tf_op jit(solution)/shard_map/cond/branch_1_fun/ppermute | solution.py:43
  61.8 8.1 %collective-permute-start.17 = (bf16[32,8192]{1,0:T(8,128)(2,1)S(1)}, bf16[32,8192]{1,0:T(8,128)(2,1)S(1)}, u32[]{:S(2)}, u32[]{:S(2)}) collective-permute-start(bf16[32,8192]{1,0:T(8,128)(2,1)S(1)} %add_convert_fusion.5), channel_id=1, source_target_pairs={{0,4},{1,5},{2,6},{3,7},{4,0},{5,1},{6,2},{7,3},{8,12},{9,13},{10,... | collective-permute-start | bytes 1572872 | tf_op jit(solution)/shard_map/cond/branch_1_fun/ppermute | solution.py:43
  65.5 9.3 %collective-permute-start.22 = (bf16[32,8192]{1,0:T(8,128)(2,1)S(1)}, bf16[32,8192]{1,0:T(8,128)(2,1)S(1)}, u32[]{:S(2)}, u32[]{:S(2)}) collective-permute-start(bf16[32,8192]{1,0:T(8,128)(2,1)S(1)} %pad_maximum_fusion.3), channel_id=1, source_target_pairs={{0,1},{1,2},{2,3},{3,0},{4,5},{5,6},{6,7},{7,4},{8,9},{9,10},{10,1... | collective-permute-start | bytes 1572872 | tf_op jit(solution)/shard_map/cond/branch_1_fun/ppermute | solution.py:43
  65.7 9.1 %collective-permute-start.20 = (bf16[32,8192]{1,0:T(8,128)(2,1)S(1)}, bf16[32,8192]{1,0:T(8,128)(2,1)S(1)}, u32[]{:S(2)}, u32[]{:S(2)}) collective-permute-start(bf16[32,8192]{1,0:T(8,128)(2,1)S(1)} %pad_maximum_fusion.2), channel_id=1, source_target_pairs={{0,3},{1,0},{2,1},{3,2},{4,7},{5,4},{6,5},{7,6},{8,11},{9,8},{10,9... | collective-permute-start | bytes 1572872 | tf_op jit(solution)/shard_map/cond/branch_1_fun/ppermute | solution.py:43
  76.0 2.1 %collective-permute-start.23 = (bf16[32,8192]{1,0:T(8,128)(2,1)S(1)}, bf16[32,8192]{1,0:T(8,128)(2,1)S(1)}, u32[]{:S(2)}, u32[]{:S(2)}) collective-permute-start(bf16[32,8192]{1,0:T(8,128)(2,1)S(1)} %get-tuple-element.158), channel_id=1, source_target_pairs={{120,24},{121,25},{122,26},{123,27},{124,28},{125,29},{126,30},{12... | collective-permute-start | bytes 1572872 | tf_op jit(solution)/shard_map/cond/branch_1_fun/ppermute | solution.py:47
  76.7 1.4 collective-permute-start.24
  77.4 0.7 collective-permute-start.25
  78.2 20.2 %collective-permute-start.26 = (bf16[32,8192]{1,0:T(8,128)(2,1)S(1)}, bf16[32,8192]{1,0:T(8,128)(2,1)S(1)}, u32[]{:S(2)}, u32[]{:S(2)}) collective-permute-start(bf16[32,8192]{1,0:T(8,128)(2,1)S(1)} %select_select_fusion), channel_id=1, source_target_pairs={{24,12},{25,13},{26,14},{27,15},{28,8},{29,9},{30,10},{31,11},{56,... | collective-permute-start | bytes 1572872 | tf_op jit(solution)/shard_map/cond/branch_1_fun/ppermute | solution.py:305
  98.5 9.4 %collective-permute-start.28 = (bf16[32,8192]{1,0:T(8,128)(2,1)S(1)}, bf16[32,8192]{1,0:T(8,128)(2,1)S(1)}, u32[]{:S(2)}, u32[]{:S(2)}) collective-permute-start(bf16[32,8192]{1,0:T(8,128)(2,1)S(1)} %broadcast_select_fusion.refs_0_), channel_id=1, source_target_pairs={{0,1},{1,2},{2,3},{3,0},{4,5},{5,6},{6,7},{7,4},{8,9},{9,10},{10,1... | collective-permute-start | bytes 1572872 | tf_op jit(solution)/shard_map/cond/branch_1_fun/ppermute | solution.py:43
  98.6 12.2 %collective-permute-start.30 = (bf16[32,8192]{1,0:T(8,128)(2,1)S(1)}, bf16[32,8192]{1,0:T(8,128)(2,1)S(1)}, u32[]{:S(2)}, u32[]{:S(2)}) collective-permute-start(bf16[32,8192]{1,0:T(8,128)(2,1)S(1)} %broadcast_select_fusion.refs_0_), channel_id=1, source_target_pairs={{0,4},{1,5},{2,6},{3,7},{4,0},{5,1},{6,2},{7,3},{8,12},{9,13},{10,... | collective-permute-start | bytes 1572872 | tf_op jit(solution)/shard_map/cond/branch_1_fun/ppermute | solution.py:43
  107.9 9.2 %collective-permute-start.29 = (bf16[32,8192]{1,0:T(8,128)(2,1)S(1)}, bf16[32,8192]{1,0:T(8,128)(2,1)S(1)}, u32[]{:S(2)}, u32[]{:S(2)}) collective-permute-start(bf16[32,8192]{1,0:T(8,128)(2,1)S(1)} %collective-permute-done.28.refs_3_), channel_id=1, source_target_pairs={{0,1},{1,2},{2,3},{3,0},{4,5},{5,6},{6,7},{7,4},{8,9},{9,10},{10,1... | collective-permute-start | bytes 1572872 | tf_op jit(solution)/shard_map/cond/branch_1_fun/ppermute | solution.py:43
  108.1 9.9 %collective-permute-start.27 = (bf16[32,8192]{1,0:T(8,128)(2,1)S(1)}, bf16[32,8192]{1,0:T(8,128)(2,1)S(1)}, u32[]{:S(2)}, u32[]{:S(2)}) collective-permute-start(bf16[32,8192]{1,0:T(8,128)(2,1)S(1)} %broadcast_select_fusion.refs_0_), channel_id=1, source_target_pairs={{0,3},{1,0},{2,1},{3,2},{4,7},{5,4},{6,5},{7,6},{8,11},{9,8},{10,9... | collective-permute-start | bytes 1572872 | tf_op jit(solution)/shard_map/cond/branch_1_fun/ppermute | solution.py:43
  110.9 11.7 %collective-permute-start.31 = (bf16[32,8192]{1,0:T(8,128)(2,1)S(1)}, bf16[32,8192]{1,0:T(8,128)(2,1)S(1)}, u32[]{:S(2)}, u32[]{:S(2)}) collective-permute-start(bf16[32,8192]{1,0:T(8,128)(2,1)S(1)} %collective-permute-done.30.refs_4_), channel_id=1, source_target_pairs={{0,3},{1,0},{2,1},{3,2},{4,7},{5,4},{6,5},{7,6},{8,11},{9,8},{10,9... | collective-permute-start | bytes 1572872 | tf_op jit(solution)/shard_map/cond/branch_1_fun/ppermute | solution.py:43
  111.1 11.7 %collective-permute-start.33 = (bf16[32,8192]{1,0:T(8,128)(2,1)S(1)}, bf16[32,8192]{1,0:T(8,128)(2,1)}, u32[]{:S(2)}, u32[]{:S(2)}) collective-permute-start(bf16[32,8192]{1,0:T(8,128)(2,1)S(1)} %collective-permute-done.30.refs_4_), channel_id=1, source_target_pairs={{0,1},{1,2},{2,3},{3,0},{4,5},{5,6},{6,7},{7,4},{8,9},{9,10},{10,1... | collective-permute-start | bytes 1572872 | tf_op jit(solution)/shard_map/cond/branch_1_fun/ppermute | solution.py:43
  117.1 8.1 %collective-permute-start.32 = (bf16[32,8192]{1,0:T(8,128)(2,1)S(1)}, bf16[32,8192]{1,0:T(8,128)(2,1)}, u32[]{:S(2)}, u32[]{:S(2)}) collective-permute-start(bf16[32,8192]{1,0:T(8,128)(2,1)S(1)} %collective-permute-done.29.refs_2_), channel_id=1, source_target_pairs={{0,4},{1,5},{2,6},{3,7},{4,0},{5,1},{6,2},{7,3},{8,12},{9,13},{10,... | collective-permute-start | bytes 1572872 | tf_op jit(solution)/shard_map/cond/branch_1_fun/ppermute | solution.py:43
  131.5 23.6 %collective-permute-start.42 = (bf16[32,8192]{1,0:T(8,128)(2,1)}, bf16[32,8192]{1,0:T(8,128)(2,1)S(1)}, u32[]{:S(2)}, u32[]{:S(2)}) collective-permute-start(bf16[32,8192]{1,0:T(8,128)(2,1)} %get-tuple-element.189), channel_id=1, source_target_pairs={{0,8},{8,16},{16,24},{24,32},{32,40},{40,48},{48,56},{56,64},{64,7... | collective-permute-start | bytes 1572872 | tf_op jit(solution)/shard_map/ppermute | solution.py:47

commit v4 on v3

--- a/solution.py
+++ b/solution.py
@@ -64,6 +64,31 @@
 
 def gather_rows(own):
     return gather_rest(own, gather_first(own))
+
+
+def gather_rows_split(own):
+    from_x = over_tensor(own, TO_X)
+    below = over_tensor(own, TO_UP)
+    above = over_tensor(own, TO_DOWN)
+    far_a = over_tensor(below[:HALF], TO_UP)
+    far_b = over_tensor(above[HALF:], TO_DOWN)
+    x_below = over_tensor(from_x, TO_UP)
+    x_above = over_tensor(from_x, TO_DOWN)
+    far = jnp.concatenate([far_a, far_b])
+    x_far = over_tensor(far, TO_X)
+    return own, above, far, below, from_x, x_above, x_far, x_below
+
+
+def gather_pairs(own):
+    from_x = over_tensor(own, TO_X)
+    pair = jnp.concatenate([own, from_x])
+    below = over_tensor(pair, TO_UP)
+    above = over_tensor(pair, TO_DOWN)
+    far_a = over_tensor(below[:HALF], TO_UP)
+    far_b = over_tensor(above[HALF:ROWS], TO_DOWN)
+    far = jnp.concatenate([far_a, far_b])
+    x_far = over_tensor(far, TO_X)
+    return own, above[:ROWS], far, below[:ROWS], from_x, above[ROWS:], x_far, below[ROWS:]
 
 
 def scatter_sum(parts):
@@ -141,7 +166,7 @@
     blocks = refs[:8]
     wq_ref, wkv_ref, wo_ref, cos_ref, sin_ref, allow_ref = refs[8:14]
     outs = refs[14:22]
-    rows, w, wo, acc, ctx, res, row_sem, w_sem, wo_sem, out_sem = refs[22:]
+    rows, w, wo, acc, ctx, row_sem, w_sem, wo_sem = refs[22:]
 
     for i, b in enumerate(blocks):
         pltpu.make_async_copy(b, rows.at[pl.ds(i * ROWS, ROWS)], row_sem).start()
@@ -192,11 +217,9 @@
     def _(n):
         cols = at(n, NC)
         pltpu.make_async_copy(wo.at[:, cols], wo.at[:, cols], wo_sem.at[n]).wait()
-        res[:, cols] = jnp.dot(ctx[...], wo[:, cols], preferred_element_type=F32).astype(BF16)
+        part = jnp.dot(ctx[...], wo[:, cols], preferred_element_type=F32).astype(BF16)
         for i, o in enumerate(outs):
-            pltpu.make_async_copy(res.at[pl.ds(i * ROWS, ROWS), cols], o.at[:, cols], out_sem).start()
-
-    pltpu.make_async_copy(res, res, out_sem).wait()
+            o[:, cols] = part[i * ROWS : (i + 1) * ROWS]
 
 
 def layer(blocks, wq, wkv, wo, cos, sin, allow):
@@ -206,18 +229,16 @@
         layer_kernel,
         out_shape=[jax.ShapeDtypeStruct((ROWS, WIDTH), BF16)] * 8,
         in_specs=[hbm] * 11 + [vmem] * 3,
-        out_specs=[hbm] * 8,
+        out_specs=[vmem] * 8,
         scratch_shapes=[
             pltpu.VMEM((2 * MB, WIDTH), BF16),
             pltpu.VMEM((WIDTH, QKV), BF16),
             pltpu.VMEM((HEADS * HEAD, WIDTH), BF16),
             pltpu.VMEM((2 * MB, QKV), F32),
             pltpu.VMEM((2 * MB, HEADS * HEAD), BF16),
-            pltpu.VMEM((2 * MB, WIDTH), BF16),
             pltpu.SemaphoreType.DMA,
             pltpu.SemaphoreType.DMA((WIDTH // KC,)),
             pltpu.SemaphoreType.DMA((WIDTH // NC,)),
-            pltpu.SemaphoreType.DMA,
         ],
         compiler_params=pltpu.CompilerParams(vmem_limit_bytes=48 * 1024 * 1024),
         cost_estimate=pl.CostEstimate(flops=6 * 10**9, bytes_accessed=28 * 2**20, transcendentals=0),
@@ -312,7 +333,7 @@
     core, x, z = section % 2, rank // NZ, rank % NZ
     my_rows = section_input[0]
     normed = rms_norm(my_rows, attn_gain[0])
-    other_vocab = over_section(w_vocab, [(s, s + 1) for s in range(0, 16, 2)])
+    other_vocab = over_section(w_vocab, [(s, s ^ 1) for s in range(16)])
 
     zs = (z + jnp.arange(NZ)) % NZ
 
@@ -336,8 +357,10 @@
     blank = jnp.zeros((ROWS, WIDTH), BF16)
     weights = (w_query[0], w_keyval[0].reshape(WIDTH, -1), w_out_proj[0])
     blocks, angles = lax.cond(
-        odd, lambda: (gather_rows(normed), tables()), lambda: ((blank,) * 8, tables())
+        odd, lambda: (gather_rows(normed)[1:], tables()), lambda: ((blank,) * 7, tables())
     )
+    blocks = (normed, *blocks)
+
     def layer_rows(blocks):
         return finish(my_rows, scatter_sum(layer(blocks, *weights, *angles)), final_gain)
 
@@ -350,11 +373,11 @@
         inside = (local >= 0) & (local < VL)
         want = jnp.max(jnp.where(inside, local + jnp.arange(2)[None, :] * VL, -1), axis=1)
         want = jnp.broadcast_to(want[:, None], (2 * MB, 128))
-        all_rows = gather_rows(spread_from_last(final_rows, section))
+        all_rows = gather_rows_split(spread_from_last(final_rows, section))
         return layer_out, vocab(order, all_rows, w_vocab, other_vocab, want)
 
     def even_path():
-        return layer_rows(gather_rows(normed))[0], jnp.zeros((128, 128), F32)
+        return layer_rows(gather_pairs(normed))[0], jnp.zeros((128, 128), F32)
 
     layer_out, stats = lax.cond(odd, odd_path, even_path)
     handed = over_section(layer_out, [(s, s + 1) for s in range(15)])[None]

time: 156 us -> 150 us (0.962)
  waiting for transfers between devices: 73.6 us -> 64 us
  starting transfers between devices: 31.6 us -> 36.6 us
    ppermute x22 -> x23, waiting for transfers between devices: 54.7 us -> 43.7 us  [over_tensor(): return lax.ppermute(block, 'tensor', pairs)]
    ppermute x22 -> x23, starting transfers between devices: 25 us -> 29.8 us  [over_tensor(): return lax.ppermute(block, 'tensor', pairs)]
  transfers between devices with their start and end apart: 28 -> 29, of which waited for: 13 -> 14; matrix products, arithmetic and copies ran while one was open for 4% -> 4% of each run, Pallas kernels for 2% -> 2%
where the time goes in v4:
time: 150 us; the launch traced here: 149 us
  waiting for transfers between devices  64 us (43%)
  starting transfers between devices  36.6 us (24%)
  Pallas kernels  21.2 us (14%)
  blocking collectives  19.6 us (13%)
  other arithmetic  3.55 us (2%)
  local copies, waits for them, and re-layouts  3.25 us (2%)
    ppermute x23, waiting for transfers between devices, over_tensor(): return lax.ppermute(block, 'tensor', pairs)  43.7 us
    ppermute x23, starting transfers between devices, over_tensor(): return lax.ppermute(block, 'tensor', pairs)  29.8 us
    ppermute x1, waiting for transfers between devices, spread_from_last(): lax.ppermute(rows, ('section', 'tensor'), here)  20.3 us
    all_to_all x1, blocking collectives, body(): got = lax.all_to_all(stats, ('section', 'tensor'), 0, 0, tiled=True)  19.6 us
    pallas_call x1, Pallas kernels, layer(): pl.pallas_call(layer_kernel, out_shape=[jax.ShapeDtypeStruct((ROWS, WIDTH...  10.8 us
    pallas_call x1, Pallas kernels, vocab(): pl.pallas_call(vocab_kernel, out_shape=jax.ShapeDtypeStruct((128, 128), F...  6.15 us
    ppermute x5, starting transfers between devices, over_section(): return lax.ppermute(block, 'section', pairs)  5.49 us
  transfers between devices with their start and end apart: 29, of which 14 were waited for; matrix products, arithmetic and copies ran while one was open for 4% of the time, Pallas kernels for 2%

profile of v4, /device:TPU:1, one launch (start us, length us, event | category | flops | bytes accessed | tf_op | source)
XLA Modules:
  0.0 149.4 jit_solution(8652546601429671818)
XLA Ops:
  0.7 1.5 %collective-permute-start.41 = (bf16[8192,256]{1,0:T(8,128)(2,1)}, bf16[8192,256]{1,0:T(8,128)(2,1)}, u32[]{:S(2)}, u32[]{:S(2)}) collective-permute-start(bf16[8192,256]{1,0:T(8,128)(2,1)} %param.22), channel_id=1, source_target_pairs={{0,8},{8,0},{16,24},{24,16},{32,40},{40,32},{48,56},{56,48},{64,72... | collective-permute-start | bytes 12582920 | tf_op jit(solution)/shard_map/ppermute | solution.py:47
  2.2 1.4 norm.1
  3.6 28.7 %conditional.6 = (bf16[32,8192]{1,0:T(8,128)(2,1)}, bf16[32,8192]{1,0:T(8,128)(2,1)}, bf16[32,8192]{1,0:T(8,128)(2,1)}, bf16[32,8192]{1,0:T(8,128)(2,1)}, bf16[3...) conditional(s32[]{:T(128)} %convert_element_type.122, ...), branch_computations={%region_0.2_spmd, %region_1.3_spmd} | conditional | flops 231513 | bytes 15493352
  3.6 1.8 %collective-permute-start.35 = (bf16[32,8192]{1,0:T(8,128)(2,1)S(1)}, bf16[32,8192]{1,0:T(8,128)(2,1)}, u32[]{:S(2)}, u32[]{:S(2)}) collective-permute-start(bf16[32,8192]{1,0:T(8,128)(2,1)S(1)} %get-tuple-element.106), channel_id=1, source_target_pairs={{0,1},{1,2},{2,3},{3,0},{4,5},{5,6},{6,7},{7,4},{8,9},{9,10},{10,1... | collective-permute-start | bytes 1572872 | tf_op jit(solution)/shard_map/cond/branch_1_fun/ppermute | solution.py:43
  6.6 2.2 %collective-permute-start.34 = (bf16[32,8192]{1,0:T(8,128)(2,1)S(1)}, bf16[32,8192]{1,0:T(8,128)(2,1)}, u32[]{:S(2)}, u32[]{:S(2)}) collective-permute-start(bf16[32,8192]{1,0:T(8,128)(2,1)S(1)} %get-tuple-element.106), channel_id=1, source_target_pairs={{0,3},{1,0},{2,1},{3,2},{4,7},{5,4},{6,5},{7,6},{8,11},{9,8},{10,9... | collective-permute-start | bytes 1572872 | tf_op jit(solution)/shard_map/cond/branch_1_fun/ppermute | solution.py:43
  11.9 2.3 %collective-permute-done.35 = bf16[32,8192]{1,0:T(8,128)(2,1)} collective-permute-done((bf16[32,8192]{1,0:T(8,128)(2,1)S(1)}, bf16[32,8192]{1,0:T(8,128)(2,1)}, u32[]{:S(2)}, u32[]{:S(2)}) %collective-permute-start.35) | collective-permute-done | bytes 524320 | tf_op jit(solution)/shard_map/cond/branch_1_fun/ppermute | solution.py:43
  14.3 2.7 %collective-permute-start.38 = (bf16[32,8192]{1,0:T(8,128)(2,1)}, bf16[32,8192]{1,0:T(8,128)(2,1)}, u32[]{:S(2)}, u32[]{:S(2)}) collective-permute-start(bf16[32,8192]{1,0:T(8,128)(2,1)} %collective-permute-done.37), channel_id=1, source_target_pairs={{0,3},{1,0},{2,1},{3,2},{4,7},{5,4},{6,5},{7,6},{8,11},{9,8},{10,9... | collective-permute-start | bytes 1572872 | tf_op jit(solution)/shard_map/cond/branch_1_fun/ppermute | solution.py:43
  17.0 6.8 %collective-permute-done.36 = bf16[32,8192]{1,0:T(8,128)(2,1)} collective-permute-done((bf16[32,8192]{1,0:T(8,128)(2,1)}, bf16[32,8192]{1,0:T(8,128)(2,1)}, u32[]{:S(2)}, u32[]{:S(2)}) %collective-permute-start.36) | collective-permute-done | bytes 524320 | tf_op jit(solution)/shard_map/cond/branch_1_fun/ppermute | solution.py:43
  25.8 5.0 %collective-permute-done.40 = bf16[32,8192]{1,0:T(8,128)(2,1)} collective-permute-done((bf16[32,8192]{1,0:T(8,128)(2,1)}, bf16[32,8192]{1,0:T(8,128)(2,1)}, u32[]{:S(2)}, u32[]{:S(2)}) %collective-permute-start.40) | collective-permute-done | bytes 524320 | tf_op jit(solution)/shard_map/cond/branch_1_fun/ppermute | solution.py:43
  30.8 1.5 %collective-permute-done.39 = bf16[32,8192]{1,0:T(8,128)(2,1)} collective-permute-done((bf16[32,8192]{1,0:T(8,128)(2,1)}, bf16[32,8192]{1,0:T(8,128)(2,1)}, u32[]{:S(2)}, u32[]{:S(2)}) %collective-permute-start.39) | collective-permute-done | bytes 524320 | tf_op jit(solution)/shard_map/cond/branch_1_fun/ppermute | solution.py:43
  32.3 93.2 %conditional.5 = (bf16[32,8192]{1,0:T(8,128)(2,1)}, f32[128,128]{1,0:T(8,128)}) conditional(s32[]{:T(128)} %convert_element_type.122, (bf16[32,8192]{1,0:T(8,128)(2,1)S(1)}, bf16[8192,512]{1,0:T(8,128)(2,1)}, bf16[8192,256]{1,0:T(8,128)(2,1)}, bf16[512,8192]{1,0:T(8,128)(2,1)}, f32[256,128]{1,0:T(8,128)S(1)}, /*index=5*/f32[256,128]{1,0:T(8,128)S(1)}, ...), branch_computations={%region_2.4_spmd, %region_3.6_spmd} | conditional | flops 8006819840 | bytes 113345168 | solution.py:382
  32.5 10.8 %layer.3 = (bf16[32,8192]{1,0:T(8,128)(2,1)S(1)}, bf16[32,8192]{1,0:T(8,128)(2,1)S(1)}, bf16[32,8192]{1,0:T(8,128)(2,1)S(1)}, bf16[32,8192]{1,0:T(8,128)(2,1)S(1...) custom-call(bf16[32,8192]{1,0:T(8,128)(2,1)S(1)} %get-tuple-element., ...), custom_call_target="tpu_custom_call" | custom-call | flops 6000000000 | bytes 29360128 | tf_op jit(solution)/shard_map/cond/branch_1_fun/layer/pallas_call | solution.py:228
  44.7 2.7 %collective-permute-start.1 = (bf16[32,8192]{1,0:T(8,128)(2,1)S(1)}, bf16[32,8192]{1,0:T(8,128)(2,1)S(1)}, u32[]{:S(2)}, u32[]{:S(2)}) collective-permute-start(bf16[32,8192]{1,0:T(8,128)(2,1)S(1)} %get-tuple-element.146), channel_id=1, source_target_pairs={{0,3},{1,0},{2,1},{3,2},{4,7},{5,4},{6,5},{7,6},{8,11},{9,8},{10,9... | collective-permute-start | bytes 1572872 | tf_op jit(solution)/shard_map/cond/branch_1_fun/ppermute | solution.py:43
  47.4 4.1 %collective-permute-done.3 = bf16[32,8192]{1,0:T(8,128)(2,1)S(1)} collective-permute-done((bf16[32,8192]{1,0:T(8,128)(2,1)S(1)}, bf16[32,8192]{1,0:T(8,128)(2,1)S(1)}, u32[]{:S(2)}, u32[]{:S(2)}) %collective-permute-start.3) | collective-permute-done | bytes 524320 | tf_op jit(solution)/shard_map/cond/branch_1_fun/ppermute | solution.py:43
  51.7 2.7 %collective-permute-start.4 = (bf16[16,8192]{1,0:T(8,128)(2,1)S(1)}, bf16[16,8192]{1,0:T(8,128)(2,1)S(1)}, u32[]{:S(2)}, u32[]{:S(2)}) collective-permute-start(bf16[16,8192]{1,0:T(8,128)(2,1)S(1)} %get-tuple-element.208), channel_id=1, source_target_pairs={{0,3},{1,0},{2,1},{3,2},{4,7},{5,4},{6,5},{7,6},{8,11},{9,8},{10,9... | collective-permute-start | bytes 786440 | tf_op jit(solution)/shard_map/cond/branch_1_fun/ppermute | solution.py:43
  55.8 2.3 %collective-permute-done.6 = bf16[16,8192]{1,0:T(8,128)(2,1)S(1)} collective-permute-done((bf16[16,8192]{1,0:T(8,128)(2,1)S(1)}, bf16[16,8192]{1,0:T(8,128)(2,1)S(1)}, u32[]{:S(2)}, u32[]{:S(2)}) %collective-permute-start.6) | collective-permute-done | bytes 262176 | tf_op jit(solution)/shard_map/cond/branch_1_fun/ppermute | solution.py:43
  58.4 2.7 %collective-permute-start.5 = (bf16[32,8192]{1,0:T(8,128)(2,1)S(1)}, bf16[32,8192]{1,0:T(8,128)(2,1)S(1)}, u32[]{:S(2)}, u32[]{:S(2)}) collective-permute-start(bf16[32,8192]{1,0:T(8,128)(2,1)S(1)} %pad_maximum_fusion.2), channel_id=1, source_target_pairs={{0,3},{1,0},{2,1},{3,2},{4,7},{5,4},{6,5},{7,6},{8,11},{9,8},{10,9... | collective-permute-start | bytes 1572872 | tf_op jit(solution)/shard_map/cond/branch_1_fun/ppermute | solution.py:43
  61.2 2.2 %collective-permute-done.2.b_ref = bf16[32,8192]{1,0:T(8,128)(2,1)S(1)} collective-permute-done((bf16[32,8192]{1,0:T(8,128)(2,1)S(1)}, bf16[32,8192]{1,0:T(8,128)(2,1)S(1)}, u32[]{:S(2)}, u32[]{:S(2)}) %collective-permute-start.2) | collective-permute-done | bytes 524320 | tf_op jit(solution)/shard_map/cond/branch_1_fun/ppermute | solution.py:43
  63.4 4.2 %collective-permute-done.7.d_ref = bf16[32,8192]{1,0:T(8,128)(2,1)S(1)} collective-permute-done((bf16[32,8192]{1,0:T(8,128)(2,1)S(1)}, bf16[32,8192]{1,0:T(8,128)(2,1)S(1)}, u32[]{:S(2)}, u32[]{:S(2)}) %collective-permute-start.7) | collective-permute-done | bytes 524320 | tf_op jit(solution)/shard_map/cond/branch_1_fun/ppermute | solution.py:43
  72.3 20.3 %collective-permute-done.11 = bf16[32,8192]{1,0:T(8,128)(2,1)S(1)} collective-permute-done((bf16[32,8192]{1,0:T(8,128)(2,1)S(1)}, bf16[32,8192]{1,0:T(8,128)(2,1)S(1)}, u32[]{:S(2)}, u32[]{:S(2)}) %collective-permute-start.11) | collective-permute-done | bytes 524320 | tf_op jit(solution)/shard_map/cond/branch_1_fun/ppermute | solution.py:326
  92.8 2.9 %collective-permute-start.12 = (bf16[32,8192]{1,0:T(8,128)(2,1)S(1)}, bf16[32,8192]{1,0:T(8,128)(2,1)S(1)}, u32[]{:S(2)}, u32[]{:S(2)}) collective-permute-start(bf16[32,8192]{1,0:T(8,128)(2,1)S(1)} %broadcast_select_fusion.refs_0_), channel_id=1, source_target_pairs={{0,3},{1,0},{2,1},{3,2},{4,7},{5,4},{6,5},{7,6},{8,11},{9,8},{10,9... | collective-permute-start | bytes 1572872 | tf_op jit(solution)/shard_map/cond/branch_1_fun/ppermute | solution.py:43
  96.4 7.8 %collective-permute-done.13.refs_3_ = bf16[32,8192]{1,0:T(8,128)(2,1)S(1)} collective-permute-done((bf16[32,8192]{1,0:T(8,128)(2,1)S(1)}, bf16[32,8192]{1,0:T(8,128)(2,1)S(1)}, u32[]{:S(2)}, u32[]{:S(2)}) %collective-permute-start.13) | collective-permute-done | bytes 524320 | tf_op jit(solution)/shard_map/cond/branch_1_fun/ppermute | solution.py:43
  104.4 3.0 %collective-permute-start.15 = (bf16[16,8192]{1,0:T(8,128)(2,1)S(1)}, bf16[16,8192]{1,0:T(8,128)(2,1)S(1)}, u32[]{:S(2)}, u32[]{:S(2)}) collective-permute-start(bf16[16,8192]{1,0:T(8,128)(2,1)S(1)} %slice.89), channel_id=1, source_target_pairs={{0,3},{1,0},{2,1},{3,2},{4,7},{5,4},{6,5},{7,6},{8,11},{9,8},{10,9... | collective-permute-start | bytes 786440 | tf_op jit(solution)/shard_map/cond/branch_1_fun/ppermute | solution.py:43
  107.5 1.4 collective-permute-start.19
  108.8 1.8 %collective-permute-done.14 = bf16[16,8192]{1,0:T(8,128)(2,1)S(1)} collective-permute-done((bf16[16,8192]{1,0:T(8,128)(2,1)S(1)}, bf16[16,8192]{1,0:T(8,128)(2,1)S(1)}, u32[]{:S(2)}, u32[]{:S(2)}) %collective-permute-start.14) | collective-permute-done | bytes 262176 | tf_op jit(solution)/shard_map/cond/branch_1_fun/ppermute | solution.py:43
  110.7 1.8 %collective-permute-start.18 = (bf16[32,8192]{1,0:T(8,128)(2,1)S(1)}, bf16[32,8192]{1,0:T(8,128)(2,1)}, u32[]{:S(2)}, u32[]{:S(2)}) collective-permute-start(bf16[32,8192]{1,0:T(8,128)(2,1)S(1)} %constant_dynamic-update-slice_fusion.4.refs_2_), channel_id=1, source_target_pairs={{0,4},{1,5},{2,6},{3,7},{4,0},{5,1},{6,2},{7,3},{8,12},{9,13},{10,... | collective-permute-start | bytes 1572872 | tf_op jit(solution)/shard_map/cond/branch_1_fun/ppermute | solution.py:43
  113.4 2.9 %collective-permute-done.17.refs_5_ = bf16[32,8192]{1,0:T(8,128)(2,1)S(1)} collective-permute-done((bf16[32,8192]{1,0:T(8,128)(2,1)S(1)}, bf16[32,8192]{1,0:T(8,128)(2,1)S(1)}, u32[]{:S(2)}, u32[]{:S(2)}) %collective-permute-start.17) | collective-permute-done | bytes 524320 | tf_op jit(solution)/shard_map/cond/branch_1_fun/ppermute | solution.py:43
  116.8 2.4 %collective-permute-done.18.refs_6_ = bf16[32,8192]{1,0:T(8,128)(2,1)} collective-permute-done((bf16[32,8192]{1,0:T(8,128)(2,1)S(1)}, bf16[32,8192]{1,0:T(8,128)(2,1)}, u32[]{:S(2)}, u32[]{:S(2)}) %collective-permute-start.18) | collective-permute-done | bytes 524320 | tf_op jit(solution)/shard_map/cond/branch_1_fun/ppermute | solution.py:43
  119.3 6.1 %vocab.1 = f32[128,128]{1,0:T(8,128)} custom-call(s32[8]{0:T(128)S(1)} %add.172.order_ref, bf16[32,8192]{1,0:T(8,128)(2,1)S(1)} %broadcast_select_fusion.refs_0_, bf16[32,8192]{1,0:T(8,128)(2,1)S(1)} %collective-permute-done.12.refs_1_, bf16[32,8192]{1,0:T(8,128)(2,1)S(1)} %constant_dynamic-update-slice_fusion.4.refs_2_, ...), custom_call_target="tpu_custom_call" | custom-call | flops 2000000000 | bytes 14680064 | tf_op jit(solution)/shard_map/cond/branch_1_fun/vocab/pallas_call | solution.py:292
  125.5 1.9 %collective-permute-start.42 = (bf16[32,8192]{1,0:T(8,128)(2,1)}, bf16[32,8192]{1,0:T(8,128)(2,1)S(1)}, u32[]{:S(2)}, u32[]{:S(2)}) collective-permute-start(bf16[32,8192]{1,0:T(8,128)(2,1)} %get-tuple-element.185), channel_id=1, source_target_pairs={{0,8},{8,16},{16,24},{24,32},{32,40},{40,48},{48,56},{56,64},{64,7... | collective-permute-start | bytes 1572872 | tf_op jit(solution)/shard_map/ppermute | solution.py:47
  127.4 19.6 %all_to_all.11 = f32[128,1,128]{2,1,0:T(1,128)} all-to-all(f32[128,1,128]{2,1,0:T(1,128)} %bitcast.13), channel_id=1, replica_groups=mesh['section'=16,'tensor'=8] {'section','tensor'}, dimensions={0} | all-to-all | bytes 131072 | tf_op jit(solution)/shard_map/all_to_all | solution.py:384
  147.0 1.6 %merge.1 = f32[32]{0:T(128)} custom-call(f32[128,128]{1,0:T(8,128)} %bitcast.25), custom_call_target="tpu_custom_call" | custom-call | tf_op jit(solution)/shard_map/merge/pallas_call | solution.py:151
  (93 shorter events, 17.8 us)
Async XLA Ops:
  0.6 31.7 %copy-start.1 = (bf16[1,32,8192]{2,1,0:T(8,128)(2,1)S(1)}, bf16[1,32,8192]{2,1,0:T(8,128)(2,1)}, u32[]{:S(2)}) copy-start(bf16[1,32,8192]{2,1,0:T(8,128)(2,1)} %param.15) | copy-start | bytes 1572868
  0.6 31.7 %copy-start.4 = (bf16[8192]{0:T(1024)(128)(2,1)S(1)}, bf16[8192]{0:T(1024)(128)(2,1)}, u32[]{:S(2)}) copy-start(bf16[8192]{0:T(1024)(128)(2,1)} %param.21) | copy-start | bytes 49156
  0.7 31.7 %copy-start.5 = (s32[256]{0:T(256)S(1)}, s32[256]{0:T(256)}, u32[]{:S(2)}) copy-start(s32[256]{0:T(256)} %param.23) | copy-start | bytes 3076
  0.7 31.6 %collective-permute-start.41 = (bf16[8192,256]{1,0:T(8,128)(2,1)}, bf16[8192,256]{1,0:T(8,128)(2,1)}, u32[]{:S(2)}, u32[]{:S(2)}) collective-permute-start(bf16[8192,256]{1,0:T(8,128)(2,1)} %param.22), channel_id=1, source_target_pairs={{0,8},{8,0},{16,24},{24,16},{32,40},{40,32},{48,56},{56,48},{64,72... | collective-permute-start | bytes 12582920 | tf_op jit(solution)/shard_map/ppermute | solution.py:47
  3.6 10.6 %collective-permute-start.35 = (bf16[32,8192]{1,0:T(8,128)(2,1)S(1)}, bf16[32,8192]{1,0:T(8,128)(2,1)}, u32[]{:S(2)}, u32[]{:S(2)}) collective-permute-start(bf16[32,8192]{1,0:T(8,128)(2,1)S(1)} %get-tuple-element.106), channel_id=1, source_target_pairs={{0,1},{1,2},{2,3},{3,0},{4,5},{5,6},{6,7},{7,4},{8,9},{9,10},{10,1... | collective-permute-start | bytes 1572872 | tf_op jit(solution)/shard_map/cond/branch_1_fun/ppermute | solution.py:43
  5.4 8.9 %collective-permute-start.37 = (bf16[32,8192]{1,0:T(8,128)(2,1)S(1)}, bf16[32,8192]{1,0:T(8,128)(2,1)}, u32[]{:S(2)}, u32[]{:S(2)}) collective-permute-start(bf16[32,8192]{1,0:T(8,128)(2,1)S(1)} %get-tuple-element.106), channel_id=1, source_target_pairs={{0,4},{1,5},{2,6},{3,7},{4,0},{5,1},{6,2},{7,3},{8,12},{9,13},{10,... | collective-permute-start | bytes 1572872 | tf_op jit(solution)/shard_map/cond/branch_1_fun/ppermute | solution.py:43
  6.6 19.2 %collective-permute-start.34 = (bf16[32,8192]{1,0:T(8,128)(2,1)S(1)}, bf16[32,8192]{1,0:T(8,128)(2,1)}, u32[]{:S(2)}, u32[]{:S(2)}) collective-permute-start(bf16[32,8192]{1,0:T(8,128)(2,1)S(1)} %get-tuple-element.106), channel_id=1, source_target_pairs={{0,3},{1,0},{2,1},{3,2},{4,7},{5,4},{6,5},{7,6},{8,11},{9,8},{10,9... | collective-permute-start | bytes 1572872 | tf_op jit(solution)/shard_map/cond/branch_1_fun/ppermute | solution.py:43
  14.2 9.6 %collective-permute-start.36 = (bf16[32,8192]{1,0:T(8,128)(2,1)}, bf16[32,8192]{1,0:T(8,128)(2,1)}, u32[]{:S(2)}, u32[]{:S(2)}) collective-permute-start(bf16[32,8192]{1,0:T(8,128)(2,1)} %collective-permute-done.35), channel_id=1, source_target_pairs={{0,1},{1,2},{2,3},{3,0},{4,5},{5,6},{6,7},{7,4},{8,9},{9,10},{10,1... | collective-permute-start | bytes 1572872 | tf_op jit(solution)/shard_map/cond/branch_1_fun/ppermute | solution.py:43
  14.3 11.5 %collective-permute-start.38 = (bf16[32,8192]{1,0:T(8,128)(2,1)}, bf16[32,8192]{1,0:T(8,128)(2,1)}, u32[]{:S(2)}, u32[]{:S(2)}) collective-permute-start(bf16[32,8192]{1,0:T(8,128)(2,1)} %collective-permute-done.37), channel_id=1, source_target_pairs={{0,3},{1,0},{2,1},{3,2},{4,7},{5,4},{6,5},{7,6},{8,11},{9,8},{10,9... | collective-permute-start | bytes 1572872 | tf_op jit(solution)/shard_map/cond/branch_1_fun/ppermute | solution.py:43
  17.0 13.8 %collective-permute-start.40 = (bf16[32,8192]{1,0:T(8,128)(2,1)}, bf16[32,8192]{1,0:T(8,128)(2,1)}, u32[]{:S(2)}, u32[]{:S(2)}) collective-permute-start(bf16[32,8192]{1,0:T(8,128)(2,1)} %collective-permute-done.37), channel_id=1, source_target_pairs={{0,1},{1,2},{2,3},{3,0},{4,5},{5,6},{6,7},{7,4},{8,9},{9,10},{10,1... | collective-permute-start | bytes 1572872 | tf_op jit(solution)/shard_map/cond/branch_1_fun/ppermute | solution.py:43
  23.8 8.5 %collective-permute-start.39 = (bf16[32,8192]{1,0:T(8,128)(2,1)}, bf16[32,8192]{1,0:T(8,128)(2,1)}, u32[]{:S(2)}, u32[]{:S(2)}) collective-permute-start(bf16[32,8192]{1,0:T(8,128)(2,1)} %collective-permute-done.36), channel_id=1, source_target_pairs={{0,4},{1,5},{2,6},{3,7},{4,0},{5,1},{6,2},{7,3},{8,12},{9,13},{10,... | collective-permute-start | bytes 1572872 | tf_op jit(solution)/shard_map/cond/branch_1_fun/ppermute | solution.py:43
  43.4 8.1 %collective-permute-start.3 = (bf16[32,8192]{1,0:T(8,128)(2,1)S(1)}, bf16[32,8192]{1,0:T(8,128)(2,1)S(1)}, u32[]{:S(2)}, u32[]{:S(2)}) collective-permute-start(bf16[32,8192]{1,0:T(8,128)(2,1)S(1)} %get-tuple-element.149), channel_id=1, source_target_pairs={{0,4},{1,5},{2,6},{3,7},{4,0},{5,1},{6,2},{7,3},{8,12},{9,13},{10,... | collective-permute-start | bytes 1572872 | tf_op jit(solution)/shard_map/cond/branch_1_fun/ppermute | solution.py:43
  44.7 9.7 %collective-permute-start = (bf16[32,8192]{1,0:T(8,128)(2,1)S(1)}, bf16[32,8192]{1,0:T(8,128)(2,1)S(1)}, u32[]{:S(2)}, u32[]{:S(2)}) collective-permute-start(bf16[32,8192]{1,0:T(8,128)(2,1)S(1)} %get-tuple-element.145), channel_id=1, source_target_pairs={{0,1},{1,2},{2,3},{3,0},{4,5},{5,6},{6,7},{7,4},{8,9},{9,10},{10,1... | collective-permute-start | bytes 1572872 | tf_op jit(solution)/shard_map/cond/branch_1_fun/ppermute | solution.py:43
  44.7 9.7 %collective-permute-start.1 = (bf16[32,8192]{1,0:T(8,128)(2,1)S(1)}, bf16[32,8192]{1,0:T(8,128)(2,1)S(1)}, u32[]{:S(2)}, u32[]{:S(2)}) collective-permute-start(bf16[32,8192]{1,0:T(8,128)(2,1)S(1)} %get-tuple-element.146), channel_id=1, source_target_pairs={{0,3},{1,0},{2,1},{3,2},{4,7},{5,4},{6,5},{7,6},{8,11},{9,8},{10,9... | collective-permute-start | bytes 1572872 | tf_op jit(solution)/shard_map/cond/branch_1_fun/ppermute | solution.py:43
  51.6 6.5 %collective-permute-start.6 = (bf16[16,8192]{1,0:T(8,128)(2,1)S(1)}, bf16[16,8192]{1,0:T(8,128)(2,1)S(1)}, u32[]{:S(2)}, u32[]{:S(2)}) collective-permute-start(bf16[16,8192]{1,0:T(8,128)(2,1)S(1)} %get-tuple-element.207), channel_id=1, source_target_pairs={{0,1},{1,2},{2,3},{3,0},{4,5},{5,6},{6,7},{7,4},{8,9},{9,10},{10,1... | collective-permute-start | bytes 786440 | tf_op jit(solution)/shard_map/cond/branch_1_fun/ppermute | solution.py:43
  51.7 6.6 %collective-permute-start.4 = (bf16[16,8192]{1,0:T(8,128)(2,1)S(1)}, bf16[16,8192]{1,0:T(8,128)(2,1)S(1)}, u32[]{:S(2)}, u32[]{:S(2)}) collective-permute-start(bf16[16,8192]{1,0:T(8,128)(2,1)S(1)} %get-tuple-element.208), channel_id=1, source_target_pairs={{0,3},{1,0},{2,1},{3,2},{4,7},{5,4},{6,5},{7,6},{8,11},{9,8},{10,9... | collective-permute-start | bytes 786440 | tf_op jit(solution)/shard_map/cond/branch_1_fun/ppermute | solution.py:43
  54.6 8.8 %collective-permute-start.2 = (bf16[32,8192]{1,0:T(8,128)(2,1)S(1)}, bf16[32,8192]{1,0:T(8,128)(2,1)S(1)}, u32[]{:S(2)}, u32[]{:S(2)}) collective-permute-start(bf16[32,8192]{1,0:T(8,128)(2,1)S(1)} %add_convert_fusion.5), channel_id=1, source_target_pairs={{0,4},{1,5},{2,6},{3,7},{4,0},{5,1},{6,2},{7,3},{8,12},{9,13},{10,... | collective-permute-start | bytes 1572872 | tf_op jit(solution)/shard_map/cond/branch_1_fun/ppermute | solution.py:43
  58.2 9.3 %collective-permute-start.7 = (bf16[32,8192]{1,0:T(8,128)(2,1)S(1)}, bf16[32,8192]{1,0:T(8,128)(2,1)S(1)}, u32[]{:S(2)}, u32[]{:S(2)}) collective-permute-start(bf16[32,8192]{1,0:T(8,128)(2,1)S(1)} %pad_maximum_fusion.3), channel_id=1, source_target_pairs={{0,1},{1,2},{2,3},{3,0},{4,5},{5,6},{6,7},{7,4},{8,9},{9,10},{10,1... | collective-permute-start | bytes 1572872 | tf_op jit(solution)/shard_map/cond/branch_1_fun/ppermute | solution.py:43
  58.4 9.1 %collective-permute-start.5 = (bf16[32,8192]{1,0:T(8,128)(2,1)S(1)}, bf16[32,8192]{1,0:T(8,128)(2,1)S(1)}, u32[]{:S(2)}, u32[]{:S(2)}) collective-permute-start(bf16[32,8192]{1,0:T(8,128)(2,1)S(1)} %pad_maximum_fusion.2), channel_id=1, source_target_pairs={{0,3},{1,0},{2,1},{3,2},{4,7},{5,4},{6,5},{7,6},{8,11},{9,8},{10,9... | collective-permute-start | bytes 1572872 | tf_op jit(solution)/shard_map/cond/branch_1_fun/ppermute | solution.py:43
  68.7 2.1 %collective-permute-start.10 = (bf16[32,8192]{1,0:T(8,128)(2,1)S(1)}, bf16[32,8192]{1,0:T(8,128)(2,1)S(1)}, u32[]{:S(2)}, u32[]{:S(2)}) collective-permute-start(bf16[32,8192]{1,0:T(8,128)(2,1)S(1)} %get-tuple-element.156), channel_id=1, source_target_pairs={{120,56},{121,57},{122,58},{123,59},{124,60},{125,61},{126,62},{12... | collective-permute-start | bytes 1572872 | tf_op jit(solution)/shard_map/cond/branch_1_fun/ppermute | solution.py:47
  69.4 1.4 collective-permute-start.8
  70.1 0.7 collective-permute-start.9
  71.0 21.6 %collective-permute-start.11 = (bf16[32,8192]{1,0:T(8,128)(2,1)S(1)}, bf16[32,8192]{1,0:T(8,128)(2,1)S(1)}, u32[]{:S(2)}, u32[]{:S(2)}) collective-permute-start(bf16[32,8192]{1,0:T(8,128)(2,1)S(1)} %select_select_fusion), channel_id=1, source_target_pairs={{24,12},{25,13},{26,14},{27,15},{28,8},{29,9},{30,10},{31,11},{56,... | collective-permute-start | bytes 1572872 | tf_op jit(solution)/shard_map/cond/branch_1_fun/ppermute | solution.py:326
  92.7 11.5 %collective-permute-start.13 = (bf16[32,8192]{1,0:T(8,128)(2,1)S(1)}, bf16[32,8192]{1,0:T(8,128)(2,1)S(1)}, u32[]{:S(2)}, u32[]{:S(2)}) collective-permute-start(bf16[32,8192]{1,0:T(8,128)(2,1)S(1)} %broadcast_select_fusion.refs_0_), channel_id=1, source_target_pairs={{0,1},{1,2},{2,3},{3,0},{4,5},{5,6},{6,7},{7,4},{8,9},{9,10},{10,1... | collective-permute-start | bytes 1572872 | tf_op jit(solution)/shard_map/cond/branch_1_fun/ppermute | solution.py:43
  92.8 11.5 %collective-permute-start.12 = (bf16[32,8192]{1,0:T(8,128)(2,1)S(1)}, bf16[32,8192]{1,0:T(8,128)(2,1)S(1)}, u32[]{:S(2)}, u32[]{:S(2)}) collective-permute-start(bf16[32,8192]{1,0:T(8,128)(2,1)S(1)} %broadcast_select_fusion.refs_0_), channel_id=1, source_target_pairs={{0,3},{1,0},{2,1},{3,2},{4,7},{5,4},{6,5},{7,6},{8,11},{9,8},{10,9... | collective-permute-start | bytes 1572872 | tf_op jit(solution)/shard_map/cond/branch_1_fun/ppermute | solution.py:43
  95.7 11.7 %collective-permute-start.16 = (bf16[32,8192]{1,0:T(8,128)(2,1)S(1)}, bf16[32,8192]{1,0:T(8,128)(2,1)S(1)}, u32[]{:S(2)}, u32[]{:S(2)}) collective-permute-start(bf16[32,8192]{1,0:T(8,128)(2,1)S(1)} %broadcast_select_fusion.refs_0_), channel_id=1, source_target_pairs={{0,4},{1,5},{2,6},{3,7},{4,0},{5,1},{6,2},{7,3},{8,12},{9,13},{10,... | collective-permute-start | bytes 1572872 | tf_op jit(solution)/shard_map/cond/branch_1_fun/ppermute | solution.py:43
  104.2 6.5 %collective-permute-start.14 = (bf16[16,8192]{1,0:T(8,128)(2,1)S(1)}, bf16[16,8192]{1,0:T(8,128)(2,1)S(1)}, u32[]{:S(2)}, u32[]{:S(2)}) collective-permute-start(bf16[16,8192]{1,0:T(8,128)(2,1)S(1)} %slice.88), channel_id=1, source_target_pairs={{0,1},{1,2},{2,3},{3,0},{4,5},{5,6},{6,7},{7,4},{8,9},{9,10},{10,1... | collective-permute-start | bytes 786440 | tf_op jit(solution)/shard_map/cond/branch_1_fun/ppermute | solution.py:43
  104.4 6.3 %collective-permute-start.15 = (bf16[16,8192]{1,0:T(8,128)(2,1)S(1)}, bf16[16,8192]{1,0:T(8,128)(2,1)S(1)}, u32[]{:S(2)}, u32[]{:S(2)}) collective-permute-start(bf16[16,8192]{1,0:T(8,128)(2,1)S(1)} %slice.89), channel_id=1, source_target_pairs={{0,3},{1,0},{2,1},{3,2},{4,7},{5,4},{6,5},{7,6},{8,11},{9,8},{10,9... | collective-permute-start | bytes 786440 | tf_op jit(solution)/shard_map/cond/branch_1_fun/ppermute | solution.py:43
  107.4 8.9 %collective-permute-start.17 = (bf16[32,8192]{1,0:T(8,128)(2,1)S(1)}, bf16[32,8192]{1,0:T(8,128)(2,1)S(1)}, u32[]{:S(2)}, u32[]{:S(2)}) collective-permute-start(bf16[32,8192]{1,0:T(8,128)(2,1)S(1)} %collective-permute-done.16.refs_4_), channel_id=1, source_target_pairs={{0,3},{1,0},{2,1},{3,2},{4,7},{5,4},{6,5},{7,6},{8,11},{9,8},{10,9... | collective-permute-start | bytes 1572872 | tf_op jit(solution)/shard_map/cond/branch_1_fun/ppermute | solution.py:43
  107.5 9.3 %collective-permute-start.19 = (bf16[32,8192]{1,0:T(8,128)(2,1)S(1)}, bf16[32,8192]{1,0:T(8,128)(2,1)}, u32[]{:S(2)}, u32[]{:S(2)}) collective-permute-start(bf16[32,8192]{1,0:T(8,128)(2,1)S(1)} %collective-permute-done.16.refs_4_), channel_id=1, source_target_pairs={{0,1},{1,2},{2,3},{3,0},{4,5},{5,6},{6,7},{7,4},{8,9},{9,10},{10,1... | collective-permute-start | bytes 1572872 | tf_op jit(solution)/shard_map/cond/branch_1_fun/ppermute | solution.py:43
  110.7 8.5 %collective-permute-start.18 = (bf16[32,8192]{1,0:T(8,128)(2,1)S(1)}, bf16[32,8192]{1,0:T(8,128)(2,1)}, u32[]{:S(2)}, u32[]{:S(2)}) collective-permute-start(bf16[32,8192]{1,0:T(8,128)(2,1)S(1)} %constant_dynamic-update-slice_fusion.4.refs_2_), channel_id=1, source_target_pairs={{0,4},{1,5},{2,6},{3,7},{4,0},{5,1},{6,2},{7,3},{8,12},{9,13},{10,... | collective-permute-start | bytes 1572872 | tf_op jit(solution)/shard_map/cond/branch_1_fun/ppermute | solution.py:43
  125.5 23.2 %collective-permute-start.42 = (bf16[32,8192]{1,0:T(8,128)(2,1)}, bf16[32,8192]{1,0:T(8,128)(2,1)S(1)}, u32[]{:S(2)}, u32[]{:S(2)}) collective-permute-start(bf16[32,8192]{1,0:T(8,128)(2,1)} %get-tuple-element.185), channel_id=1, source_target_pairs={{0,8},{8,16},{16,24},{24,32},{32,40},{40,48},{48,56},{56,64},{64,7... | collective-permute-start | bytes 1572872 | tf_op jit(solution)/shard_map/ppermute | solution.py:47

commit v5 on v4

--- a/solution.py
+++ b/solution.py
@@ -1,3 +1,4 @@
+import functools
 import math
 
 import jax
@@ -86,9 +87,9 @@
     above = over_tensor(pair, TO_DOWN)
     far_a = over_tensor(below[:HALF], TO_UP)
     far_b = over_tensor(above[HALF:ROWS], TO_DOWN)
-    far = jnp.concatenate([far_a, far_b])
-    x_far = over_tensor(far, TO_X)
-    return own, above[:ROWS], far, below[:ROWS], from_x, above[ROWS:], x_far, below[ROWS:]
+    x_far_a = over_tensor(far_a, TO_X)
+    x_far_b = over_tensor(far_b, TO_X)
+    return own, above, far_a, far_b, below, from_x, x_far_a, x_far_b
 
 
 def scatter_sum(parts):
@@ -154,7 +155,7 @@
 
 
 KC = 2048
-NC = 2048
+NC = 4096
 QKV = (HEADS + 2) * HEAD
 
 
@@ -162,14 +163,17 @@
     return pl.ds(pl.multiple_of(k * size, size), size)
 
 
-def layer_kernel(*refs):
-    blocks = refs[:8]
-    wq_ref, wkv_ref, wo_ref, cos_ref, sin_ref, allow_ref = refs[8:14]
-    outs = refs[14:22]
-    rows, w, wo, acc, ctx, row_sem, w_sem, wo_sem = refs[22:]
-
-    for i, b in enumerate(blocks):
-        pltpu.make_async_copy(b, rows.at[pl.ds(i * ROWS, ROWS)], row_sem).start()
+def layer_kernel(layout, *refs):
+    n_blocks = 1 + max(block for block, *_ in layout)
+    blocks = refs[:n_blocks]
+    wq_ref, wkv_ref, wo_ref, cos_ref, sin_ref, allow_ref = refs[n_blocks : n_blocks + 6]
+    outs = refs[n_blocks + 6 : n_blocks + 14]
+    rows, w, wo, acc, ctx, row_sem, w_sem, wo_sem = refs[n_blocks + 14 :]
+
+    for block, start, n, to in layout:
+        pltpu.make_async_copy(
+            blocks[block].at[pl.ds(start, n)], rows.at[pl.ds(to, n)], row_sem
+        ).start()
 
     @pl.loop(0, WIDTH // KC)
     def _(k):
@@ -222,13 +226,20 @@
             o[:, cols] = part[i * ROWS : (i + 1) * ROWS]
 
 
-def layer(blocks, wq, wkv, wo, cos, sin, allow):
+EACH = tuple((i, 0, ROWS, i * ROWS) for i in range(8))
+PAIRED = (
+    (0, 0, 32, 0), (1, 0, 32, 32), (2, 0, 16, 64), (3, 0, 16, 80), (4, 0, 32, 96),
+    (5, 0, 32, 128), (1, 32, 32, 160), (6, 0, 16, 192), (7, 0, 16, 208), (4, 32, 32, 224),
+)
+
+
+def layer(layout, blocks, wq, wkv, wo, cos, sin, allow):
     hbm = pl.BlockSpec(memory_space=pl.ANY)
     vmem = pl.BlockSpec(memory_space=pltpu.VMEM)
     return pl.pallas_call(
-        layer_kernel,
+        functools.partial(layer_kernel, layout),
         out_shape=[jax.ShapeDtypeStruct((ROWS, WIDTH), BF16)] * 8,
-        in_specs=[hbm] * 11 + [vmem] * 3,
+        in_specs=[hbm] * (len(blocks) + 3) + [vmem] * 3,
         out_specs=[vmem] * 8,
         scratch_shapes=[
             pltpu.VMEM((2 * MB, WIDTH), BF16),
@@ -249,9 +260,10 @@
 VC = 2048
 
 
-def vocab_kernel(order_ref, *refs):
-    blocks = refs[:8]
-    w0_ref, w1_ref, want_ref, out_ref, rows, w, acc, row_sem, w_sem = refs[8:]
+def vocab_kernel(first, order_ref, *refs):
+    blocks = refs[:NZ]
+    w0_ref, w1_ref, want_ref = refs[NZ : NZ + 3]
+    out_ref, rows, w, acc, row_sem, w_sem = refs[-6:]
     for i, b in enumerate(blocks):
         pltpu.make_async_copy(b, rows.at[pl.ds(i * ROWS, ROWS)], row_sem).start()
 
@@ -274,37 +286,47 @@
     top = jnp.max(logits, axis=1, keepdims=True)
     total = jnp.sum(jnp.exp(logits - top), axis=1, keepdims=True)
     column = lax.broadcasted_iota(jnp.int32, logits.shape, 1)
-    picked = jnp.sum(jnp.where(column == want_ref[:, :1], logits, 0.0), axis=1, keepdims=True)
-    lane = lax.broadcasted_iota(jnp.int32, (2 * MB, 128), 1)
+    want = want_ref[first * ROWS : (first + NZ) * ROWS, :1]
+    picked = jnp.sum(jnp.where(column == want, logits, 0.0), axis=1, keepdims=True)
+    lane = lax.broadcasted_iota(jnp.int32, (MB, 128), 1)
     stats = jnp.where(lane == 0, top, jnp.where(lane == 1, total, picked)).T
-    for i in range(8):
+    if first:
+        out_ref[:8, :] = refs[NZ + 3][...]
+    for i in range(NZ):
         mine = slice(i * ROWS, (i + 1) * ROWS)
         line = jnp.concatenate([stats[k : k + 1, mine] for k in (0, 1, 2, 2)], axis=1)
-        out_ref[pl.ds(order_ref[i], 1), :] = line
-    lines = out_ref[:8, :]
-    for s in range(1, 16):
-        out_ref[s * 8 : (s + 1) * 8, :] = lines
-
-
-def vocab(order, blocks, w0, w1, want):
+        out_ref[pl.ds(order_ref[first + i], 1), :] = line
+    if first:
+        lines = out_ref[:8, :]
+        for s in range(1, 16):
+            out_ref[s * 8 : (s + 1) * 8, :] = lines
+
+
+def vocab_part(order, blocks, w0, w1, want, lines=None):
     hbm = pl.BlockSpec(memory_space=pl.ANY)
     vmem = pl.BlockSpec(memory_space=pltpu.VMEM)
+    given = [] if lines is None else [lines]
     return pl.pallas_call(
-        vocab_kernel,
-        out_shape=jax.ShapeDtypeStruct((128, 128), F32),
-        in_specs=[pl.BlockSpec(memory_space=pltpu.SMEM)] + [hbm] * 10 + [vmem],
+        functools.partial(vocab_kernel, NZ * len(given)),
+        out_shape=jax.ShapeDtypeStruct((128 if given else 8, 128), F32),
+        in_specs=[pl.BlockSpec(memory_space=pltpu.SMEM)] + [hbm] * (NZ + 2) + [vmem] * (1 + len(given)),
         out_specs=vmem,
         scratch_shapes=[
-            pltpu.VMEM((2 * MB, WIDTH), BF16),
+            pltpu.VMEM((MB, WIDTH), BF16),
             pltpu.VMEM((WIDTH, 2 * VL), BF16),
-            pltpu.VMEM((2 * MB, 2 * VL), F32),
+            pltpu.VMEM((MB, 2 * VL), F32),
             pltpu.SemaphoreType.DMA,
             pltpu.SemaphoreType.DMA((WIDTH // VC,)),
         ],
-        compiler_params=pltpu.CompilerParams(vmem_limit_bytes=48 * 1024 * 1024),
-        cost_estimate=pl.CostEstimate(flops=2 * 10**9, bytes_accessed=14 * 2**20, transcendentals=0),
+        compiler_params=pltpu.CompilerParams(vmem_limit_bytes=32 * 1024 * 1024),
+        cost_estimate=pl.CostEstimate(flops=10**9, bytes_accessed=10 * 2**20, transcendentals=0),
         name="vocab",
-    )(order, *blocks, w0, w1, want)
+    )(order, *blocks, w0, w1, want, *given)
+
+
+def vocab(order, blocks, w0, w1, want):
+    lines = vocab_part(order, blocks[:NZ], w0, w1, want)
+    return vocab_part(order, blocks[NZ:], w0, w1, want, lines)
 
 
 def add(*terms):
@@ -361,11 +383,12 @@
     )
     blocks = (normed, *blocks)
 
-    def layer_rows(blocks):
-        return finish(my_rows, scatter_sum(layer(blocks, *weights, *angles)), final_gain)
+    def layer_rows(layout, blocks):
+        terms = scatter_sum(layer(layout, blocks, *weights, *angles))
+        return finish(my_rows, terms, final_gain)
 
     def odd_path():
-        layer_out, final_rows = layer_rows(blocks)
+        layer_out, final_rows = layer_rows(EACH, blocks)
         order = order_from(jnp.where(section // 2 % 2 == 1, x, 1 - x))
         starts = jnp.stack([section, section ^ 1]) * 8 * VL + rank * VL
         want = jnp.take(targets.reshape(8, ROWS), order, axis=0).reshape(-1)
@@ -377,10 +400,10 @@
         return layer_out, vocab(order, all_rows, w_vocab, other_vocab, want)
 
     def even_path():
-        return layer_rows(gather_pairs(normed))[0], jnp.zeros((128, 128), F32)
+        return layer_rows(PAIRED, gather_pairs(normed))[0], jnp.zeros((128, 128), F32)
 
     layer_out, stats = lax.cond(odd, odd_path, even_path)
-    handed = over_section(layer_out, [(s, s + 1) for s in range(15)])[None]
+    handed = over_section(layer_out[None], [(s, s + 1) for s in range(15)])
     got = lax.all_to_all(stats, ("section", "tensor"), 0, 0, tiled=True)
     return handed, merge(got)
 

time: 150 us -> 148 us (0.987)
  waiting for transfers between devices: 64 us -> 58.7 us
  Pallas kernels: 21.2 us -> 24.5 us
    pallas_call x2 -> x3, Pallas kernels: 17 us -> 20.4 us  [the longest x1 10.5 us: layer(): pl.pallas_call(functools.partial(layer_kernel, layout), out_shape=[jax.Sh...]
    ppermute x23, waiting for transfers between devices: 43.7 us -> 40.4 us  [over_tensor(): return lax.ppermute(block, 'tensor', pairs)]
    ppermute x1, waiting for transfers between devices: 20.3 us -> 18.3 us  [spread_from_last(): lax.ppermute(rows, ('section', 'tensor'), here)]
  transfers between devices with their start and end apart: 29 -> 29, of which waited for: 14 -> 13; matrix products, arithmetic and copies ran while one was open for 4% -> 4% of each run, Pallas kernels for 2% -> 6%
where the time goes in v5:
time: 148 us; the launch traced here: 147 us
  waiting for transfers between devices  58.7 us (40%)
  starting transfers between devices  36.2 us (24%)
  Pallas kernels  24.5 us (17%)
  blocking collectives  19.5 us (13%)
  other arithmetic  3.56 us (2%)
  local copies, waits for them, and re-layouts  3.26 us (2%)
    ppermute x23, waiting for transfers between devices, over_tensor(): return lax.ppermute(block, 'tensor', pairs)  40.4 us
    ppermute x23, starting transfers between devices, over_tensor(): return lax.ppermute(block, 'tensor', pairs)  29.5 us
    all_to_all x1, blocking collectives, body(): got = lax.all_to_all(stats, ('section', 'tensor'), 0, 0, tiled=True)  19.5 us
    ppermute x1, waiting for transfers between devices, spread_from_last(): lax.ppermute(rows, ('section', 'tensor'), here)  18.3 us
    pallas_call x1, Pallas kernels, layer(): pl.pallas_call(functools.partial(layer_kernel, layout), out_shape=[jax.Sh...  10.5 us
    pallas_call x2, Pallas kernels, vocab_part(): pl.pallas_call(functools.partial(vocab_kernel, NZ * len(given)), out_shap...  9.87 us
    ppermute x5, starting transfers between devices, over_section(): return lax.ppermute(block, 'section', pairs)  5.49 us
  transfers between devices with their start and end apart: 29, of which 13 were waited for; matrix products, arithmetic and copies ran while one was open for 4% of the time, Pallas kernels for 6%

profile of v5, /device:TPU:1, one launch (start us, length us, event | category | flops | bytes accessed | tf_op | source)
XLA Modules:
  0.0 147.4 jit_solution(15495472585473808995)
XLA Ops:
  0.7 1.5 %collective-permute-start.42 = (bf16[8192,256]{1,0:T(8,128)(2,1)}, bf16[8192,256]{1,0:T(8,128)(2,1)}, u32[]{:S(2)}, u32[]{:S(2)}) collective-permute-start(bf16[8192,256]{1,0:T(8,128)(2,1)} %param.22), channel_id=1, source_target_pairs={{0,8},{8,0},{16,24},{24,16},{32,40},{40,32},{48,56},{56,48},{64,72... | collective-permute-start | bytes 12582920 | tf_op jit(solution)/shard_map/ppermute | solution.py:48
  2.2 1.4 norm.1
  3.6 28.7 %conditional.6 = (bf16[32,8192]{1,0:T(8,128)(2,1)}, bf16[32,8192]{1,0:T(8,128)(2,1)}, bf16[32,8192]{1,0:T(8,128)(2,1)}, bf16[32,8192]{1,0:T(8,128)(2,1)}, bf16[3...) conditional(s32[]{:T(128)} %convert_element_type.122, ...), branch_computations={%region_0.2_spmd, %region_1.3_spmd} | conditional | flops 231513 | bytes 15493352
  3.6 1.8 %collective-permute-start.36 = (bf16[32,8192]{1,0:T(8,128)(2,1)S(1)}, bf16[32,8192]{1,0:T(8,128)(2,1)}, u32[]{:S(2)}, u32[]{:S(2)}) collective-permute-start(bf16[32,8192]{1,0:T(8,128)(2,1)S(1)} %get-tuple-element.106), channel_id=1, source_target_pairs={{0,1},{1,2},{2,3},{3,0},{4,5},{5,6},{6,7},{7,4},{8,9},{9,10},{10,1... | collective-permute-start | bytes 1572872 | tf_op jit(solution)/shard_map/cond/branch_1_fun/ppermute | solution.py:44
  6.6 2.2 %collective-permute-start.35 = (bf16[32,8192]{1,0:T(8,128)(2,1)S(1)}, bf16[32,8192]{1,0:T(8,128)(2,1)}, u32[]{:S(2)}, u32[]{:S(2)}) collective-permute-start(bf16[32,8192]{1,0:T(8,128)(2,1)S(1)} %get-tuple-element.106), channel_id=1, source_target_pairs={{0,3},{1,0},{2,1},{3,2},{4,7},{5,4},{6,5},{7,6},{8,11},{9,8},{10,9... | collective-permute-start | bytes 1572872 | tf_op jit(solution)/shard_map/cond/branch_1_fun/ppermute | solution.py:44
  9.6 1.3 reduce.7
  11.9 2.3 %collective-permute-done.36 = bf16[32,8192]{1,0:T(8,128)(2,1)} collective-permute-done((bf16[32,8192]{1,0:T(8,128)(2,1)S(1)}, bf16[32,8192]{1,0:T(8,128)(2,1)}, u32[]{:S(2)}, u32[]{:S(2)}) %collective-permute-start.36) | collective-permute-done | bytes 524320 | tf_op jit(solution)/shard_map/cond/branch_1_fun/ppermute | solution.py:44
  14.3 2.7 %collective-permute-start.39 = (bf16[32,8192]{1,0:T(8,128)(2,1)}, bf16[32,8192]{1,0:T(8,128)(2,1)}, u32[]{:S(2)}, u32[]{:S(2)}) collective-permute-start(bf16[32,8192]{1,0:T(8,128)(2,1)} %collective-permute-done.38), channel_id=1, source_target_pairs={{0,3},{1,0},{2,1},{3,2},{4,7},{5,4},{6,5},{7,6},{8,11},{9,8},{10,9... | collective-permute-start | bytes 1572872 | tf_op jit(solution)/shard_map/cond/branch_1_fun/ppermute | solution.py:44
  17.0 6.8 %collective-permute-done.37 = bf16[32,8192]{1,0:T(8,128)(2,1)} collective-permute-done((bf16[32,8192]{1,0:T(8,128)(2,1)}, bf16[32,8192]{1,0:T(8,128)(2,1)}, u32[]{:S(2)}, u32[]{:S(2)}) %collective-permute-start.37) | collective-permute-done | bytes 524320 | tf_op jit(solution)/shard_map/cond/branch_1_fun/ppermute | solution.py:44
  25.8 4.9 %collective-permute-done.41 = bf16[32,8192]{1,0:T(8,128)(2,1)} collective-permute-done((bf16[32,8192]{1,0:T(8,128)(2,1)}, bf16[32,8192]{1,0:T(8,128)(2,1)}, u32[]{:S(2)}, u32[]{:S(2)}) %collective-permute-start.41) | collective-permute-done | bytes 524320 | tf_op jit(solution)/shard_map/cond/branch_1_fun/ppermute | solution.py:44
  30.7 1.6 %collective-permute-done.40 = bf16[32,8192]{1,0:T(8,128)(2,1)} collective-permute-done((bf16[32,8192]{1,0:T(8,128)(2,1)}, bf16[32,8192]{1,0:T(8,128)(2,1)}, u32[]{:S(2)}, u32[]{:S(2)}) %collective-permute-start.40) | collective-permute-done | bytes 524320 | tf_op jit(solution)/shard_map/cond/branch_1_fun/ppermute | solution.py:44
  32.3 91.3 %conditional.5 = (bf16[32,8192]{1,0:T(8,128)(2,1)}, f32[128,128]{1,0:T(8,128)}) conditional(s32[]{:T(128)} %convert_element_type.122, (bf16[32,8192]{1,0:T(8,128)(2,1)S(1)}, bf16[8192,512]{1,0:T(8,128)(2,1)}, bf16[8192,256]{1,0:T(8,128)(2,1)}, bf16[512,8192]{1,0:T(8,128)(2,1)}, f32[256,128]{1,0:T(8,128)S(1)}, /*index=5*/f32[256,128]{1,0:T(8,128)S(1)}, ...), branch_computations={%region_2.4_spmd, %region_3.6_spmd} | conditional | flops 8006819840 | bytes 119718512 | solution.py:405
  32.6 10.5 %layer.3 = (bf16[32,8192]{1,0:T(8,128)(2,1)S(1)}, bf16[32,8192]{1,0:T(8,128)(2,1)S(1)}, bf16[32,8192]{1,0:T(8,128)(2,1)S(1)}, bf16[32,8192]{1,0:T(8,128)(2,1)S(1...) custom-call(bf16[32,8192]{1,0:T(8,128)(2,1)S(1)} %get-tuple-element., ...), custom_call_target="tpu_custom_call" | custom-call | flops 6000000000 | bytes 29360128 | tf_op jit(solution)/shard_map/cond/branch_1_fun/layer/pallas_call | solution.py:239
  44.4 2.7 %collective-permute-start.16 = (bf16[32,8192]{1,0:T(8,128)(2,1)S(1)}, bf16[32,8192]{1,0:T(8,128)(2,1)S(1)}, u32[]{:S(2)}, u32[]{:S(2)}) collective-permute-start(bf16[32,8192]{1,0:T(8,128)(2,1)S(1)} %get-tuple-element.146), channel_id=1, source_target_pairs={{0,3},{1,0},{2,1},{3,2},{4,7},{5,4},{6,5},{7,6},{8,11},{9,8},{10,9... | collective-permute-start | bytes 1572872 | tf_op jit(solution)/shard_map/cond/branch_1_fun/ppermute | solution.py:44
  47.1 4.1 %collective-permute-done.18 = bf16[32,8192]{1,0:T(8,128)(2,1)S(1)} collective-permute-done((bf16[32,8192]{1,0:T(8,128)(2,1)S(1)}, bf16[32,8192]{1,0:T(8,128)(2,1)S(1)}, u32[]{:S(2)}, u32[]{:S(2)}) %collective-permute-start.18) | collective-permute-done | bytes 524320 | tf_op jit(solution)/shard_map/cond/branch_1_fun/ppermute | solution.py:44
  51.4 2.7 %collective-permute-start.19 = (bf16[16,8192]{1,0:T(8,128)(2,1)S(1)}, bf16[16,8192]{1,0:T(8,128)(2,1)S(1)}, u32[]{:S(2)}, u32[]{:S(2)}) collective-permute-start(bf16[16,8192]{1,0:T(8,128)(2,1)S(1)} %get-tuple-element.204), channel_id=1, source_target_pairs={{0,3},{1,0},{2,1},{3,2},{4,7},{5,4},{6,5},{7,6},{8,11},{9,8},{10,9... | collective-permute-start | bytes 786440 | tf_op jit(solution)/shard_map/cond/branch_1_fun/ppermute | solution.py:44
  55.5 2.3 %collective-permute-done.21 = bf16[16,8192]{1,0:T(8,128)(2,1)S(1)} collective-permute-done((bf16[16,8192]{1,0:T(8,128)(2,1)S(1)}, bf16[16,8192]{1,0:T(8,128)(2,1)S(1)}, u32[]{:S(2)}, u32[]{:S(2)}) %collective-permute-start.21) | collective-permute-done | bytes 262176 | tf_op jit(solution)/shard_map/cond/branch_1_fun/ppermute | solution.py:44
  58.1 2.7 %collective-permute-start.20 = (bf16[32,8192]{1,0:T(8,128)(2,1)S(1)}, bf16[32,8192]{1,0:T(8,128)(2,1)S(1)}, u32[]{:S(2)}, u32[]{:S(2)}) collective-permute-start(bf16[32,8192]{1,0:T(8,128)(2,1)S(1)} %pad_maximum_fusion.2), channel_id=1, source_target_pairs={{0,3},{1,0},{2,1},{3,2},{4,7},{5,4},{6,5},{7,6},{8,11},{9,8},{10,9... | collective-permute-start | bytes 1572872 | tf_op jit(solution)/shard_map/cond/branch_1_fun/ppermute | solution.py:44
  60.9 2.7 %collective-permute-done.17.b_ref = bf16[32,8192]{1,0:T(8,128)(2,1)S(1)} collective-permute-done((bf16[32,8192]{1,0:T(8,128)(2,1)S(1)}, bf16[32,8192]{1,0:T(8,128)(2,1)S(1)}, u32[]{:S(2)}, u32[]{:S(2)}) %collective-permute-start.17) | collective-permute-done | bytes 524320 | tf_op jit(solution)/shard_map/cond/branch_1_fun/ppermute | solution.py:44
  63.5 3.7 %collective-permute-done.22.d_ref = bf16[32,8192]{1,0:T(8,128)(2,1)S(1)} collective-permute-done((bf16[32,8192]{1,0:T(8,128)(2,1)S(1)}, bf16[32,8192]{1,0:T(8,128)(2,1)S(1)}, u32[]{:S(2)}, u32[]{:S(2)}) %collective-permute-start.22) | collective-permute-done | bytes 524320 | tf_op jit(solution)/shard_map/cond/branch_1_fun/ppermute | solution.py:44
  72.0 18.3 %collective-permute-done.26 = bf16[32,8192]{1,0:T(8,128)(2,1)S(1)} collective-permute-done((bf16[32,8192]{1,0:T(8,128)(2,1)S(1)}, bf16[32,8192]{1,0:T(8,128)(2,1)S(1)}, u32[]{:S(2)}, u32[]{:S(2)}) %collective-permute-start.26) | collective-permute-done | bytes 524320 | tf_op jit(solution)/shard_map/cond/branch_1_fun/ppermute | solution.py:348
  90.6 2.9 %collective-permute-start.31 = (bf16[32,8192]{1,0:T(8,128)(2,1)S(1)}, bf16[32,8192]{1,0:T(8,128)(2,1)S(1)}, u32[]{:S(2)}, u32[]{:S(2)}) collective-permute-start(bf16[32,8192]{1,0:T(8,128)(2,1)S(1)} %broadcast_select_fusion.refs_0_), channel_id=1, source_target_pairs={{0,3},{1,0},{2,1},{3,2},{4,7},{5,4},{6,5},{7,6},{8,11},{9,8},{10,9... | collective-permute-start | bytes 1572872 | tf_op jit(solution)/shard_map/cond/branch_1_fun/ppermute | solution.py:44
  93.7 9.3 %collective-permute-done.29.refs_3_ = bf16[32,8192]{1,0:T(8,128)(2,1)S(1)} collective-permute-done((bf16[32,8192]{1,0:T(8,128)(2,1)S(1)}, bf16[32,8192]{1,0:T(8,128)(2,1)S(1)}, u32[]{:S(2)}, u32[]{:S(2)}) %collective-permute-start.29) | collective-permute-done | bytes 524320 | tf_op jit(solution)/shard_map/cond/branch_1_fun/ppermute | solution.py:44
  103.9 2.7 %collective-permute-start.32 = (bf16[16,8192]{1,0:T(8,128)(2,1)S(1)}, bf16[16,8192]{1,0:T(8,128)(2,1)S(1)}, u32[]{:S(2)}, u32[]{:S(2)}) collective-permute-start(bf16[16,8192]{1,0:T(8,128)(2,1)S(1)} %slice.73), channel_id=1, source_target_pairs={{0,3},{1,0},{2,1},{3,2},{4,7},{5,4},{6,5},{7,6},{8,11},{9,8},{10,9... | collective-permute-start | bytes 786440 | tf_op jit(solution)/shard_map/cond/branch_1_fun/ppermute | solution.py:44
  106.7 1.4 collective-permute-start.34
  108.1 1.5 %collective-permute-done.30 = bf16[16,8192]{1,0:T(8,128)(2,1)S(1)} collective-permute-done((bf16[16,8192]{1,0:T(8,128)(2,1)S(1)}, bf16[16,8192]{1,0:T(8,128)(2,1)S(1)}, u32[]{:S(2)}, u32[]{:S(2)}) %collective-permute-start.30) | collective-permute-done | bytes 262176 | tf_op jit(solution)/shard_map/cond/branch_1_fun/ppermute | solution.py:44
  109.9 2.1 %collective-permute-start.33 = (bf16[32,8192]{1,0:T(8,128)(2,1)S(1)}, bf16[32,8192]{1,0:T(8,128)(2,1)}, u32[]{:S(2)}, u32[]{:S(2)}) collective-permute-start(bf16[32,8192]{1,0:T(8,128)(2,1)S(1)} %constant_dynamic-update-slice_fusion.2.refs_2_), channel_id=1, source_target_pairs={{0,4},{1,5},{2,6},{3,7},{4,0},{5,1},{6,2},{7,3},{8,12},{9,13},{10,... | collective-permute-start | bytes 1572872 | tf_op jit(solution)/shard_map/cond/branch_1_fun/ppermute | solution.py:44
  112.4 5.2 %vocab.2.refs_7_ = f32[8,128]{1,0:T(8,128)S(1)} custom-call(s32[8]{0:T(128)S(1)} %add.172.order_ref, bf16[32,8192]{1,0:T(8,128)(2,1)S(1)} %broadcast_select_fusion.refs_0_, bf16[32,8192]{1,0:T(8,128)(2,1)S(1)} %collective-permute-done.31.refs_1_, bf16[32,8192]{1,0:T(8,128)(2,1)S(1)} %constant_dynamic-update-slice_fusion.2.refs_2_, ...), custom_call_target="tpu_custom_call" | custom-call | flops 1000000000 | bytes 10485760 | tf_op jit(solution)/shard_map/cond/branch_1_fun/vocab/pallas_call | solution.py:309
  118.7 4.6 %vocab.3 = f32[128,128]{1,0:T(8,128)} custom-call(s32[8]{0:T(128)S(1)} %add.172.order_ref, bf16[32,8192]{1,0:T(8,128)(2,1)S(1)} %collective-permute-done.27.refs_0_, bf16[32,8192]{1,0:T(8,128)(2,1)S(1)} %collective-permute-done.28.refs_1_, bf16[32,8192]{1,0:T(8,128)(2,1)} %collective-permute-done.33.refs_2_, ...), custom_call_target="tpu_custom_call" | custom-call | flops 1000000000 | bytes 10485760 | tf_op jit(solution)/shard_map/cond/branch_1_fun/vocab/pallas_call | solution.py:309
  123.6 1.9 %collective-permute-start.43 = (bf16[1,32,8192]{2,1,0:T(8,128)(2,1)}, bf16[1,32,8192]{2,1,0:T(8,128)(2,1)S(1)}, u32[]{:S(2)}, u32[]{:S(2)}) collective-permute-start(bf16[1,32,8192]{2,1,0:T(8,128)(2,1)} %bitcast.12), channel_id=1, source_target_pairs={{0,8},{8,16},{16,24},{24,32},{32,40},{40,48},{48,56},{56,64},{64,7... | collective-permute-start | bytes 1572872 | tf_op jit(solution)/shard_map/ppermute | solution.py:48
  125.6 19.5 %all_to_all.11 = f32[128,1,128]{2,1,0:T(1,128)} all-to-all(f32[128,1,128]{2,1,0:T(1,128)} %bitcast.13), channel_id=1, replica_groups=mesh['section'=16,'tensor'=8] {'section','tensor'}, dimensions={0} | all-to-all | bytes 131072 | tf_op jit(solution)/shard_map/all_to_all | solution.py:407
  145.0 1.6 %merge.1 = f32[32]{0:T(128)} custom-call(f32[128,128]{1,0:T(8,128)} %bitcast.24), custom_call_target="tpu_custom_call" | custom-call | tf_op jit(solution)/shard_map/merge/pallas_call | solution.py:152
  (96 shorter events, 17.0 us)
Async XLA Ops:
  0.6 31.7 %copy-start.1 = (bf16[1,32,8192]{2,1,0:T(8,128)(2,1)S(1)}, bf16[1,32,8192]{2,1,0:T(8,128)(2,1)}, u32[]{:S(2)}) copy-start(bf16[1,32,8192]{2,1,0:T(8,128)(2,1)} %param.15) | copy-start | bytes 1572868
  0.6 31.7 %copy-start.4 = (bf16[8192]{0:T(1024)(128)(2,1)S(1)}, bf16[8192]{0:T(1024)(128)(2,1)}, u32[]{:S(2)}) copy-start(bf16[8192]{0:T(1024)(128)(2,1)} %param.21) | copy-start | bytes 49156
  0.7 31.7 %copy-start.5 = (s32[256]{0:T(256)S(1)}, s32[256]{0:T(256)}, u32[]{:S(2)}) copy-start(s32[256]{0:T(256)} %param.23) | copy-start | bytes 3076
  0.7 31.6 %collective-permute-start.42 = (bf16[8192,256]{1,0:T(8,128)(2,1)}, bf16[8192,256]{1,0:T(8,128)(2,1)}, u32[]{:S(2)}, u32[]{:S(2)}) collective-permute-start(bf16[8192,256]{1,0:T(8,128)(2,1)} %param.22), channel_id=1, source_target_pairs={{0,8},{8,0},{16,24},{24,16},{32,40},{40,32},{48,56},{56,48},{64,72... | collective-permute-start | bytes 12582920 | tf_op jit(solution)/shard_map/ppermute | solution.py:48
  3.6 10.6 %collective-permute-start.36 = (bf16[32,8192]{1,0:T(8,128)(2,1)S(1)}, bf16[32,8192]{1,0:T(8,128)(2,1)}, u32[]{:S(2)}, u32[]{:S(2)}) collective-permute-start(bf16[32,8192]{1,0:T(8,128)(2,1)S(1)} %get-tuple-element.106), channel_id=1, source_target_pairs={{0,1},{1,2},{2,3},{3,0},{4,5},{5,6},{6,7},{7,4},{8,9},{9,10},{10,1... | collective-permute-start | bytes 1572872 | tf_op jit(solution)/shard_map/cond/branch_1_fun/ppermute | solution.py:44
  5.4 8.9 %collective-permute-start.38 = (bf16[32,8192]{1,0:T(8,128)(2,1)S(1)}, bf16[32,8192]{1,0:T(8,128)(2,1)}, u32[]{:S(2)}, u32[]{:S(2)}) collective-permute-start(bf16[32,8192]{1,0:T(8,128)(2,1)S(1)} %get-tuple-element.106), channel_id=1, source_target_pairs={{0,4},{1,5},{2,6},{3,7},{4,0},{5,1},{6,2},{7,3},{8,12},{9,13},{10,... | collective-permute-start | bytes 1572872 | tf_op jit(solution)/shard_map/cond/branch_1_fun/ppermute | solution.py:44
  6.6 19.2 %collective-permute-start.35 = (bf16[32,8192]{1,0:T(8,128)(2,1)S(1)}, bf16[32,8192]{1,0:T(8,128)(2,1)}, u32[]{:S(2)}, u32[]{:S(2)}) collective-permute-start(bf16[32,8192]{1,0:T(8,128)(2,1)S(1)} %get-tuple-element.106), channel_id=1, source_target_pairs={{0,3},{1,0},{2,1},{3,2},{4,7},{5,4},{6,5},{7,6},{8,11},{9,8},{10,9... | collective-permute-start | bytes 1572872 | tf_op jit(solution)/shard_map/cond/branch_1_fun/ppermute | solution.py:44
  14.2 9.6 %collective-permute-start.37 = (bf16[32,8192]{1,0:T(8,128)(2,1)}, bf16[32,8192]{1,0:T(8,128)(2,1)}, u32[]{:S(2)}, u32[]{:S(2)}) collective-permute-start(bf16[32,8192]{1,0:T(8,128)(2,1)} %collective-permute-done.36), channel_id=1, source_target_pairs={{0,1},{1,2},{2,3},{3,0},{4,5},{5,6},{6,7},{7,4},{8,9},{9,10},{10,1... | collective-permute-start | bytes 1572872 | tf_op jit(solution)/shard_map/cond/branch_1_fun/ppermute | solution.py:44
  14.3 11.5 %collective-permute-start.39 = (bf16[32,8192]{1,0:T(8,128)(2,1)}, bf16[32,8192]{1,0:T(8,128)(2,1)}, u32[]{:S(2)}, u32[]{:S(2)}) collective-permute-start(bf16[32,8192]{1,0:T(8,128)(2,1)} %collective-permute-done.38), channel_id=1, source_target_pairs={{0,3},{1,0},{2,1},{3,2},{4,7},{5,4},{6,5},{7,6},{8,11},{9,8},{10,9... | collective-permute-start | bytes 1572872 | tf_op jit(solution)/shard_map/cond/branch_1_fun/ppermute | solution.py:44
  17.0 13.7 %collective-permute-start.41 = (bf16[32,8192]{1,0:T(8,128)(2,1)}, bf16[32,8192]{1,0:T(8,128)(2,1)}, u32[]{:S(2)}, u32[]{:S(2)}) collective-permute-start(bf16[32,8192]{1,0:T(8,128)(2,1)} %collective-permute-done.38), channel_id=1, source_target_pairs={{0,1},{1,2},{2,3},{3,0},{4,5},{5,6},{6,7},{7,4},{8,9},{9,10},{10,1... | collective-permute-start | bytes 1572872 | tf_op jit(solution)/shard_map/cond/branch_1_fun/ppermute | solution.py:44
  23.8 8.5 %collective-permute-start.40 = (bf16[32,8192]{1,0:T(8,128)(2,1)}, bf16[32,8192]{1,0:T(8,128)(2,1)}, u32[]{:S(2)}, u32[]{:S(2)}) collective-permute-start(bf16[32,8192]{1,0:T(8,128)(2,1)} %collective-permute-done.37), channel_id=1, source_target_pairs={{0,4},{1,5},{2,6},{3,7},{4,0},{5,1},{6,2},{7,3},{8,12},{9,13},{10,... | collective-permute-start | bytes 1572872 | tf_op jit(solution)/shard_map/cond/branch_1_fun/ppermute | solution.py:44
  43.1 8.1 %collective-permute-start.18 = (bf16[32,8192]{1,0:T(8,128)(2,1)S(1)}, bf16[32,8192]{1,0:T(8,128)(2,1)S(1)}, u32[]{:S(2)}, u32[]{:S(2)}) collective-permute-start(bf16[32,8192]{1,0:T(8,128)(2,1)S(1)} %get-tuple-element.149), channel_id=1, source_target_pairs={{0,4},{1,5},{2,6},{3,7},{4,0},{5,1},{6,2},{7,3},{8,12},{9,13},{10,... | collective-permute-start | bytes 1572872 | tf_op jit(solution)/shard_map/cond/branch_1_fun/ppermute | solution.py:44
  44.3 9.7 %collective-permute-start.15 = (bf16[32,8192]{1,0:T(8,128)(2,1)S(1)}, bf16[32,8192]{1,0:T(8,128)(2,1)S(1)}, u32[]{:S(2)}, u32[]{:S(2)}) collective-permute-start(bf16[32,8192]{1,0:T(8,128)(2,1)S(1)} %get-tuple-element.145), channel_id=1, source_target_pairs={{0,1},{1,2},{2,3},{3,0},{4,5},{5,6},{6,7},{7,4},{8,9},{9,10},{10,1... | collective-permute-start | bytes 1572872 | tf_op jit(solution)/shard_map/cond/branch_1_fun/ppermute | solution.py:44
  44.4 9.7 %collective-permute-start.16 = (bf16[32,8192]{1,0:T(8,128)(2,1)S(1)}, bf16[32,8192]{1,0:T(8,128)(2,1)S(1)}, u32[]{:S(2)}, u32[]{:S(2)}) collective-permute-start(bf16[32,8192]{1,0:T(8,128)(2,1)S(1)} %get-tuple-element.146), channel_id=1, source_target_pairs={{0,3},{1,0},{2,1},{3,2},{4,7},{5,4},{6,5},{7,6},{8,11},{9,8},{10,9... | collective-permute-start | bytes 1572872 | tf_op jit(solution)/shard_map/cond/branch_1_fun/ppermute | solution.py:44
  51.3 6.5 %collective-permute-start.21 = (bf16[16,8192]{1,0:T(8,128)(2,1)S(1)}, bf16[16,8192]{1,0:T(8,128)(2,1)S(1)}, u32[]{:S(2)}, u32[]{:S(2)}) collective-permute-start(bf16[16,8192]{1,0:T(8,128)(2,1)S(1)} %get-tuple-element.203), channel_id=1, source_target_pairs={{0,1},{1,2},{2,3},{3,0},{4,5},{5,6},{6,7},{7,4},{8,9},{9,10},{10,1... | collective-permute-start | bytes 786440 | tf_op jit(solution)/shard_map/cond/branch_1_fun/ppermute | solution.py:44
  51.4 6.6 %collective-permute-start.19 = (bf16[16,8192]{1,0:T(8,128)(2,1)S(1)}, bf16[16,8192]{1,0:T(8,128)(2,1)S(1)}, u32[]{:S(2)}, u32[]{:S(2)}) collective-permute-start(bf16[16,8192]{1,0:T(8,128)(2,1)S(1)} %get-tuple-element.204), channel_id=1, source_target_pairs={{0,3},{1,0},{2,1},{3,2},{4,7},{5,4},{6,5},{7,6},{8,11},{9,8},{10,9... | collective-permute-start | bytes 786440 | tf_op jit(solution)/shard_map/cond/branch_1_fun/ppermute | solution.py:44
  54.2 9.3 %collective-permute-start.17 = (bf16[32,8192]{1,0:T(8,128)(2,1)S(1)}, bf16[32,8192]{1,0:T(8,128)(2,1)S(1)}, u32[]{:S(2)}, u32[]{:S(2)}) collective-permute-start(bf16[32,8192]{1,0:T(8,128)(2,1)S(1)} %add_convert_fusion.5), channel_id=1, source_target_pairs={{0,4},{1,5},{2,6},{3,7},{4,0},{5,1},{6,2},{7,3},{8,12},{9,13},{10,... | collective-permute-start | bytes 1572872 | tf_op jit(solution)/shard_map/cond/branch_1_fun/ppermute | solution.py:44
  57.9 9.3 %collective-permute-start.22 = (bf16[32,8192]{1,0:T(8,128)(2,1)S(1)}, bf16[32,8192]{1,0:T(8,128)(2,1)S(1)}, u32[]{:S(2)}, u32[]{:S(2)}) collective-permute-start(bf16[32,8192]{1,0:T(8,128)(2,1)S(1)} %pad_maximum_fusion.3), channel_id=1, source_target_pairs={{0,1},{1,2},{2,3},{3,0},{4,5},{5,6},{6,7},{7,4},{8,9},{9,10},{10,1... | collective-permute-start | bytes 1572872 | tf_op jit(solution)/shard_map/cond/branch_1_fun/ppermute | solution.py:44
  58.1 9.1 %collective-permute-start.20 = (bf16[32,8192]{1,0:T(8,128)(2,1)S(1)}, bf16[32,8192]{1,0:T(8,128)(2,1)S(1)}, u32[]{:S(2)}, u32[]{:S(2)}) collective-permute-start(bf16[32,8192]{1,0:T(8,128)(2,1)S(1)} %pad_maximum_fusion.2), channel_id=1, source_target_pairs={{0,3},{1,0},{2,1},{3,2},{4,7},{5,4},{6,5},{7,6},{8,11},{9,8},{10,9... | collective-permute-start | bytes 1572872 | tf_op jit(solution)/shard_map/cond/branch_1_fun/ppermute | solution.py:44
  68.4 2.1 %collective-permute-start.23 = (bf16[32,8192]{1,0:T(8,128)(2,1)S(1)}, bf16[32,8192]{1,0:T(8,128)(2,1)S(1)}, u32[]{:S(2)}, u32[]{:S(2)}) collective-permute-start(bf16[32,8192]{1,0:T(8,128)(2,1)S(1)} %get-tuple-element.156), channel_id=1, source_target_pairs={{120,24},{121,25},{122,26},{123,27},{124,28},{125,29},{126,30},{12... | collective-permute-start | bytes 1572872 | tf_op jit(solution)/shard_map/cond/branch_1_fun/ppermute | solution.py:48
  69.1 1.4 collective-permute-start.24
  69.8 0.7 collective-permute-start.25
  70.6 19.6 %collective-permute-start.26 = (bf16[32,8192]{1,0:T(8,128)(2,1)S(1)}, bf16[32,8192]{1,0:T(8,128)(2,1)S(1)}, u32[]{:S(2)}, u32[]{:S(2)}) collective-permute-start(bf16[32,8192]{1,0:T(8,128)(2,1)S(1)} %select_select_fusion), channel_id=1, source_target_pairs={{24,12},{25,13},{26,14},{27,15},{28,8},{29,9},{30,10},{31,11},{56,... | collective-permute-start | bytes 1572872 | tf_op jit(solution)/shard_map/cond/branch_1_fun/ppermute | solution.py:348
  90.3 12.7 %collective-permute-start.29 = (bf16[32,8192]{1,0:T(8,128)(2,1)S(1)}, bf16[32,8192]{1,0:T(8,128)(2,1)S(1)}, u32[]{:S(2)}, u32[]{:S(2)}) collective-permute-start(bf16[32,8192]{1,0:T(8,128)(2,1)S(1)} %broadcast_select_fusion.refs_0_), channel_id=1, source_target_pairs={{0,1},{1,2},{2,3},{3,0},{4,5},{5,6},{6,7},{7,4},{8,9},{9,10},{10,1... | collective-permute-start | bytes 1572872 | tf_op jit(solution)/shard_map/cond/branch_1_fun/ppermute | solution.py:44
  90.6 13.2 %collective-permute-start.31 = (bf16[32,8192]{1,0:T(8,128)(2,1)S(1)}, bf16[32,8192]{1,0:T(8,128)(2,1)S(1)}, u32[]{:S(2)}, u32[]{:S(2)}) collective-permute-start(bf16[32,8192]{1,0:T(8,128)(2,1)S(1)} %broadcast_select_fusion.refs_0_), channel_id=1, source_target_pairs={{0,3},{1,0},{2,1},{3,2},{4,7},{5,4},{6,5},{7,6},{8,11},{9,8},{10,9... | collective-permute-start | bytes 1572872 | tf_op jit(solution)/shard_map/cond/branch_1_fun/ppermute | solution.py:44
  93.5 13.1 %collective-permute-start.27 = (bf16[32,8192]{1,0:T(8,128)(2,1)S(1)}, bf16[32,8192]{1,0:T(8,128)(2,1)S(1)}, u32[]{:S(2)}, u32[]{:S(2)}) collective-permute-start(bf16[32,8192]{1,0:T(8,128)(2,1)S(1)} %broadcast_select_fusion.refs_0_), channel_id=1, source_target_pairs={{0,4},{1,5},{2,6},{3,7},{4,0},{5,1},{6,2},{7,3},{8,12},{9,13},{10,... | collective-permute-start | bytes 1572872 | tf_op jit(solution)/shard_map/cond/branch_1_fun/ppermute | solution.py:44
  103.1 6.5 %collective-permute-start.30 = (bf16[16,8192]{1,0:T(8,128)(2,1)S(1)}, bf16[16,8192]{1,0:T(8,128)(2,1)S(1)}, u32[]{:S(2)}, u32[]{:S(2)}) collective-permute-start(bf16[16,8192]{1,0:T(8,128)(2,1)S(1)} %slice.72), channel_id=1, source_target_pairs={{0,1},{1,2},{2,3},{3,0},{4,5},{5,6},{6,7},{7,4},{8,9},{9,10},{10,1... | collective-permute-start | bytes 786440 | tf_op jit(solution)/shard_map/cond/branch_1_fun/ppermute | solution.py:44
  103.9 6.0 %collective-permute-start.32 = (bf16[16,8192]{1,0:T(8,128)(2,1)S(1)}, bf16[16,8192]{1,0:T(8,128)(2,1)S(1)}, u32[]{:S(2)}, u32[]{:S(2)}) collective-permute-start(bf16[16,8192]{1,0:T(8,128)(2,1)S(1)} %slice.73), channel_id=1, source_target_pairs={{0,3},{1,0},{2,1},{3,2},{4,7},{5,4},{6,5},{7,6},{8,11},{9,8},{10,9... | collective-permute-start | bytes 786440 | tf_op jit(solution)/shard_map/cond/branch_1_fun/ppermute | solution.py:44
  106.6 11.1 %collective-permute-start.28 = (bf16[32,8192]{1,0:T(8,128)(2,1)S(1)}, bf16[32,8192]{1,0:T(8,128)(2,1)S(1)}, u32[]{:S(2)}, u32[]{:S(2)}) collective-permute-start(bf16[32,8192]{1,0:T(8,128)(2,1)S(1)} %collective-permute-done.27.refs_0_), channel_id=1, source_target_pairs={{0,3},{1,0},{2,1},{3,2},{4,7},{5,4},{6,5},{7,6},{8,11},{9,8},{10,9... | collective-permute-start | bytes 1572872 | tf_op jit(solution)/shard_map/cond/branch_1_fun/ppermute | solution.py:44
  106.7 11.0 %collective-permute-start.34 = (bf16[32,8192]{1,0:T(8,128)(2,1)S(1)}, bf16[32,8192]{1,0:T(8,128)(2,1)}, u32[]{:S(2)}, u32[]{:S(2)}) collective-permute-start(bf16[32,8192]{1,0:T(8,128)(2,1)S(1)} %collective-permute-done.27.refs_0_), channel_id=1, source_target_pairs={{0,1},{1,2},{2,3},{3,0},{4,5},{5,6},{6,7},{7,4},{8,9},{9,10},{10,1... | collective-permute-start | bytes 1572872 | tf_op jit(solution)/shard_map/cond/branch_1_fun/ppermute | solution.py:44
  109.9 8.8 %collective-permute-start.33 = (bf16[32,8192]{1,0:T(8,128)(2,1)S(1)}, bf16[32,8192]{1,0:T(8,128)(2,1)}, u32[]{:S(2)}, u32[]{:S(2)}) collective-permute-start(bf16[32,8192]{1,0:T(8,128)(2,1)S(1)} %constant_dynamic-update-slice_fusion.2.refs_2_), channel_id=1, source_target_pairs={{0,4},{1,5},{2,6},{3,7},{4,0},{5,1},{6,2},{7,3},{8,12},{9,13},{10,... | collective-permute-start | bytes 1572872 | tf_op jit(solution)/shard_map/cond/branch_1_fun/ppermute | solution.py:44
  123.6 23.0 %collective-permute-start.43 = (bf16[1,32,8192]{2,1,0:T(8,128)(2,1)}, bf16[1,32,8192]{2,1,0:T(8,128)(2,1)S(1)}, u32[]{:S(2)}, u32[]{:S(2)}) collective-permute-start(bf16[1,32,8192]{2,1,0:T(8,128)(2,1)} %bitcast.12), channel_id=1, source_target_pairs={{0,8},{8,16},{16,24},{24,32},{32,40},{40,48},{48,56},{56,64},{64,7... | collective-permute-start | bytes 1572872 | tf_op jit(solution)/shard_map/ppermute | solution.py:48
  (1 other events, 6.3 us)

commit v6 on v5

--- a/solution.py
+++ b/solution.py
@@ -65,19 +65,6 @@
 
 def gather_rows(own):
     return gather_rest(own, gather_first(own))
-
-
-def gather_rows_split(own):
-    from_x = over_tensor(own, TO_X)
-    below = over_tensor(own, TO_UP)
-    above = over_tensor(own, TO_DOWN)
-    far_a = over_tensor(below[:HALF], TO_UP)
-    far_b = over_tensor(above[HALF:], TO_DOWN)
-    x_below = over_tensor(from_x, TO_UP)
-    x_above = over_tensor(from_x, TO_DOWN)
-    far = jnp.concatenate([far_a, far_b])
-    x_far = over_tensor(far, TO_X)
-    return own, above, far, below, from_x, x_above, x_far, x_below
 
 
 def gather_pairs(own):
@@ -396,7 +383,7 @@
         inside = (local >= 0) & (local < VL)
         want = jnp.max(jnp.where(inside, local + jnp.arange(2)[None, :] * VL, -1), axis=1)
         want = jnp.broadcast_to(want[:, None], (2 * MB, 128))
-        all_rows = gather_rows_split(spread_from_last(final_rows, section))
+        all_rows = gather_rows(spread_from_last(final_rows, section))
         return layer_out, vocab(order, all_rows, w_vocab, other_vocab, want)
 
     def even_path():

time: 148 us -> 147 us (level)
  waiting for transfers between devices: 58.7 us -> 64 us
  starting transfers between devices: 36.2 us -> 33.1 us
  blocking collectives: 19.5 us -> 16.5 us
    ppermute x23 -> x22, waiting for transfers between devices: 40.4 us -> 45.7 us  [over_tensor(): return lax.ppermute(block, 'tensor', pairs)]
    ppermute x23 -> x22, starting transfers between devices: 29.5 us -> 26.3 us  [over_tensor(): return lax.ppermute(block, 'tensor', pairs)]
    all_to_all x1, blocking collectives: 19.5 us -> 16.5 us  [body(): got = lax.all_to_all(stats, ('section', 'tensor'), 0, 0, tiled=True)]
  transfers between devices with their start and end apart: 29 -> 28, of which waited for: 13 -> 12; matrix products, arithmetic and copies ran while one was open for 4% -> 4% of each run, Pallas kernels for 6% -> 6%
where the time goes in v6:
time: 147 us; the launch traced here: 146 us
  waiting for transfers between devices  64 us (44%)
  starting transfers between devices  33.1 us (23%)
  Pallas kernels  24.5 us (17%)
  blocking collectives  16.5 us (11%)
  other arithmetic  3.55 us (2%)
  local copies, waits for them, and re-layouts  3.18 us (2%)
    ppermute x22, waiting for transfers between devices, over_tensor(): return lax.ppermute(block, 'tensor', pairs)  45.7 us
    ppermute x22, starting transfers between devices, over_tensor(): return lax.ppermute(block, 'tensor', pairs)  26.3 us
    ppermute x1, waiting for transfers between devices, spread_from_last(): lax.ppermute(rows, ('section', 'tensor'), here)  18.3 us
    all_to_all x1, blocking collectives, body(): got = lax.all_to_all(stats, ('section', 'tensor'), 0, 0, tiled=True)  16.5 us
    pallas_call x1, Pallas kernels, layer(): pl.pallas_call(functools.partial(layer_kernel, layout), out_shape=[jax.Sh...  10.5 us
    pallas_call x2, Pallas kernels, vocab_part(): pl.pallas_call(functools.partial(vocab_kernel, NZ * len(given)), out_shap...  9.85 us
    ppermute x5, starting transfers between devices, over_section(): return lax.ppermute(block, 'section', pairs)  5.49 us
  transfers between devices with their start and end apart: 28, of which 12 were waited for; matrix products, arithmetic and copies ran while one was open for 4% of the time, Pallas kernels for 6%

profile of v6, /device:TPU:1, one launch (start us, length us, event | category | flops | bytes accessed | tf_op | source)
XLA Modules:
  0.0 146.4 jit_solution(3636239389073535152)
XLA Ops:
  0.7 1.5 %collective-permute-start.41 = (bf16[8192,256]{1,0:T(8,128)(2,1)}, bf16[8192,256]{1,0:T(8,128)(2,1)}, u32[]{:S(2)}, u32[]{:S(2)}) collective-permute-start(bf16[8192,256]{1,0:T(8,128)(2,1)} %param.22), channel_id=1, source_target_pairs={{0,8},{8,0},{16,24},{24,16},{32,40},{40,32},{48,56},{56,48},{64,72... | collective-permute-start | bytes 12582920 | tf_op jit(solution)/shard_map/ppermute | solution.py:48
  2.2 1.4 norm.1
  3.6 28.7 %conditional.6 = (bf16[32,8192]{1,0:T(8,128)(2,1)}, bf16[32,8192]{1,0:T(8,128)(2,1)}, bf16[32,8192]{1,0:T(8,128)(2,1)}, bf16[32,8192]{1,0:T(8,128)(2,1)}, bf16[3...) conditional(s32[]{:T(128)} %convert_element_type.122, ...), branch_computations={%region_0.2_spmd, %region_1.3_spmd} | conditional | flops 231513 | bytes 15493352
  3.6 1.8 %collective-permute-start.35 = (bf16[32,8192]{1,0:T(8,128)(2,1)S(1)}, bf16[32,8192]{1,0:T(8,128)(2,1)}, u32[]{:S(2)}, u32[]{:S(2)}) collective-permute-start(bf16[32,8192]{1,0:T(8,128)(2,1)S(1)} %get-tuple-element.106), channel_id=1, source_target_pairs={{0,1},{1,2},{2,3},{3,0},{4,5},{5,6},{6,7},{7,4},{8,9},{9,10},{10,1... | collective-permute-start | bytes 1572872 | tf_op jit(solution)/shard_map/cond/branch_1_fun/ppermute | solution.py:44
  6.6 2.2 %collective-permute-start.34 = (bf16[32,8192]{1,0:T(8,128)(2,1)S(1)}, bf16[32,8192]{1,0:T(8,128)(2,1)}, u32[]{:S(2)}, u32[]{:S(2)}) collective-permute-start(bf16[32,8192]{1,0:T(8,128)(2,1)S(1)} %get-tuple-element.106), channel_id=1, source_target_pairs={{0,3},{1,0},{2,1},{3,2},{4,7},{5,4},{6,5},{7,6},{8,11},{9,8},{10,9... | collective-permute-start | bytes 1572872 | tf_op jit(solution)/shard_map/cond/branch_1_fun/ppermute | solution.py:44
  9.6 1.3 reduce.7
  11.9 2.3 %collective-permute-done.35 = bf16[32,8192]{1,0:T(8,128)(2,1)} collective-permute-done((bf16[32,8192]{1,0:T(8,128)(2,1)S(1)}, bf16[32,8192]{1,0:T(8,128)(2,1)}, u32[]{:S(2)}, u32[]{:S(2)}) %collective-permute-start.35) | collective-permute-done | bytes 524320 | tf_op jit(solution)/shard_map/cond/branch_1_fun/ppermute | solution.py:44
  14.3 2.7 %collective-permute-start.38 = (bf16[32,8192]{1,0:T(8,128)(2,1)}, bf16[32,8192]{1,0:T(8,128)(2,1)}, u32[]{:S(2)}, u32[]{:S(2)}) collective-permute-start(bf16[32,8192]{1,0:T(8,128)(2,1)} %collective-permute-done.37), channel_id=1, source_target_pairs={{0,3},{1,0},{2,1},{3,2},{4,7},{5,4},{6,5},{7,6},{8,11},{9,8},{10,9... | collective-permute-start | bytes 1572872 | tf_op jit(solution)/shard_map/cond/branch_1_fun/ppermute | solution.py:44
  17.0 6.8 %collective-permute-done.36 = bf16[32,8192]{1,0:T(8,128)(2,1)} collective-permute-done((bf16[32,8192]{1,0:T(8,128)(2,1)}, bf16[32,8192]{1,0:T(8,128)(2,1)}, u32[]{:S(2)}, u32[]{:S(2)}) %collective-permute-start.36) | collective-permute-done | bytes 524320 | tf_op jit(solution)/shard_map/cond/branch_1_fun/ppermute | solution.py:44
  25.8 5.0 %collective-permute-done.40 = bf16[32,8192]{1,0:T(8,128)(2,1)} collective-permute-done((bf16[32,8192]{1,0:T(8,128)(2,1)}, bf16[32,8192]{1,0:T(8,128)(2,1)}, u32[]{:S(2)}, u32[]{:S(2)}) %collective-permute-start.40) | collective-permute-done | bytes 524320 | tf_op jit(solution)/shard_map/cond/branch_1_fun/ppermute | solution.py:44
  30.8 1.5 %collective-permute-done.39 = bf16[32,8192]{1,0:T(8,128)(2,1)} collective-permute-done((bf16[32,8192]{1,0:T(8,128)(2,1)}, bf16[32,8192]{1,0:T(8,128)(2,1)}, u32[]{:S(2)}, u32[]{:S(2)}) %collective-permute-start.39) | collective-permute-done | bytes 524320 | tf_op jit(solution)/shard_map/cond/branch_1_fun/ppermute | solution.py:44
  32.3 93.3 %conditional.5 = (bf16[32,8192]{1,0:T(8,128)(2,1)}, f32[128,128]{1,0:T(8,128)}) conditional(s32[]{:T(128)} %convert_element_type.122, (bf16[32,8192]{1,0:T(8,128)(2,1)S(1)}, bf16[8192,512]{1,0:T(8,128)(2,1)}, bf16[8192,256]{1,0:T(8,128)(2,1)}, bf16[512,8192]{1,0:T(8,128)(2,1)}, f32[256,128]{1,0:T(8,128)S(1)}, /*index=5*/f32[256,128]{1,0:T(8,128)S(1)}, ...), branch_computations={%region_2.4_spmd, %region_3.6_spmd} | conditional | flops 8006819840 | bytes 117621320 | solution.py:392
  32.6 10.5 %layer.3 = (bf16[32,8192]{1,0:T(8,128)(2,1)S(1)}, bf16[32,8192]{1,0:T(8,128)(2,1)S(1)}, bf16[32,8192]{1,0:T(8,128)(2,1)S(1)}, bf16[32,8192]{1,0:T(8,128)(2,1)S(1...) custom-call(bf16[32,8192]{1,0:T(8,128)(2,1)S(1)} %get-tuple-element., ...), custom_call_target="tpu_custom_call" | custom-call | flops 6000000000 | bytes 29360128 | tf_op jit(solution)/shard_map/cond/branch_1_fun/layer/pallas_call | solution.py:226
  44.4 2.7 %collective-permute-start.16 = (bf16[32,8192]{1,0:T(8,128)(2,1)S(1)}, bf16[32,8192]{1,0:T(8,128)(2,1)S(1)}, u32[]{:S(2)}, u32[]{:S(2)}) collective-permute-start(bf16[32,8192]{1,0:T(8,128)(2,1)S(1)} %get-tuple-element.146), channel_id=1, source_target_pairs={{0,3},{1,0},{2,1},{3,2},{4,7},{5,4},{6,5},{7,6},{8,11},{9,8},{10,9... | collective-permute-start | bytes 1572872 | tf_op jit(solution)/shard_map/cond/branch_1_fun/ppermute | solution.py:44
  47.1 4.1 %collective-permute-done.18 = bf16[32,8192]{1,0:T(8,128)(2,1)S(1)} collective-permute-done((bf16[32,8192]{1,0:T(8,128)(2,1)S(1)}, bf16[32,8192]{1,0:T(8,128)(2,1)S(1)}, u32[]{:S(2)}, u32[]{:S(2)}) %collective-permute-start.18) | collective-permute-done | bytes 524320 | tf_op jit(solution)/shard_map/cond/branch_1_fun/ppermute | solution.py:44
  51.4 2.7 %collective-permute-start.19 = (bf16[16,8192]{1,0:T(8,128)(2,1)S(1)}, bf16[16,8192]{1,0:T(8,128)(2,1)S(1)}, u32[]{:S(2)}, u32[]{:S(2)}) collective-permute-start(bf16[16,8192]{1,0:T(8,128)(2,1)S(1)} %get-tuple-element.204), channel_id=1, source_target_pairs={{0,3},{1,0},{2,1},{3,2},{4,7},{5,4},{6,5},{7,6},{8,11},{9,8},{10,9... | collective-permute-start | bytes 786440 | tf_op jit(solution)/shard_map/cond/branch_1_fun/ppermute | solution.py:44
  55.5 2.3 %collective-permute-done.21 = bf16[16,8192]{1,0:T(8,128)(2,1)S(1)} collective-permute-done((bf16[16,8192]{1,0:T(8,128)(2,1)S(1)}, bf16[16,8192]{1,0:T(8,128)(2,1)S(1)}, u32[]{:S(2)}, u32[]{:S(2)}) %collective-permute-start.21) | collective-permute-done | bytes 262176 | tf_op jit(solution)/shard_map/cond/branch_1_fun/ppermute | solution.py:44
  58.1 2.7 %collective-permute-start.20 = (bf16[32,8192]{1,0:T(8,128)(2,1)S(1)}, bf16[32,8192]{1,0:T(8,128)(2,1)S(1)}, u32[]{:S(2)}, u32[]{:S(2)}) collective-permute-start(bf16[32,8192]{1,0:T(8,128)(2,1)S(1)} %pad_maximum_fusion.2), channel_id=1, source_target_pairs={{0,3},{1,0},{2,1},{3,2},{4,7},{5,4},{6,5},{7,6},{8,11},{9,8},{10,9... | collective-permute-start | bytes 1572872 | tf_op jit(solution)/shard_map/cond/branch_1_fun/ppermute | solution.py:44
  60.9 2.7 %collective-permute-done.17.b_ref = bf16[32,8192]{1,0:T(8,128)(2,1)S(1)} collective-permute-done((bf16[32,8192]{1,0:T(8,128)(2,1)S(1)}, bf16[32,8192]{1,0:T(8,128)(2,1)S(1)}, u32[]{:S(2)}, u32[]{:S(2)}) %collective-permute-start.17) | collective-permute-done | bytes 524320 | tf_op jit(solution)/shard_map/cond/branch_1_fun/ppermute | solution.py:44
  63.5 3.7 %collective-permute-done.22.d_ref = bf16[32,8192]{1,0:T(8,128)(2,1)S(1)} collective-permute-done((bf16[32,8192]{1,0:T(8,128)(2,1)S(1)}, bf16[32,8192]{1,0:T(8,128)(2,1)S(1)}, u32[]{:S(2)}, u32[]{:S(2)}) %collective-permute-start.22) | collective-permute-done | bytes 524320 | tf_op jit(solution)/shard_map/cond/branch_1_fun/ppermute | solution.py:44
  70.6 1.3 collective-permute-start.26
  72.0 18.3 %collective-permute-done.26 = bf16[32,8192]{1,0:T(8,128)(2,1)S(1)} collective-permute-done((bf16[32,8192]{1,0:T(8,128)(2,1)S(1)}, bf16[32,8192]{1,0:T(8,128)(2,1)S(1)}, u32[]{:S(2)}, u32[]{:S(2)}) %collective-permute-start.26) | collective-permute-done | bytes 524320 | tf_op jit(solution)/shard_map/cond/branch_1_fun/ppermute | solution.py:335
  91.0 12.1 %collective-permute-done.29.refs_3_ = bf16[32,8192]{1,0:T(8,128)(2,1)S(1)} collective-permute-done((bf16[32,8192]{1,0:T(8,128)(2,1)S(1)}, bf16[32,8192]{1,0:T(8,128)(2,1)S(1)}, u32[]{:S(2)}, u32[]{:S(2)}) %collective-permute-start.29) | collective-permute-done | bytes 524320 | tf_op jit(solution)/shard_map/cond/branch_1_fun/ppermute | solution.py:44
  103.1 2.7 %collective-permute-start.33 = (bf16[32,8192]{1,0:T(8,128)(2,1)S(1)}, bf16[32,8192]{1,0:T(8,128)(2,1)S(1)}, u32[]{:S(2)}, u32[]{:S(2)}) collective-permute-start(bf16[32,8192]{1,0:T(8,128)(2,1)S(1)} %broadcast_select_fusion.refs_0_), channel_id=1, source_target_pairs={{0,3},{1,0},{2,1},{3,2},{4,7},{5,4},{6,5},{7,6},{8,11},{9,8},{10,9... | collective-permute-start | bytes 1572872 | tf_op jit(solution)/shard_map/cond/branch_1_fun/ppermute | solution.py:44
  106.5 1.4 collective-permute-start.32
  107.9 4.4 %collective-permute-done.30.refs_2_ = bf16[32,8192]{1,0:T(8,128)(2,1)S(1)} collective-permute-done((bf16[32,8192]{1,0:T(8,128)(2,1)S(1)}, bf16[32,8192]{1,0:T(8,128)(2,1)S(1)}, u32[]{:S(2)}, u32[]{:S(2)}) %collective-permute-start.30) | collective-permute-done | bytes 524320 | tf_op jit(solution)/shard_map/cond/branch_1_fun/ppermute | solution.py:44
  112.3 1.7 %collective-permute-start.31 = (bf16[32,8192]{1,0:T(8,128)(2,1)S(1)}, bf16[32,8192]{1,0:T(8,128)(2,1)}, u32[]{:S(2)}, u32[]{:S(2)}) collective-permute-start(bf16[32,8192]{1,0:T(8,128)(2,1)S(1)} %collective-permute-done.30.refs_2_), channel_id=1, source_target_pairs={{0,4},{1,5},{2,6},{3,7},{4,0},{5,1},{6,2},{7,3},{8,12},{9,13},{10,... | collective-permute-start | bytes 1572872 | tf_op jit(solution)/shard_map/cond/branch_1_fun/ppermute | solution.py:44
  114.5 5.2 %vocab.2.refs_7_ = f32[8,128]{1,0:T(8,128)S(1)} custom-call(s32[8]{0:T(128)S(1)} %add.172.order_ref, bf16[32,8192]{1,0:T(8,128)(2,1)S(1)} %broadcast_select_fusion.refs_0_, bf16[32,8192]{1,0:T(8,128)(2,1)S(1)} %collective-permute-done.33.refs_1_, bf16[32,8192]{1,0:T(8,128)(2,1)S(1)} %collective-permute-done.30.refs_2_, ...), custom_call_target="tpu_custom_call" | custom-call | flops 1000000000 | bytes 10485760 | tf_op jit(solution)/shard_map/cond/branch_1_fun/vocab/pallas_call | solution.py:296
  120.7 4.6 %vocab.3 = f32[128,128]{1,0:T(8,128)} custom-call(s32[8]{0:T(128)S(1)} %add.172.order_ref, bf16[32,8192]{1,0:T(8,128)(2,1)S(1)} %collective-permute-done.27.refs_0_, bf16[32,8192]{1,0:T(8,128)(2,1)S(1)} %collective-permute-done.28.refs_1_, bf16[32,8192]{1,0:T(8,128)(2,1)} %collective-permute-done.31.refs_2_, ...), custom_call_target="tpu_custom_call" | custom-call | flops 1000000000 | bytes 10485760 | tf_op jit(solution)/shard_map/cond/branch_1_fun/vocab/pallas_call | solution.py:296
  125.6 1.9 %collective-permute-start.42 = (bf16[1,32,8192]{2,1,0:T(8,128)(2,1)}, bf16[1,32,8192]{2,1,0:T(8,128)(2,1)S(1)}, u32[]{:S(2)}, u32[]{:S(2)}) collective-permute-start(bf16[1,32,8192]{2,1,0:T(8,128)(2,1)} %bitcast.12), channel_id=1, source_target_pairs={{0,8},{8,16},{16,24},{24,32},{32,40},{40,48},{48,56},{56,64},{64,7... | collective-permute-start | bytes 1572872 | tf_op jit(solution)/shard_map/ppermute | solution.py:48
  127.6 16.5 %all_to_all.11 = f32[128,1,128]{2,1,0:T(1,128)} all-to-all(f32[128,1,128]{2,1,0:T(1,128)} %bitcast.13), channel_id=1, replica_groups=mesh['section'=16,'tensor'=8] {'section','tensor'}, dimensions={0} | all-to-all | bytes 131072 | tf_op jit(solution)/shard_map/all_to_all | solution.py:394
  144.0 1.6 %merge.1 = f32[32]{0:T(128)} custom-call(f32[128,128]{1,0:T(8,128)} %bitcast.24), custom_call_target="tpu_custom_call" | custom-call | tf_op jit(solution)/shard_map/merge/pallas_call | solution.py:139
  (90 shorter events, 15.2 us)
Async XLA Ops:
  0.6 31.7 %copy-start.1 = (bf16[1,32,8192]{2,1,0:T(8,128)(2,1)S(1)}, bf16[1,32,8192]{2,1,0:T(8,128)(2,1)}, u32[]{:S(2)}) copy-start(bf16[1,32,8192]{2,1,0:T(8,128)(2,1)} %param.15) | copy-start | bytes 1572868
  0.6 31.7 %copy-start.4 = (bf16[8192]{0:T(1024)(128)(2,1)S(1)}, bf16[8192]{0:T(1024)(128)(2,1)}, u32[]{:S(2)}) copy-start(bf16[8192]{0:T(1024)(128)(2,1)} %param.21) | copy-start | bytes 49156
  0.7 31.7 %copy-start.5 = (s32[256]{0:T(256)S(1)}, s32[256]{0:T(256)}, u32[]{:S(2)}) copy-start(s32[256]{0:T(256)} %param.23) | copy-start | bytes 3076
  0.7 31.6 %collective-permute-start.41 = (bf16[8192,256]{1,0:T(8,128)(2,1)}, bf16[8192,256]{1,0:T(8,128)(2,1)}, u32[]{:S(2)}, u32[]{:S(2)}) collective-permute-start(bf16[8192,256]{1,0:T(8,128)(2,1)} %param.22), channel_id=1, source_target_pairs={{0,8},{8,0},{16,24},{24,16},{32,40},{40,32},{48,56},{56,48},{64,72... | collective-permute-start | bytes 12582920 | tf_op jit(solution)/shard_map/ppermute | solution.py:48
  3.6 10.6 %collective-permute-start.35 = (bf16[32,8192]{1,0:T(8,128)(2,1)S(1)}, bf16[32,8192]{1,0:T(8,128)(2,1)}, u32[]{:S(2)}, u32[]{:S(2)}) collective-permute-start(bf16[32,8192]{1,0:T(8,128)(2,1)S(1)} %get-tuple-element.106), channel_id=1, source_target_pairs={{0,1},{1,2},{2,3},{3,0},{4,5},{5,6},{6,7},{7,4},{8,9},{9,10},{10,1... | collective-permute-start | bytes 1572872 | tf_op jit(solution)/shard_map/cond/branch_1_fun/ppermute | solution.py:44
  5.4 8.9 %collective-permute-start.37 = (bf16[32,8192]{1,0:T(8,128)(2,1)S(1)}, bf16[32,8192]{1,0:T(8,128)(2,1)}, u32[]{:S(2)}, u32[]{:S(2)}) collective-permute-start(bf16[32,8192]{1,0:T(8,128)(2,1)S(1)} %get-tuple-element.106), channel_id=1, source_target_pairs={{0,4},{1,5},{2,6},{3,7},{4,0},{5,1},{6,2},{7,3},{8,12},{9,13},{10,... | collective-permute-start | bytes 1572872 | tf_op jit(solution)/shard_map/cond/branch_1_fun/ppermute | solution.py:44
  6.6 19.2 %collective-permute-start.34 = (bf16[32,8192]{1,0:T(8,128)(2,1)S(1)}, bf16[32,8192]{1,0:T(8,128)(2,1)}, u32[]{:S(2)}, u32[]{:S(2)}) collective-permute-start(bf16[32,8192]{1,0:T(8,128)(2,1)S(1)} %get-tuple-element.106), channel_id=1, source_target_pairs={{0,3},{1,0},{2,1},{3,2},{4,7},{5,4},{6,5},{7,6},{8,11},{9,8},{10,9... | collective-permute-start | bytes 1572872 | tf_op jit(solution)/shard_map/cond/branch_1_fun/ppermute | solution.py:44
  14.2 9.6 %collective-permute-start.36 = (bf16[32,8192]{1,0:T(8,128)(2,1)}, bf16[32,8192]{1,0:T(8,128)(2,1)}, u32[]{:S(2)}, u32[]{:S(2)}) collective-permute-start(bf16[32,8192]{1,0:T(8,128)(2,1)} %collective-permute-done.35), channel_id=1, source_target_pairs={{0,1},{1,2},{2,3},{3,0},{4,5},{5,6},{6,7},{7,4},{8,9},{9,10},{10,1... | collective-permute-start | bytes 1572872 | tf_op jit(solution)/shard_map/cond/branch_1_fun/ppermute | solution.py:44
  14.3 11.5 %collective-permute-start.38 = (bf16[32,8192]{1,0:T(8,128)(2,1)}, bf16[32,8192]{1,0:T(8,128)(2,1)}, u32[]{:S(2)}, u32[]{:S(2)}) collective-permute-start(bf16[32,8192]{1,0:T(8,128)(2,1)} %collective-permute-done.37), channel_id=1, source_target_pairs={{0,3},{1,0},{2,1},{3,2},{4,7},{5,4},{6,5},{7,6},{8,11},{9,8},{10,9... | collective-permute-start | bytes 1572872 | tf_op jit(solution)/shard_map/cond/branch_1_fun/ppermute | solution.py:44
  17.0 13.8 %collective-permute-start.40 = (bf16[32,8192]{1,0:T(8,128)(2,1)}, bf16[32,8192]{1,0:T(8,128)(2,1)}, u32[]{:S(2)}, u32[]{:S(2)}) collective-permute-start(bf16[32,8192]{1,0:T(8,128)(2,1)} %collective-permute-done.37), channel_id=1, source_target_pairs={{0,1},{1,2},{2,3},{3,0},{4,5},{5,6},{6,7},{7,4},{8,9},{9,10},{10,1... | collective-permute-start | bytes 1572872 | tf_op jit(solution)/shard_map/cond/branch_1_fun/ppermute | solution.py:44
  23.8 8.5 %collective-permute-start.39 = (bf16[32,8192]{1,0:T(8,128)(2,1)}, bf16[32,8192]{1,0:T(8,128)(2,1)}, u32[]{:S(2)}, u32[]{:S(2)}) collective-permute-start(bf16[32,8192]{1,0:T(8,128)(2,1)} %collective-permute-done.36), channel_id=1, source_target_pairs={{0,4},{1,5},{2,6},{3,7},{4,0},{5,1},{6,2},{7,3},{8,12},{9,13},{10,... | collective-permute-start | bytes 1572872 | tf_op jit(solution)/shard_map/cond/branch_1_fun/ppermute | solution.py:44
  43.1 8.1 %collective-permute-start.18 = (bf16[32,8192]{1,0:T(8,128)(2,1)S(1)}, bf16[32,8192]{1,0:T(8,128)(2,1)S(1)}, u32[]{:S(2)}, u32[]{:S(2)}) collective-permute-start(bf16[32,8192]{1,0:T(8,128)(2,1)S(1)} %get-tuple-element.149), channel_id=1, source_target_pairs={{0,4},{1,5},{2,6},{3,7},{4,0},{5,1},{6,2},{7,3},{8,12},{9,13},{10,... | collective-permute-start | bytes 1572872 | tf_op jit(solution)/shard_map/cond/branch_1_fun/ppermute | solution.py:44
  44.3 9.7 %collective-permute-start.15 = (bf16[32,8192]{1,0:T(8,128)(2,1)S(1)}, bf16[32,8192]{1,0:T(8,128)(2,1)S(1)}, u32[]{:S(2)}, u32[]{:S(2)}) collective-permute-start(bf16[32,8192]{1,0:T(8,128)(2,1)S(1)} %get-tuple-element.145), channel_id=1, source_target_pairs={{0,1},{1,2},{2,3},{3,0},{4,5},{5,6},{6,7},{7,4},{8,9},{9,10},{10,1... | collective-permute-start | bytes 1572872 | tf_op jit(solution)/shard_map/cond/branch_1_fun/ppermute | solution.py:44
  44.4 9.7 %collective-permute-start.16 = (bf16[32,8192]{1,0:T(8,128)(2,1)S(1)}, bf16[32,8192]{1,0:T(8,128)(2,1)S(1)}, u32[]{:S(2)}, u32[]{:S(2)}) collective-permute-start(bf16[32,8192]{1,0:T(8,128)(2,1)S(1)} %get-tuple-element.146), channel_id=1, source_target_pairs={{0,3},{1,0},{2,1},{3,2},{4,7},{5,4},{6,5},{7,6},{8,11},{9,8},{10,9... | collective-permute-start | bytes 1572872 | tf_op jit(solution)/shard_map/cond/branch_1_fun/ppermute | solution.py:44
  51.3 6.5 %collective-permute-start.21 = (bf16[16,8192]{1,0:T(8,128)(2,1)S(1)}, bf16[16,8192]{1,0:T(8,128)(2,1)S(1)}, u32[]{:S(2)}, u32[]{:S(2)}) collective-permute-start(bf16[16,8192]{1,0:T(8,128)(2,1)S(1)} %get-tuple-element.203), channel_id=1, source_target_pairs={{0,1},{1,2},{2,3},{3,0},{4,5},{5,6},{6,7},{7,4},{8,9},{9,10},{10,1... | collective-permute-start | bytes 786440 | tf_op jit(solution)/shard_map/cond/branch_1_fun/ppermute | solution.py:44
  51.4 6.6 %collective-permute-start.19 = (bf16[16,8192]{1,0:T(8,128)(2,1)S(1)}, bf16[16,8192]{1,0:T(8,128)(2,1)S(1)}, u32[]{:S(2)}, u32[]{:S(2)}) collective-permute-start(bf16[16,8192]{1,0:T(8,128)(2,1)S(1)} %get-tuple-element.204), channel_id=1, source_target_pairs={{0,3},{1,0},{2,1},{3,2},{4,7},{5,4},{6,5},{7,6},{8,11},{9,8},{10,9... | collective-permute-start | bytes 786440 | tf_op jit(solution)/shard_map/cond/branch_1_fun/ppermute | solution.py:44
  54.2 9.3 %collective-permute-start.17 = (bf16[32,8192]{1,0:T(8,128)(2,1)S(1)}, bf16[32,8192]{1,0:T(8,128)(2,1)S(1)}, u32[]{:S(2)}, u32[]{:S(2)}) collective-permute-start(bf16[32,8192]{1,0:T(8,128)(2,1)S(1)} %add_convert_fusion.5), channel_id=1, source_target_pairs={{0,4},{1,5},{2,6},{3,7},{4,0},{5,1},{6,2},{7,3},{8,12},{9,13},{10,... | collective-permute-start | bytes 1572872 | tf_op jit(solution)/shard_map/cond/branch_1_fun/ppermute | solution.py:44
  57.9 9.3 %collective-permute-start.22 = (bf16[32,8192]{1,0:T(8,128)(2,1)S(1)}, bf16[32,8192]{1,0:T(8,128)(2,1)S(1)}, u32[]{:S(2)}, u32[]{:S(2)}) collective-permute-start(bf16[32,8192]{1,0:T(8,128)(2,1)S(1)} %pad_maximum_fusion.3), channel_id=1, source_target_pairs={{0,1},{1,2},{2,3},{3,0},{4,5},{5,6},{6,7},{7,4},{8,9},{9,10},{10,1... | collective-permute-start | bytes 1572872 | tf_op jit(solution)/shard_map/cond/branch_1_fun/ppermute | solution.py:44
  58.1 9.1 %collective-permute-start.20 = (bf16[32,8192]{1,0:T(8,128)(2,1)S(1)}, bf16[32,8192]{1,0:T(8,128)(2,1)S(1)}, u32[]{:S(2)}, u32[]{:S(2)}) collective-permute-start(bf16[32,8192]{1,0:T(8,128)(2,1)S(1)} %pad_maximum_fusion.2), channel_id=1, source_target_pairs={{0,3},{1,0},{2,1},{3,2},{4,7},{5,4},{6,5},{7,6},{8,11},{9,8},{10,9... | collective-permute-start | bytes 1572872 | tf_op jit(solution)/shard_map/cond/branch_1_fun/ppermute | solution.py:44
  68.4 2.1 %collective-permute-start.23 = (bf16[32,8192]{1,0:T(8,128)(2,1)S(1)}, bf16[32,8192]{1,0:T(8,128)(2,1)S(1)}, u32[]{:S(2)}, u32[]{:S(2)}) collective-permute-start(bf16[32,8192]{1,0:T(8,128)(2,1)S(1)} %get-tuple-element.156), channel_id=1, source_target_pairs={{120,24},{121,25},{122,26},{123,27},{124,28},{125,29},{126,30},{12... | collective-permute-start | bytes 1572872 | tf_op jit(solution)/shard_map/cond/branch_1_fun/ppermute | solution.py:48
  69.1 1.4 collective-permute-start.24
  69.8 0.7 collective-permute-start.25
  70.6 19.6 %collective-permute-start.26 = (bf16[32,8192]{1,0:T(8,128)(2,1)S(1)}, bf16[32,8192]{1,0:T(8,128)(2,1)S(1)}, u32[]{:S(2)}, u32[]{:S(2)}) collective-permute-start(bf16[32,8192]{1,0:T(8,128)(2,1)S(1)} %select_select_fusion), channel_id=1, source_target_pairs={{24,12},{25,13},{26,14},{27,15},{28,8},{29,9},{30,10},{31,11},{56,... | collective-permute-start | bytes 1572872 | tf_op jit(solution)/shard_map/cond/branch_1_fun/ppermute | solution.py:335
  90.3 12.7 %collective-permute-start.29 = (bf16[32,8192]{1,0:T(8,128)(2,1)S(1)}, bf16[32,8192]{1,0:T(8,128)(2,1)S(1)}, u32[]{:S(2)}, u32[]{:S(2)}) collective-permute-start(bf16[32,8192]{1,0:T(8,128)(2,1)S(1)} %broadcast_select_fusion.refs_0_), channel_id=1, source_target_pairs={{0,1},{1,2},{2,3},{3,0},{4,5},{5,6},{6,7},{7,4},{8,9},{9,10},{10,1... | collective-permute-start | bytes 1572872 | tf_op jit(solution)/shard_map/cond/branch_1_fun/ppermute | solution.py:44
  90.7 15.7 %collective-permute-start.27 = (bf16[32,8192]{1,0:T(8,128)(2,1)S(1)}, bf16[32,8192]{1,0:T(8,128)(2,1)S(1)}, u32[]{:S(2)}, u32[]{:S(2)}) collective-permute-start(bf16[32,8192]{1,0:T(8,128)(2,1)S(1)} %broadcast_select_fusion.refs_0_), channel_id=1, source_target_pairs={{0,4},{1,5},{2,6},{3,7},{4,0},{5,1},{6,2},{7,3},{8,12},{9,13},{10,... | collective-permute-start | bytes 1572872 | tf_op jit(solution)/shard_map/cond/branch_1_fun/ppermute | solution.py:44
  103.1 9.2 %collective-permute-start.30 = (bf16[32,8192]{1,0:T(8,128)(2,1)S(1)}, bf16[32,8192]{1,0:T(8,128)(2,1)S(1)}, u32[]{:S(2)}, u32[]{:S(2)}) collective-permute-start(bf16[32,8192]{1,0:T(8,128)(2,1)S(1)} %collective-permute-done.29.refs_3_), channel_id=1, source_target_pairs={{0,1},{1,2},{2,3},{3,0},{4,5},{5,6},{6,7},{7,4},{8,9},{9,10},{10,1... | collective-permute-start | bytes 1572872 | tf_op jit(solution)/shard_map/cond/branch_1_fun/ppermute | solution.py:44
  103.1 11.3 %collective-permute-start.33 = (bf16[32,8192]{1,0:T(8,128)(2,1)S(1)}, bf16[32,8192]{1,0:T(8,128)(2,1)S(1)}, u32[]{:S(2)}, u32[]{:S(2)}) collective-permute-start(bf16[32,8192]{1,0:T(8,128)(2,1)S(1)} %broadcast_select_fusion.refs_0_), channel_id=1, source_target_pairs={{0,3},{1,0},{2,1},{3,2},{4,7},{5,4},{6,5},{7,6},{8,11},{9,8},{10,9... | collective-permute-start | bytes 1572872 | tf_op jit(solution)/shard_map/cond/branch_1_fun/ppermute | solution.py:44
  106.4 13.3 %collective-permute-start.28 = (bf16[32,8192]{1,0:T(8,128)(2,1)S(1)}, bf16[32,8192]{1,0:T(8,128)(2,1)S(1)}, u32[]{:S(2)}, u32[]{:S(2)}) collective-permute-start(bf16[32,8192]{1,0:T(8,128)(2,1)S(1)} %collective-permute-done.27.refs_0_), channel_id=1, source_target_pairs={{0,3},{1,0},{2,1},{3,2},{4,7},{5,4},{6,5},{7,6},{8,11},{9,8},{10,9... | collective-permute-start | bytes 1572872 | tf_op jit(solution)/shard_map/cond/branch_1_fun/ppermute | solution.py:44
  106.5 13.2 %collective-permute-start.32 = (bf16[32,8192]{1,0:T(8,128)(2,1)S(1)}, bf16[32,8192]{1,0:T(8,128)(2,1)}, u32[]{:S(2)}, u32[]{:S(2)}) collective-permute-start(bf16[32,8192]{1,0:T(8,128)(2,1)S(1)} %collective-permute-done.27.refs_0_), channel_id=1, source_target_pairs={{0,1},{1,2},{2,3},{3,0},{4,5},{5,6},{6,7},{7,4},{8,9},{9,10},{10,1... | collective-permute-start | bytes 1572872 | tf_op jit(solution)/shard_map/cond/branch_1_fun/ppermute | solution.py:44
  112.3 8.4 %collective-permute-start.31 = (bf16[32,8192]{1,0:T(8,128)(2,1)S(1)}, bf16[32,8192]{1,0:T(8,128)(2,1)}, u32[]{:S(2)}, u32[]{:S(2)}) collective-permute-start(bf16[32,8192]{1,0:T(8,128)(2,1)S(1)} %collective-permute-done.30.refs_2_), channel_id=1, source_target_pairs={{0,4},{1,5},{2,6},{3,7},{4,0},{5,1},{6,2},{7,3},{8,12},{9,13},{10,... | collective-permute-start | bytes 1572872 | tf_op jit(solution)/shard_map/cond/branch_1_fun/ppermute | solution.py:44
  114.5 6.3 %copy-start = (bf16[8192,256]{1,0:T(8,128)(2,1)S(1)}, bf16[8192,256]{1,0:T(8,128)(2,1)}, u32[]{:S(2)}) copy-start(bf16[8192,256]{1,0:T(8,128)(2,1)} %get-tuple-element.157.refs_4_) | copy-start | bytes 12582916 | tf_op jit(solution)/shard_map/cond
  125.6 20.0 %collective-permute-start.42 = (bf16[1,32,8192]{2,1,0:T(8,128)(2,1)}, bf16[1,32,8192]{2,1,0:T(8,128)(2,1)S(1)}, u32[]{:S(2)}, u32[]{:S(2)}) collective-permute-start(bf16[1,32,8192]{2,1,0:T(8,128)(2,1)} %bitcast.12), channel_id=1, source_target_pairs={{0,8},{8,16},{16,24},{24,32},{32,40},{40,48},{48,56},{56,64},{64,7... | collective-permute-start | bytes 1572872 | tf_op jit(solution)/shard_map/ppermute | solution.py:48

commit v7 on v6

--- a/solution.py
+++ b/solution.py
@@ -247,9 +247,11 @@
 VC = 2048
 
 
-def vocab_kernel(first, order_ref, *refs):
-    blocks = refs[:NZ]
-    w0_ref, w1_ref, want_ref = refs[NZ : NZ + 3]
+def vocab_kernel(ids, order_ref, *refs):
+    n = len(ids)
+    blocks = refs[:n]
+    w0_ref, w1_ref, want_ref = refs[n : n + 3]
+    last = len(refs) > n + 9
     out_ref, rows, w, acc, row_sem, w_sem = refs[-6:]
     for i, b in enumerate(blocks):
         pltpu.make_async_copy(b, rows.at[pl.ds(i * ROWS, ROWS)], row_sem).start()
@@ -273,47 +275,52 @@
     top = jnp.max(logits, axis=1, keepdims=True)
     total = jnp.sum(jnp.exp(logits - top), axis=1, keepdims=True)
     column = lax.broadcasted_iota(jnp.int32, logits.shape, 1)
-    want = want_ref[first * ROWS : (first + NZ) * ROWS, :1]
+    want = jnp.concatenate([want_ref[i * ROWS : (i + 1) * ROWS, :1] for i in ids], axis=0)
     picked = jnp.sum(jnp.where(column == want, logits, 0.0), axis=1, keepdims=True)
-    lane = lax.broadcasted_iota(jnp.int32, (MB, 128), 1)
-    stats = jnp.where(lane == 0, top, jnp.where(lane == 1, total, picked)).T
-    if first:
-        out_ref[:8, :] = refs[NZ + 3][...]
-    for i in range(NZ):
+    lane = lax.broadcasted_iota(jnp.int32, (n * ROWS, 128), 1)
+    stats = jnp.where(lane == 0, top, jnp.where(lane == 1, total, picked))
+    if n < NZ:
+        stats = jnp.concatenate([stats, jnp.zeros((MB - n * ROWS, 128), F32)], axis=0)
+    if n * ROWS % MB and n > NZ:
+        stats = jnp.concatenate([stats, jnp.zeros((2 * MB - n * ROWS, 128), F32)], axis=0)
+    stats = stats.T
+    if last:
+        out_ref[:8, :] = refs[n + 3][...]
+    for i, block in enumerate(ids):
         mine = slice(i * ROWS, (i + 1) * ROWS)
         line = jnp.concatenate([stats[k : k + 1, mine] for k in (0, 1, 2, 2)], axis=1)
-        out_ref[pl.ds(order_ref[first + i], 1), :] = line
-    if first:
+        out_ref[pl.ds(order_ref[block], 1), :] = line
+    if last:
         lines = out_ref[:8, :]
         for s in range(1, 16):
             out_ref[s * 8 : (s + 1) * 8, :] = lines
 
 
-def vocab_part(order, blocks, w0, w1, want, lines=None):
+def vocab_part(ids, order, blocks, w0, w1, want, lines=None):
     hbm = pl.BlockSpec(memory_space=pl.ANY)
     vmem = pl.BlockSpec(memory_space=pltpu.VMEM)
     given = [] if lines is None else [lines]
     return pl.pallas_call(
-        functools.partial(vocab_kernel, NZ * len(given)),
+        functools.partial(vocab_kernel, ids),
         out_shape=jax.ShapeDtypeStruct((128 if given else 8, 128), F32),
-        in_specs=[pl.BlockSpec(memory_space=pltpu.SMEM)] + [hbm] * (NZ + 2) + [vmem] * (1 + len(given)),
+        in_specs=[pl.BlockSpec(memory_space=pltpu.SMEM)] + [hbm] * (len(ids) + 2) + [vmem] * (1 + len(given)),
         out_specs=vmem,
         scratch_shapes=[
-            pltpu.VMEM((MB, WIDTH), BF16),
+            pltpu.VMEM((len(ids) * ROWS, WIDTH), BF16),
             pltpu.VMEM((WIDTH, 2 * VL), BF16),
-            pltpu.VMEM((MB, 2 * VL), F32),
+            pltpu.VMEM((len(ids) * ROWS, 2 * VL), F32),
             pltpu.SemaphoreType.DMA,
             pltpu.SemaphoreType.DMA((WIDTH // VC,)),
         ],
         compiler_params=pltpu.CompilerParams(vmem_limit_bytes=32 * 1024 * 1024),
         cost_estimate=pl.CostEstimate(flops=10**9, bytes_accessed=10 * 2**20, transcendentals=0),
         name="vocab",
-    )(order, *blocks, w0, w1, want, *given)
+    )(order, *[blocks[i] for i in ids], w0, w1, want, *given)
 
 
 def vocab(order, blocks, w0, w1, want):
-    lines = vocab_part(order, blocks[:NZ], w0, w1, want)
-    return vocab_part(order, blocks[NZ:], w0, w1, want, lines)
+    lines = vocab_part((0, 1, 2, 3, 4), order, blocks, w0, w1, want)
+    return vocab_part((5, 6, 7), order, blocks, w0, w1, want, lines)
 
 
 def add(*terms):

time: 147 us -> 147 us (level)
  no operation moved by 1% of the time
where the time goes in v7:
time: 147 us
  waiting for transfers between devices  64.1 us (44%)
  starting transfers between devices  33.1 us (23%)
  Pallas kernels  24.5 us (17%)
  blocking collectives  16.5 us (11%)
  other arithmetic  3.55 us (2%)
  local copies, waits for them, and re-layouts  3.18 us (2%)
    ppermute x22, waiting for transfers between devices, over_tensor(): return lax.ppermute(block, 'tensor', pairs)  45.8 us
    ppermute x22, starting transfers between devices, over_tensor(): return lax.ppermute(block, 'tensor', pairs)  26.3 us
    ppermute x1, waiting for transfers between devices, spread_from_last(): lax.ppermute(rows, ('section', 'tensor'), here)  18.3 us
    all_to_all x1, blocking collectives, body(): got = lax.all_to_all(stats, ('section', 'tensor'), 0, 0, tiled=True)  16.5 us
    pallas_call x1, Pallas kernels, layer(): pl.pallas_call(functools.partial(layer_kernel, layout), out_shape=[jax.Sh...  10.5 us
    pallas_call x2, Pallas kernels, vocab_part(): pl.pallas_call(functools.partial(vocab_kernel, ids), out_shape=jax.ShapeD...  9.88 us
    ppermute x5, starting transfers between devices, over_section(): return lax.ppermute(block, 'section', pairs)  5.49 us
  transfers between devices with their start and end apart: 28, of which 12 were waited for; matrix products, arithmetic and copies ran while one was open for 4% of the time, Pallas kernels for 6%

profile of v7, /device:TPU:1, one launch (start us, length us, event | category | flops | bytes accessed | tf_op | source)
XLA Modules:
  0.0 146.5 jit_solution(8636464392787852115)
XLA Ops:
  0.7 1.5 %collective-permute-start.41 = (bf16[8192,256]{1,0:T(8,128)(2,1)}, bf16[8192,256]{1,0:T(8,128)(2,1)}, u32[]{:S(2)}, u32[]{:S(2)}) collective-permute-start(bf16[8192,256]{1,0:T(8,128)(2,1)} %param.22), channel_id=1, source_target_pairs={{0,8},{8,0},{16,24},{24,16},{32,40},{40,32},{48,56},{56,48},{64,72... | collective-permute-start | bytes 12582920 | tf_op jit(solution)/shard_map/ppermute | solution.py:48
  2.2 1.4 norm.1
  3.6 28.7 %conditional.6 = (bf16[32,8192]{1,0:T(8,128)(2,1)}, bf16[32,8192]{1,0:T(8,128)(2,1)}, bf16[32,8192]{1,0:T(8,128)(2,1)}, bf16[32,8192]{1,0:T(8,128)(2,1)}, bf16[3...) conditional(s32[]{:T(128)} %convert_element_type.122, ...), branch_computations={%region_0.2_spmd, %region_1.3_spmd} | conditional | flops 231513 | bytes 15493352
  3.6 1.8 %collective-permute-start.35 = (bf16[32,8192]{1,0:T(8,128)(2,1)S(1)}, bf16[32,8192]{1,0:T(8,128)(2,1)}, u32[]{:S(2)}, u32[]{:S(2)}) collective-permute-start(bf16[32,8192]{1,0:T(8,128)(2,1)S(1)} %get-tuple-element.106), channel_id=1, source_target_pairs={{0,1},{1,2},{2,3},{3,0},{4,5},{5,6},{6,7},{7,4},{8,9},{9,10},{10,1... | collective-permute-start | bytes 1572872 | tf_op jit(solution)/shard_map/cond/branch_1_fun/ppermute | solution.py:44
  6.6 2.2 %collective-permute-start.34 = (bf16[32,8192]{1,0:T(8,128)(2,1)S(1)}, bf16[32,8192]{1,0:T(8,128)(2,1)}, u32[]{:S(2)}, u32[]{:S(2)}) collective-permute-start(bf16[32,8192]{1,0:T(8,128)(2,1)S(1)} %get-tuple-element.106), channel_id=1, source_target_pairs={{0,3},{1,0},{2,1},{3,2},{4,7},{5,4},{6,5},{7,6},{8,11},{9,8},{10,9... | collective-permute-start | bytes 1572872 | tf_op jit(solution)/shard_map/cond/branch_1_fun/ppermute | solution.py:44
  9.6 1.3 reduce.7
  11.9 2.3 %collective-permute-done.35 = bf16[32,8192]{1,0:T(8,128)(2,1)} collective-permute-done((bf16[32,8192]{1,0:T(8,128)(2,1)S(1)}, bf16[32,8192]{1,0:T(8,128)(2,1)}, u32[]{:S(2)}, u32[]{:S(2)}) %collective-permute-start.35) | collective-permute-done | bytes 524320 | tf_op jit(solution)/shard_map/cond/branch_1_fun/ppermute | solution.py:44
  14.3 2.7 %collective-permute-start.38 = (bf16[32,8192]{1,0:T(8,128)(2,1)}, bf16[32,8192]{1,0:T(8,128)(2,1)}, u32[]{:S(2)}, u32[]{:S(2)}) collective-permute-start(bf16[32,8192]{1,0:T(8,128)(2,1)} %collective-permute-done.37), channel_id=1, source_target_pairs={{0,3},{1,0},{2,1},{3,2},{4,7},{5,4},{6,5},{7,6},{8,11},{9,8},{10,9... | collective-permute-start | bytes 1572872 | tf_op jit(solution)/shard_map/cond/branch_1_fun/ppermute | solution.py:44
  17.0 6.8 %collective-permute-done.36 = bf16[32,8192]{1,0:T(8,128)(2,1)} collective-permute-done((bf16[32,8192]{1,0:T(8,128)(2,1)}, bf16[32,8192]{1,0:T(8,128)(2,1)}, u32[]{:S(2)}, u32[]{:S(2)}) %collective-permute-start.36) | collective-permute-done | bytes 524320 | tf_op jit(solution)/shard_map/cond/branch_1_fun/ppermute | solution.py:44
  25.8 5.0 %collective-permute-done.40 = bf16[32,8192]{1,0:T(8,128)(2,1)} collective-permute-done((bf16[32,8192]{1,0:T(8,128)(2,1)}, bf16[32,8192]{1,0:T(8,128)(2,1)}, u32[]{:S(2)}, u32[]{:S(2)}) %collective-permute-start.40) | collective-permute-done | bytes 524320 | tf_op jit(solution)/shard_map/cond/branch_1_fun/ppermute | solution.py:44
  30.8 1.5 %collective-permute-done.39 = bf16[32,8192]{1,0:T(8,128)(2,1)} collective-permute-done((bf16[32,8192]{1,0:T(8,128)(2,1)}, bf16[32,8192]{1,0:T(8,128)(2,1)}, u32[]{:S(2)}, u32[]{:S(2)}) %collective-permute-start.39) | collective-permute-done | bytes 524320 | tf_op jit(solution)/shard_map/cond/branch_1_fun/ppermute | solution.py:44
  32.3 93.4 %conditional.5 = (bf16[32,8192]{1,0:T(8,128)(2,1)}, f32[128,128]{1,0:T(8,128)}) conditional(s32[]{:T(128)} %convert_element_type.122, (bf16[32,8192]{1,0:T(8,128)(2,1)S(1)}, bf16[8192,512]{1,0:T(8,128)(2,1)}, bf16[8192,256]{1,0:T(8,128)(2,1)}, bf16[512,8192]{1,0:T(8,128)(2,1)}, f32[256,128]{1,0:T(8,128)S(1)}, /*index=5*/f32[256,128]{1,0:T(8,128)S(1)}, ...), branch_computations={%region_2.4_spmd, %region_3.6_spmd} | conditional | flops 8006819840 | bytes 117621320 | solution.py:399
  32.6 10.5 %layer.3 = (bf16[32,8192]{1,0:T(8,128)(2,1)S(1)}, bf16[32,8192]{1,0:T(8,128)(2,1)S(1)}, bf16[32,8192]{1,0:T(8,128)(2,1)S(1)}, bf16[32,8192]{1,0:T(8,128)(2,1)S(1...) custom-call(bf16[32,8192]{1,0:T(8,128)(2,1)S(1)} %get-tuple-element., ...), custom_call_target="tpu_custom_call" | custom-call | flops 6000000000 | bytes 29360128 | tf_op jit(solution)/shard_map/cond/branch_1_fun/layer/pallas_call | solution.py:226
  44.4 2.7 %collective-permute-start.16 = (bf16[32,8192]{1,0:T(8,128)(2,1)S(1)}, bf16[32,8192]{1,0:T(8,128)(2,1)S(1)}, u32[]{:S(2)}, u32[]{:S(2)}) collective-permute-start(bf16[32,8192]{1,0:T(8,128)(2,1)S(1)} %get-tuple-element.146), channel_id=1, source_target_pairs={{0,3},{1,0},{2,1},{3,2},{4,7},{5,4},{6,5},{7,6},{8,11},{9,8},{10,9... | collective-permute-start | bytes 1572872 | tf_op jit(solution)/shard_map/cond/branch_1_fun/ppermute | solution.py:44
  47.1 4.1 %collective-permute-done.18 = bf16[32,8192]{1,0:T(8,128)(2,1)S(1)} collective-permute-done((bf16[32,8192]{1,0:T(8,128)(2,1)S(1)}, bf16[32,8192]{1,0:T(8,128)(2,1)S(1)}, u32[]{:S(2)}, u32[]{:S(2)}) %collective-permute-start.18) | collective-permute-done | bytes 524320 | tf_op jit(solution)/shard_map/cond/branch_1_fun/ppermute | solution.py:44
  51.4 2.7 %collective-permute-start.19 = (bf16[16,8192]{1,0:T(8,128)(2,1)S(1)}, bf16[16,8192]{1,0:T(8,128)(2,1)S(1)}, u32[]{:S(2)}, u32[]{:S(2)}) collective-permute-start(bf16[16,8192]{1,0:T(8,128)(2,1)S(1)} %get-tuple-element.204), channel_id=1, source_target_pairs={{0,3},{1,0},{2,1},{3,2},{4,7},{5,4},{6,5},{7,6},{8,11},{9,8},{10,9... | collective-permute-start | bytes 786440 | tf_op jit(solution)/shard_map/cond/branch_1_fun/ppermute | solution.py:44
  55.5 2.3 %collective-permute-done.21 = bf16[16,8192]{1,0:T(8,128)(2,1)S(1)} collective-permute-done((bf16[16,8192]{1,0:T(8,128)(2,1)S(1)}, bf16[16,8192]{1,0:T(8,128)(2,1)S(1)}, u32[]{:S(2)}, u32[]{:S(2)}) %collective-permute-start.21) | collective-permute-done | bytes 262176 | tf_op jit(solution)/shard_map/cond/branch_1_fun/ppermute | solution.py:44
  58.1 2.7 %collective-permute-start.20 = (bf16[32,8192]{1,0:T(8,128)(2,1)S(1)}, bf16[32,8192]{1,0:T(8,128)(2,1)S(1)}, u32[]{:S(2)}, u32[]{:S(2)}) collective-permute-start(bf16[32,8192]{1,0:T(8,128)(2,1)S(1)} %pad_maximum_fusion.2), channel_id=1, source_target_pairs={{0,3},{1,0},{2,1},{3,2},{4,7},{5,4},{6,5},{7,6},{8,11},{9,8},{10,9... | collective-permute-start | bytes 1572872 | tf_op jit(solution)/shard_map/cond/branch_1_fun/ppermute | solution.py:44
  60.9 2.7 %collective-permute-done.17.b_ref = bf16[32,8192]{1,0:T(8,128)(2,1)S(1)} collective-permute-done((bf16[32,8192]{1,0:T(8,128)(2,1)S(1)}, bf16[32,8192]{1,0:T(8,128)(2,1)S(1)}, u32[]{:S(2)}, u32[]{:S(2)}) %collective-permute-start.17) | collective-permute-done | bytes 524320 | tf_op jit(solution)/shard_map/cond/branch_1_fun/ppermute | solution.py:44
  63.5 3.7 %collective-permute-done.22.d_ref = bf16[32,8192]{1,0:T(8,128)(2,1)S(1)} collective-permute-done((bf16[32,8192]{1,0:T(8,128)(2,1)S(1)}, bf16[32,8192]{1,0:T(8,128)(2,1)S(1)}, u32[]{:S(2)}, u32[]{:S(2)}) %collective-permute-start.22) | collective-permute-done | bytes 524320 | tf_op jit(solution)/shard_map/cond/branch_1_fun/ppermute | solution.py:44
  70.6 1.3 collective-permute-start.26
  72.0 18.3 %collective-permute-done.26 = bf16[32,8192]{1,0:T(8,128)(2,1)S(1)} collective-permute-done((bf16[32,8192]{1,0:T(8,128)(2,1)S(1)}, bf16[32,8192]{1,0:T(8,128)(2,1)S(1)}, u32[]{:S(2)}, u32[]{:S(2)}) %collective-permute-start.26) | collective-permute-done | bytes 524320 | tf_op jit(solution)/shard_map/cond/branch_1_fun/ppermute | solution.py:342
  91.0 12.1 %collective-permute-done.29.refs_3_ = bf16[32,8192]{1,0:T(8,128)(2,1)S(1)} collective-permute-done((bf16[32,8192]{1,0:T(8,128)(2,1)S(1)}, bf16[32,8192]{1,0:T(8,128)(2,1)S(1)}, u32[]{:S(2)}, u32[]{:S(2)}) %collective-permute-start.29) | collective-permute-done | bytes 524320 | tf_op jit(solution)/shard_map/cond/branch_1_fun/ppermute | solution.py:44
  103.1 2.7 %collective-permute-start.33 = (bf16[32,8192]{1,0:T(8,128)(2,1)S(1)}, bf16[32,8192]{1,0:T(8,128)(2,1)}, u32[]{:S(2)}, u32[]{:S(2)}) collective-permute-start(bf16[32,8192]{1,0:T(8,128)(2,1)S(1)} %broadcast_select_fusion.refs_0_), channel_id=1, source_target_pairs={{0,3},{1,0},{2,1},{3,2},{4,7},{5,4},{6,5},{7,6},{8,11},{9,8},{10,9... | collective-permute-start | bytes 1572872 | tf_op jit(solution)/shard_map/cond/branch_1_fun/ppermute | solution.py:44
  106.5 1.4 collective-permute-start.32
  107.9 4.5 %collective-permute-done.30.refs_2_ = bf16[32,8192]{1,0:T(8,128)(2,1)} collective-permute-done((bf16[32,8192]{1,0:T(8,128)(2,1)S(1)}, bf16[32,8192]{1,0:T(8,128)(2,1)}, u32[]{:S(2)}, u32[]{:S(2)}) %collective-permute-start.30) | collective-permute-done | bytes 524320 | tf_op jit(solution)/shard_map/cond/branch_1_fun/ppermute | solution.py:44
  112.4 1.7 %collective-permute-start.31 = (bf16[32,8192]{1,0:T(8,128)(2,1)}, bf16[32,8192]{1,0:T(8,128)(2,1)S(1)}, u32[]{:S(2)}, u32[]{:S(2)}) collective-permute-start(bf16[32,8192]{1,0:T(8,128)(2,1)} %collective-permute-done.30.refs_2_), channel_id=1, source_target_pairs={{0,4},{1,5},{2,6},{3,7},{4,0},{5,1},{6,2},{7,3},{8,12},{9,13},{10,... | collective-permute-start | bytes 1572872 | tf_op jit(solution)/shard_map/cond/branch_1_fun/ppermute | solution.py:44
  114.6 5.4 %vocab.2.refs_6_ = f32[8,128]{1,0:T(8,128)S(1)} custom-call(s32[8]{0:T(128)S(1)} %add.172.order_ref, bf16[32,8192]{1,0:T(8,128)(2,1)S(1)} %broadcast_select_fusion.refs_0_, bf16[32,8192]{1,0:T(8,128)(2,1)} %collective-permute-done.33.refs_1_, bf16[32,8192]{1,0:T(8,128)(2,1)} %collective-permute-done.30.refs_2_, ...), custom_call_target="tpu_custom_call" | custom-call | flops 1000000000 | bytes 10485760 | tf_op jit(solution)/shard_map/cond/branch_1_fun/vocab/pallas_call | solution.py:303
  120.9 4.5 %vocab.3 = f32[128,128]{1,0:T(8,128)} custom-call(s32[8]{0:T(128)S(1)} %add.172.order_ref, bf16[32,8192]{1,0:T(8,128)(2,1)S(1)} %collective-permute-done.28.refs_0_, bf16[32,8192]{1,0:T(8,128)(2,1)S(1)} %collective-permute-done.31.refs_1_, bf16[32,8192]{1,0:T(8,128)(2,1)S(1)} %collective-permute-done.32.refs_2_, bf16[8192,256]{1,0:T(8,128)(2,1)S(1)} %copy-done, ...), custom_call_target="tpu_custom_call" | custom-call | flops 1000000000 | bytes 10485760 | tf_op jit(solution)/shard_map/cond/branch_1_fun/vocab/pallas_call | solution.py:303
  125.7 1.9 %collective-permute-start.42 = (bf16[1,32,8192]{2,1,0:T(8,128)(2,1)}, bf16[1,32,8192]{2,1,0:T(8,128)(2,1)S(1)}, u32[]{:S(2)}, u32[]{:S(2)}) collective-permute-start(bf16[1,32,8192]{2,1,0:T(8,128)(2,1)} %bitcast.12), channel_id=1, source_target_pairs={{0,8},{8,16},{16,24},{24,32},{32,40},{40,48},{48,56},{56,64},{64,7... | collective-permute-start | bytes 1572872 | tf_op jit(solution)/shard_map/ppermute | solution.py:48
  127.6 16.5 %all_to_all.11 = f32[128,1,128]{2,1,0:T(1,128)} all-to-all(f32[128,1,128]{2,1,0:T(1,128)} %bitcast.13), channel_id=1, replica_groups=mesh['section'=16,'tensor'=8] {'section','tensor'}, dimensions={0} | all-to-all | bytes 131072 | tf_op jit(solution)/shard_map/all_to_all | solution.py:401
  144.1 1.6 %merge.1 = f32[32]{0:T(128)} custom-call(f32[128,128]{1,0:T(8,128)} %bitcast.24), custom_call_target="tpu_custom_call" | custom-call | tf_op jit(solution)/shard_map/merge/pallas_call | solution.py:139
  (90 shorter events, 15.1 us)
Async XLA Ops:
  0.6 31.7 %copy-start.1 = (bf16[1,32,8192]{2,1,0:T(8,128)(2,1)S(1)}, bf16[1,32,8192]{2,1,0:T(8,128)(2,1)}, u32[]{:S(2)}) copy-start(bf16[1,32,8192]{2,1,0:T(8,128)(2,1)} %param.15) | copy-start | bytes 1572868
  0.6 31.7 %copy-start.4 = (bf16[8192]{0:T(1024)(128)(2,1)S(1)}, bf16[8192]{0:T(1024)(128)(2,1)}, u32[]{:S(2)}) copy-start(bf16[8192]{0:T(1024)(128)(2,1)} %param.21) | copy-start | bytes 49156
  0.7 31.7 %copy-start.5 = (s32[256]{0:T(256)S(1)}, s32[256]{0:T(256)}, u32[]{:S(2)}) copy-start(s32[256]{0:T(256)} %param.23) | copy-start | bytes 3076
  0.7 31.6 %collective-permute-start.41 = (bf16[8192,256]{1,0:T(8,128)(2,1)}, bf16[8192,256]{1,0:T(8,128)(2,1)}, u32[]{:S(2)}, u32[]{:S(2)}) collective-permute-start(bf16[8192,256]{1,0:T(8,128)(2,1)} %param.22), channel_id=1, source_target_pairs={{0,8},{8,0},{16,24},{24,16},{32,40},{40,32},{48,56},{56,48},{64,72... | collective-permute-start | bytes 12582920 | tf_op jit(solution)/shard_map/ppermute | solution.py:48
  3.6 10.6 %collective-permute-start.35 = (bf16[32,8192]{1,0:T(8,128)(2,1)S(1)}, bf16[32,8192]{1,0:T(8,128)(2,1)}, u32[]{:S(2)}, u32[]{:S(2)}) collective-permute-start(bf16[32,8192]{1,0:T(8,128)(2,1)S(1)} %get-tuple-element.106), channel_id=1, source_target_pairs={{0,1},{1,2},{2,3},{3,0},{4,5},{5,6},{6,7},{7,4},{8,9},{9,10},{10,1... | collective-permute-start | bytes 1572872 | tf_op jit(solution)/shard_map/cond/branch_1_fun/ppermute | solution.py:44
  5.4 8.9 %collective-permute-start.37 = (bf16[32,8192]{1,0:T(8,128)(2,1)S(1)}, bf16[32,8192]{1,0:T(8,128)(2,1)}, u32[]{:S(2)}, u32[]{:S(2)}) collective-permute-start(bf16[32,8192]{1,0:T(8,128)(2,1)S(1)} %get-tuple-element.106), channel_id=1, source_target_pairs={{0,4},{1,5},{2,6},{3,7},{4,0},{5,1},{6,2},{7,3},{8,12},{9,13},{10,... | collective-permute-start | bytes 1572872 | tf_op jit(solution)/shard_map/cond/branch_1_fun/ppermute | solution.py:44
  6.6 19.2 %collective-permute-start.34 = (bf16[32,8192]{1,0:T(8,128)(2,1)S(1)}, bf16[32,8192]{1,0:T(8,128)(2,1)}, u32[]{:S(2)}, u32[]{:S(2)}) collective-permute-start(bf16[32,8192]{1,0:T(8,128)(2,1)S(1)} %get-tuple-element.106), channel_id=1, source_target_pairs={{0,3},{1,0},{2,1},{3,2},{4,7},{5,4},{6,5},{7,6},{8,11},{9,8},{10,9... | collective-permute-start | bytes 1572872 | tf_op jit(solution)/shard_map/cond/branch_1_fun/ppermute | solution.py:44
  14.2 9.6 %collective-permute-start.36 = (bf16[32,8192]{1,0:T(8,128)(2,1)}, bf16[32,8192]{1,0:T(8,128)(2,1)}, u32[]{:S(2)}, u32[]{:S(2)}) collective-permute-start(bf16[32,8192]{1,0:T(8,128)(2,1)} %collective-permute-done.35), channel_id=1, source_target_pairs={{0,1},{1,2},{2,3},{3,0},{4,5},{5,6},{6,7},{7,4},{8,9},{9,10},{10,1... | collective-permute-start | bytes 1572872 | tf_op jit(solution)/shard_map/cond/branch_1_fun/ppermute | solution.py:44
  14.3 11.5 %collective-permute-start.38 = (bf16[32,8192]{1,0:T(8,128)(2,1)}, bf16[32,8192]{1,0:T(8,128)(2,1)}, u32[]{:S(2)}, u32[]{:S(2)}) collective-permute-start(bf16[32,8192]{1,0:T(8,128)(2,1)} %collective-permute-done.37), channel_id=1, source_target_pairs={{0,3},{1,0},{2,1},{3,2},{4,7},{5,4},{6,5},{7,6},{8,11},{9,8},{10,9... | collective-permute-start | bytes 1572872 | tf_op jit(solution)/shard_map/cond/branch_1_fun/ppermute | solution.py:44
  17.0 13.8 %collective-permute-start.40 = (bf16[32,8192]{1,0:T(8,128)(2,1)}, bf16[32,8192]{1,0:T(8,128)(2,1)}, u32[]{:S(2)}, u32[]{:S(2)}) collective-permute-start(bf16[32,8192]{1,0:T(8,128)(2,1)} %collective-permute-done.37), channel_id=1, source_target_pairs={{0,1},{1,2},{2,3},{3,0},{4,5},{5,6},{6,7},{7,4},{8,9},{9,10},{10,1... | collective-permute-start | bytes 1572872 | tf_op jit(solution)/shard_map/cond/branch_1_fun/ppermute | solution.py:44
  23.8 8.5 %collective-permute-start.39 = (bf16[32,8192]{1,0:T(8,128)(2,1)}, bf16[32,8192]{1,0:T(8,128)(2,1)}, u32[]{:S(2)}, u32[]{:S(2)}) collective-permute-start(bf16[32,8192]{1,0:T(8,128)(2,1)} %collective-permute-done.36), channel_id=1, source_target_pairs={{0,4},{1,5},{2,6},{3,7},{4,0},{5,1},{6,2},{7,3},{8,12},{9,13},{10,... | collective-permute-start | bytes 1572872 | tf_op jit(solution)/shard_map/cond/branch_1_fun/ppermute | solution.py:44
  43.1 8.1 %collective-permute-start.18 = (bf16[32,8192]{1,0:T(8,128)(2,1)S(1)}, bf16[32,8192]{1,0:T(8,128)(2,1)S(1)}, u32[]{:S(2)}, u32[]{:S(2)}) collective-permute-start(bf16[32,8192]{1,0:T(8,128)(2,1)S(1)} %get-tuple-element.149), channel_id=1, source_target_pairs={{0,4},{1,5},{2,6},{3,7},{4,0},{5,1},{6,2},{7,3},{8,12},{9,13},{10,... | collective-permute-start | bytes 1572872 | tf_op jit(solution)/shard_map/cond/branch_1_fun/ppermute | solution.py:44
  44.3 9.7 %collective-permute-start.15 = (bf16[32,8192]{1,0:T(8,128)(2,1)S(1)}, bf16[32,8192]{1,0:T(8,128)(2,1)S(1)}, u32[]{:S(2)}, u32[]{:S(2)}) collective-permute-start(bf16[32,8192]{1,0:T(8,128)(2,1)S(1)} %get-tuple-element.145), channel_id=1, source_target_pairs={{0,1},{1,2},{2,3},{3,0},{4,5},{5,6},{6,7},{7,4},{8,9},{9,10},{10,1... | collective-permute-start | bytes 1572872 | tf_op jit(solution)/shard_map/cond/branch_1_fun/ppermute | solution.py:44
  44.4 9.7 %collective-permute-start.16 = (bf16[32,8192]{1,0:T(8,128)(2,1)S(1)}, bf16[32,8192]{1,0:T(8,128)(2,1)S(1)}, u32[]{:S(2)}, u32[]{:S(2)}) collective-permute-start(bf16[32,8192]{1,0:T(8,128)(2,1)S(1)} %get-tuple-element.146), channel_id=1, source_target_pairs={{0,3},{1,0},{2,1},{3,2},{4,7},{5,4},{6,5},{7,6},{8,11},{9,8},{10,9... | collective-permute-start | bytes 1572872 | tf_op jit(solution)/shard_map/cond/branch_1_fun/ppermute | solution.py:44
  51.3 6.5 %collective-permute-start.21 = (bf16[16,8192]{1,0:T(8,128)(2,1)S(1)}, bf16[16,8192]{1,0:T(8,128)(2,1)S(1)}, u32[]{:S(2)}, u32[]{:S(2)}) collective-permute-start(bf16[16,8192]{1,0:T(8,128)(2,1)S(1)} %get-tuple-element.203), channel_id=1, source_target_pairs={{0,1},{1,2},{2,3},{3,0},{4,5},{5,6},{6,7},{7,4},{8,9},{9,10},{10,1... | collective-permute-start | bytes 786440 | tf_op jit(solution)/shard_map/cond/branch_1_fun/ppermute | solution.py:44
  51.4 6.6 %collective-permute-start.19 = (bf16[16,8192]{1,0:T(8,128)(2,1)S(1)}, bf16[16,8192]{1,0:T(8,128)(2,1)S(1)}, u32[]{:S(2)}, u32[]{:S(2)}) collective-permute-start(bf16[16,8192]{1,0:T(8,128)(2,1)S(1)} %get-tuple-element.204), channel_id=1, source_target_pairs={{0,3},{1,0},{2,1},{3,2},{4,7},{5,4},{6,5},{7,6},{8,11},{9,8},{10,9... | collective-permute-start | bytes 786440 | tf_op jit(solution)/shard_map/cond/branch_1_fun/ppermute | solution.py:44
  54.2 9.3 %collective-permute-start.17 = (bf16[32,8192]{1,0:T(8,128)(2,1)S(1)}, bf16[32,8192]{1,0:T(8,128)(2,1)S(1)}, u32[]{:S(2)}, u32[]{:S(2)}) collective-permute-start(bf16[32,8192]{1,0:T(8,128)(2,1)S(1)} %add_convert_fusion.5), channel_id=1, source_target_pairs={{0,4},{1,5},{2,6},{3,7},{4,0},{5,1},{6,2},{7,3},{8,12},{9,13},{10,... | collective-permute-start | bytes 1572872 | tf_op jit(solution)/shard_map/cond/branch_1_fun/ppermute | solution.py:44
  57.9 9.3 %collective-permute-start.22 = (bf16[32,8192]{1,0:T(8,128)(2,1)S(1)}, bf16[32,8192]{1,0:T(8,128)(2,1)S(1)}, u32[]{:S(2)}, u32[]{:S(2)}) collective-permute-start(bf16[32,8192]{1,0:T(8,128)(2,1)S(1)} %pad_maximum_fusion.3), channel_id=1, source_target_pairs={{0,1},{1,2},{2,3},{3,0},{4,5},{5,6},{6,7},{7,4},{8,9},{9,10},{10,1... | collective-permute-start | bytes 1572872 | tf_op jit(solution)/shard_map/cond/branch_1_fun/ppermute | solution.py:44
  58.1 9.1 %collective-permute-start.20 = (bf16[32,8192]{1,0:T(8,128)(2,1)S(1)}, bf16[32,8192]{1,0:T(8,128)(2,1)S(1)}, u32[]{:S(2)}, u32[]{:S(2)}) collective-permute-start(bf16[32,8192]{1,0:T(8,128)(2,1)S(1)} %pad_maximum_fusion.2), channel_id=1, source_target_pairs={{0,3},{1,0},{2,1},{3,2},{4,7},{5,4},{6,5},{7,6},{8,11},{9,8},{10,9... | collective-permute-start | bytes 1572872 | tf_op jit(solution)/shard_map/cond/branch_1_fun/ppermute | solution.py:44
  68.4 2.1 %collective-permute-start.23 = (bf16[32,8192]{1,0:T(8,128)(2,1)S(1)}, bf16[32,8192]{1,0:T(8,128)(2,1)S(1)}, u32[]{:S(2)}, u32[]{:S(2)}) collective-permute-start(bf16[32,8192]{1,0:T(8,128)(2,1)S(1)} %get-tuple-element.156), channel_id=1, source_target_pairs={{120,24},{121,25},{122,26},{123,27},{124,28},{125,29},{126,30},{12... | collective-permute-start | bytes 1572872 | tf_op jit(solution)/shard_map/cond/branch_1_fun/ppermute | solution.py:48
  69.1 1.4 collective-permute-start.24
  69.8 0.7 collective-permute-start.25
  70.6 19.6 %collective-permute-start.26 = (bf16[32,8192]{1,0:T(8,128)(2,1)S(1)}, bf16[32,8192]{1,0:T(8,128)(2,1)S(1)}, u32[]{:S(2)}, u32[]{:S(2)}) collective-permute-start(bf16[32,8192]{1,0:T(8,128)(2,1)S(1)} %select_select_fusion), channel_id=1, source_target_pairs={{24,12},{25,13},{26,14},{27,15},{28,8},{29,9},{30,10},{31,11},{56,... | collective-permute-start | bytes 1572872 | tf_op jit(solution)/shard_map/cond/branch_1_fun/ppermute | solution.py:342
  90.3 12.7 %collective-permute-start.29 = (bf16[32,8192]{1,0:T(8,128)(2,1)S(1)}, bf16[32,8192]{1,0:T(8,128)(2,1)S(1)}, u32[]{:S(2)}, u32[]{:S(2)}) collective-permute-start(bf16[32,8192]{1,0:T(8,128)(2,1)S(1)} %broadcast_select_fusion.refs_0_), channel_id=1, source_target_pairs={{0,1},{1,2},{2,3},{3,0},{4,5},{5,6},{6,7},{7,4},{8,9},{9,10},{10,1... | collective-permute-start | bytes 1572872 | tf_op jit(solution)/shard_map/cond/branch_1_fun/ppermute | solution.py:44
  90.7 15.7 %collective-permute-start.27 = (bf16[32,8192]{1,0:T(8,128)(2,1)S(1)}, bf16[32,8192]{1,0:T(8,128)(2,1)S(1)}, u32[]{:S(2)}, u32[]{:S(2)}) collective-permute-start(bf16[32,8192]{1,0:T(8,128)(2,1)S(1)} %broadcast_select_fusion.refs_0_), channel_id=1, source_target_pairs={{0,4},{1,5},{2,6},{3,7},{4,0},{5,1},{6,2},{7,3},{8,12},{9,13},{10,... | collective-permute-start | bytes 1572872 | tf_op jit(solution)/shard_map/cond/branch_1_fun/ppermute | solution.py:44
  103.1 9.3 %collective-permute-start.30 = (bf16[32,8192]{1,0:T(8,128)(2,1)S(1)}, bf16[32,8192]{1,0:T(8,128)(2,1)}, u32[]{:S(2)}, u32[]{:S(2)}) collective-permute-start(bf16[32,8192]{1,0:T(8,128)(2,1)S(1)} %collective-permute-done.29.refs_3_), channel_id=1, source_target_pairs={{0,1},{1,2},{2,3},{3,0},{4,5},{5,6},{6,7},{7,4},{8,9},{9,10},{10,1... | collective-permute-start | bytes 1572872 | tf_op jit(solution)/shard_map/cond/branch_1_fun/ppermute | solution.py:44
  103.1 11.4 %collective-permute-start.33 = (bf16[32,8192]{1,0:T(8,128)(2,1)S(1)}, bf16[32,8192]{1,0:T(8,128)(2,1)}, u32[]{:S(2)}, u32[]{:S(2)}) collective-permute-start(bf16[32,8192]{1,0:T(8,128)(2,1)S(1)} %broadcast_select_fusion.refs_0_), channel_id=1, source_target_pairs={{0,3},{1,0},{2,1},{3,2},{4,7},{5,4},{6,5},{7,6},{8,11},{9,8},{10,9... | collective-permute-start | bytes 1572872 | tf_op jit(solution)/shard_map/cond/branch_1_fun/ppermute | solution.py:44
  106.4 13.6 %collective-permute-start.28 = (bf16[32,8192]{1,0:T(8,128)(2,1)S(1)}, bf16[32,8192]{1,0:T(8,128)(2,1)S(1)}, u32[]{:S(2)}, u32[]{:S(2)}) collective-permute-start(bf16[32,8192]{1,0:T(8,128)(2,1)S(1)} %collective-permute-done.27.refs_4_), channel_id=1, source_target_pairs={{0,3},{1,0},{2,1},{3,2},{4,7},{5,4},{6,5},{7,6},{8,11},{9,8},{10,9... | collective-permute-start | bytes 1572872 | tf_op jit(solution)/shard_map/cond/branch_1_fun/ppermute | solution.py:44
  106.5 13.5 %collective-permute-start.32 = (bf16[32,8192]{1,0:T(8,128)(2,1)S(1)}, bf16[32,8192]{1,0:T(8,128)(2,1)S(1)}, u32[]{:S(2)}, u32[]{:S(2)}) collective-permute-start(bf16[32,8192]{1,0:T(8,128)(2,1)S(1)} %collective-permute-done.27.refs_4_), channel_id=1, source_target_pairs={{0,1},{1,2},{2,3},{3,0},{4,5},{5,6},{6,7},{7,4},{8,9},{9,10},{10,1... | collective-permute-start | bytes 1572872 | tf_op jit(solution)/shard_map/cond/branch_1_fun/ppermute | solution.py:44
  112.4 8.5 %collective-permute-start.31 = (bf16[32,8192]{1,0:T(8,128)(2,1)}, bf16[32,8192]{1,0:T(8,128)(2,1)S(1)}, u32[]{:S(2)}, u32[]{:S(2)}) collective-permute-start(bf16[32,8192]{1,0:T(8,128)(2,1)} %collective-permute-done.30.refs_2_), channel_id=1, source_target_pairs={{0,4},{1,5},{2,6},{3,7},{4,0},{5,1},{6,2},{7,3},{8,12},{9,13},{10,... | collective-permute-start | bytes 1572872 | tf_op jit(solution)/shard_map/cond/branch_1_fun/ppermute | solution.py:44
  114.6 6.4 %copy-start = (bf16[8192,256]{1,0:T(8,128)(2,1)S(1)}, bf16[8192,256]{1,0:T(8,128)(2,1)}, u32[]{:S(2)}) copy-start(bf16[8192,256]{1,0:T(8,128)(2,1)} %get-tuple-element.157.refs_5_.refs_3_) | copy-start | bytes 12582916 | tf_op jit(solution)/shard_map/cond
  125.7 20.0 %collective-permute-start.42 = (bf16[1,32,8192]{2,1,0:T(8,128)(2,1)}, bf16[1,32,8192]{2,1,0:T(8,128)(2,1)S(1)}, u32[]{:S(2)}, u32[]{:S(2)}) collective-permute-start(bf16[1,32,8192]{2,1,0:T(8,128)(2,1)} %bitcast.12), channel_id=1, source_target_pairs={{0,8},{8,16},{16,24},{24,32},{32,40},{40,48},{48,56},{56,64},{64,7... | collective-permute-start | bytes 1572872 | tf_op jit(solution)/shard_map/ppermute | solution.py:48
